TPU v7x, 32 devices: a whole 2x2x4 slice. The times are simulated.
32 devices in a mesh: tgt: 4 (over z), src: 8 (over y, x, core).
Axes of the slice: x: 2, y: 2, z: 4, core: 2. Of those that a mesh axis runs over, the one named last changes fastest.
Arguments:
- vol_grad: float32 [128, 16384], P(None, ('tgt', 'src')), may hold values from -6 to 6
- vol_coords: float32 [3, 16384], P(None, ('tgt', 'src')), may hold values from 0 to 1
- ctrl_coords: float32 [3, 8192], P(None, ('tgt', 'src')), may hold values from 0 to 1
Outputs:
- adjoint_controls: float32 [128, 8192], P(None, ('tgt', 'src'))
All inputs are finite; a program needn't handle non-finite values.
Results may differ from a plain program's by a relative error of at most 0.0003.
Values sent between devices are 32-bit elements; how exact they have to be, the bound alone decides.
No kernel may reach another device: no remote copies, remote signals or barrier semaphores. Data moves between devices by JAX's collectives and lax.ppermute only.
A program may use at most 64 MiB of HBM per device.

v0:
```python
import math

import jax
import jax.numpy as jnp
from jax import lax
from jax.sharding import PartitionSpec as P

STEPS = 2


neighbours = 64.0
ridge_term = 1.0
omegas = [1.0 / (0.55 + 0.45 * math.cos(math.pi * (2 * k + 1) / 4.0)) for k in range(2)]


def wendland(sources, targets, radius):
    delta_x = sources[0][:, None] - targets[0][None, :]
    delta_y = sources[1][:, None] - targets[1][None, :]
    delta_z = sources[2][:, None] - targets[2][None, :]
    distance = jnp.sqrt(delta_x * delta_x + delta_y * delta_y + delta_z * delta_z)
    falloff = jnp.maximum(1.0 - distance / radius, 0.0)
    square = falloff * falloff
    return square * square * (4.0 * distance / radius + 1.0)


def contract(sources, vectors, targets, radius, with_sums):
    length_in = sources.shape[1]
    block_len = math.gcd(length_in, 512)
    blocks = length_in // block_len
    width = targets.shape[1]

    def add(which, state_pair):
        accum, column_sums = state_pair
        chosen = lax.dynamic_slice_in_dim(sources, which * block_len, block_len, 1)
        values = lax.dynamic_slice_in_dim(vectors, which * block_len, block_len, 1)
        kernel_tile = wendland(chosen, targets, radius)
        accum = accum + jnp.dot(
            values, kernel_tile, precision=lax.Precision.HIGHEST, preferred_element_type=jnp.float32
        )
        if with_sums:
            column_sums = column_sums + jnp.sum(kernel_tile, axis=0, keepdims=True)
        return (accum, column_sums)

    start = (jnp.zeros((vectors.shape[0], width), jnp.float32), jnp.zeros((1, width), jnp.float32))
    return lax.fori_loop(0, blocks, add, start)


def per_device(vol_grad, vol_coords, ctrl_coords):
    owned = ctrl_coords.shape[1]
    overall = owned * lax.axis_size("tgt") * lax.axis_size("src")
    radius = (3.0 * neighbours / (4.0 * math.pi * overall)) ** (1.0 / 3.0)
    gradients, positions, row_points = (
        lax.all_gather(vol_grad, "tgt", axis=1, tiled=True),
        lax.all_gather(vol_coords, "tgt", axis=1, tiled=True),
        lax.all_gather(ctrl_coords, "tgt", axis=1, tiled=True),
    )
    col_points = lax.all_gather(ctrl_coords, "src", axis=1, tiled=True)
    partial_value, unused = contract(positions, gradients, col_points, radius, False)
    pullback = lax.psum_scatter(partial_value, "src", scatter_dimension=1, tiled=True)
    iterate = pullback
    for sweep in range(STEPS):
        columns = lax.all_gather(iterate, "src", axis=1, tiled=True)
        product, column_sums = contract(col_points, columns, row_points, radius, True)
        product, column_sums = (
            lax.psum_scatter(product, "tgt", scatter_dimension=1, tiled=True),
            lax.psum_scatter(column_sums, "tgt", scatter_dimension=1, tiled=True),
        )
        scaling = 1.0 / (column_sums + ridge_term)
        iterate = iterate + omegas[sweep] * scaling * (pullback - product - iterate)
    return iterate


def solution(mesh):
    placed = (P(None, ("tgt", "src")), P(None, ("tgt", "src")), P(None, ("tgt", "src")))
    return jax.shard_map(
        per_device, mesh=mesh, in_specs=placed, out_specs=P(None, ("tgt", "src")), check_vma=False
    )
```

profile of v0, /device:TPU:0, one launch (start us, length us, event | category | flops | bytes accessed | tf_op | source)
XLA Modules:
  0.0 298.8 jit_solution(1107481222811550937)
XLA Ops:
  6.5 0.7 all-gather.4.cloned.1.call-update
  7.3 0.0 reduce-scatter.10.cloned.1.call-start
  7.3 10.7 %all_gather.20 = f32[3,2048]{1,0:T(4,128)S(1)} all-gather(f32[3,256]{1,0:T(4,128)} %param.11), channel_id=1, replica_groups=mesh['tgt'=4,'src'=8] {'src'}, dimensions={1}, use_global_device_ids=true | all-gather | bytes 27648 | tf_op jit(solution)/shard_map/all_gather | solution.py:57
  18.0 13.8 %all_gather.19 = f32[3,2048]{1,0:T(4,128)S(1)} all-gather(f32[3,512]{1,0:T(4,128)} %param.10), channel_id=1, replica_groups=mesh['tgt'=4,'src'=8] {'tgt'}, dimensions={1}, use_global_device_ids=true | all-gather | bytes 30720 | tf_op jit(solution)/shard_map/all_gather | solution.py:54
  31.7 8.3 %all-gather.4.cloned.1.call-done = f32[128,2048]{1,0:T(8,128)} async-done(((f32[128,512]{1,0:T(8,128)}), f32[128,2048]{1,0:T(8,128)}) %all-gather.4.cloned.1.call-update) | async-done | bytes 1048592 | tf_op jit(solution)/shard_map/all_gather | solution.py:53
  40.0 27.9 %while.52 = (s32[]{:T(128)}, f32[128,2048]{1,0:T(8,128)S(1)}, f32[128,2048]{1,0:T(8,128)}, f32[3,2048]{1,0:T(4,128)S(1)}, f32[3,2048]{1,0:T(4,128)S(1)}, /*index...) while((s32[]{:T(128)}, f32[128,2048]{1,0:T(8,128)S(1)}, ...), condition=%wide.region_1.0_spmd.clone, body=%wide.region_0.0_spmd.clone.sunk | while | flops 1627914240 | bytes 2451661 | solution.py:45
  40.0 0.1 constant_dynamic-slice_fusion.6
  40.1 6.8 %fusion.73 = f32[128,2048]{1,0:T(8,128)S(1)} fusion(f32[2048]{0:T(1024)S(1)} %bitcast.73, f32[512]{0:T(512)S(1)} %bitcast.103, f32[2048]{0:T(1024)S(1)} %bitcast.74, f32[512]{0:T(512)S(1)} %bitcast.102, f32[2048]{0:T(1024)S(1)} %bitcast.72, f32[512]{0:T(512)S(1)} %bitcast.101, f32[128,2048]{1,0:T(8,128)S(1)} %get-tuple-element.717, ...), kind=kOutput, calls=%fused_computation.18.clone.1 | convolution fusion | flops 1627914240 | bytes 2390021 | tf_op jit(solution)/shard_map/while/body/eval_jaxpr/dot_general | solution.py:37
  47.0 0.1 constant_dynamic-slice_fusion.6
  47.1 6.8 %fusion.73 = f32[128,2048]{1,0:T(8,128)S(1)} fusion(f32[2048]{0:T(1024)S(1)} %bitcast.73, f32[512]{0:T(512)S(1)} %bitcast.103, f32[2048]{0:T(1024)S(1)} %bitcast.74, f32[512]{0:T(512)S(1)} %bitcast.102, f32[2048]{0:T(1024)S(1)} %bitcast.72, f32[512]{0:T(512)S(1)} %bitcast.101, f32[128,2048]{1,0:T(8,128)S(1)} %get-tuple-element.717, ...), kind=kOutput, calls=%fused_computation.18.clone.1 | convolution fusion | flops 1627914240 | bytes 2390021 | tf_op jit(solution)/shard_map/while/body/eval_jaxpr/dot_general | solution.py:37
  54.0 0.1 constant_dynamic-slice_fusion.6
  54.1 6.8 %fusion.73 = f32[128,2048]{1,0:T(8,128)S(1)} fusion(f32[2048]{0:T(1024)S(1)} %bitcast.73, f32[512]{0:T(512)S(1)} %bitcast.103, f32[2048]{0:T(1024)S(1)} %bitcast.74, f32[512]{0:T(512)S(1)} %bitcast.102, f32[2048]{0:T(1024)S(1)} %bitcast.72, f32[512]{0:T(512)S(1)} %bitcast.101, f32[128,2048]{1,0:T(8,128)S(1)} %get-tuple-element.717, ...), kind=kOutput, calls=%fused_computation.18.clone.1 | convolution fusion | flops 1627914240 | bytes 2390021 | tf_op jit(solution)/shard_map/while/body/eval_jaxpr/dot_general | solution.py:37
  61.0 0.1 constant_dynamic-slice_fusion.6
  61.1 6.8 %fusion.73 = f32[128,2048]{1,0:T(8,128)S(1)} fusion(f32[2048]{0:T(1024)S(1)} %bitcast.73, f32[512]{0:T(512)S(1)} %bitcast.103, f32[2048]{0:T(1024)S(1)} %bitcast.74, f32[512]{0:T(512)S(1)} %bitcast.102, f32[2048]{0:T(1024)S(1)} %bitcast.72, f32[512]{0:T(512)S(1)} %bitcast.101, f32[128,2048]{1,0:T(8,128)S(1)} %get-tuple-element.717, ...), kind=kOutput, calls=%fused_computation.18.clone.1 | convolution fusion | flops 1627914240 | bytes 2390021 | tf_op jit(solution)/shard_map/while/body/eval_jaxpr/dot_general | solution.py:37
  68.0 1.0 copy-done.2
  68.9 0.0 all-gather.6.cloned.1.call-start
  69.0 35.7 %reduce-scatter.10.cloned.1.call-done = f32[128,256]{1,0:T(8,128)} async-done(((f32[128,2048]{1,0:T(8,128)}), f32[128,256]{1,0:T(8,128)}) %reduce-scatter.10.cloned.1.call-update) | async-done | bytes 131088 | tf_op jit(solution)/shard_map/reduce_scatter | solution.py:59
  104.8 13.4 %all_gather.22 = f32[3,1024]{1,0:T(4,128)S(1)} all-gather(f32[3,256]{1,0:T(4,128)S(1)} %copy-done.5), channel_id=1, replica_groups=mesh['tgt'=4,'src'=8] {'tgt'}, dimensions={1}, use_global_device_ids=true | all-gather | bytes 15360 | tf_op jit(solution)/shard_map/all_gather | solution.py:55
  118.2 12.0 %all-gather.6.cloned.1.call-done = f32[128,2048]{1,0:T(8,128)} async-done(((f32[128,256]{1,0:T(8,128)}), f32[128,2048]{1,0:T(8,128)}) %all-gather.6.cloned.1.call-update) | async-done | bytes 1048592 | tf_op jit(solution)/shard_map/all_gather | solution.py:62
  130.2 23.4 %while.53 = (s32[]{:T(128)}, f32[128,1024]{1,0:T(8,128)S(1)}, f32[1,1024]{1,0:T(1,128)S(1)}, f32[128,2048]{1,0:T(8,128)}, f32[3,2048]{1,0:T(4,128)S(1)}, /*index...) while((s32[]{:T(128)}, f32[128,1024]{1,0:T(8,128)S(1)}, ...), condition=%wide.region_5.0_spmd.clone, body=%wide.region_3.0_spmd.clone.sunk | while | flops 822871040 | bytes 1401046 | solution.py:45
  130.2 0.1 constant_dynamic-slice_fusion.7
  130.3 4.0 %convolution_add_fusion.4 = f32[128,1024]{1,0:T(8,128)S(1)} fusion(f32[1024]{0:T(1024)S(1)} %bitcast.79, f32[512]{0:T(512)S(1)} %bitcast.93, f32[1024]{0:T(1024)S(1)} %bitcast.81, f32[512]{0:T(512)S(1)} %bitcast.91, f32[1024]{0:T(1024)S(1)} %bitcast.77, f32[512]{0:T(512)S(1)} %bitcast.89, f32[128,1024]{1,0:T(8,128)S(1)} %get-tuple-element.751, ...), kind=kOutput, calls=%fused_computation.37.clone.1 | convolution fusion | flops 813957120 | bytes 1329157 | tf_op jit(solution)/shard_map/while/body/eval_jaxpr/dot_general | solution.py:37
  134.3 1.7 fusion.76
  136.0 0.1 constant_dynamic-slice_fusion.7
  136.1 4.0 %convolution_add_fusion.4 = f32[128,1024]{1,0:T(8,128)S(1)} fusion(f32[1024]{0:T(1024)S(1)} %bitcast.79, f32[512]{0:T(512)S(1)} %bitcast.93, f32[1024]{0:T(1024)S(1)} %bitcast.81, f32[512]{0:T(512)S(1)} %bitcast.91, f32[1024]{0:T(1024)S(1)} %bitcast.77, f32[512]{0:T(512)S(1)} %bitcast.89, f32[128,1024]{1,0:T(8,128)S(1)} %get-tuple-element.751, ...), kind=kOutput, calls=%fused_computation.37.clone.1 | convolution fusion | flops 813957120 | bytes 1329157 | tf_op jit(solution)/shard_map/while/body/eval_jaxpr/dot_general | solution.py:37
  140.1 1.7 fusion.76
  141.8 0.1 constant_dynamic-slice_fusion.7
  142.0 4.0 %convolution_add_fusion.4 = f32[128,1024]{1,0:T(8,128)S(1)} fusion(f32[1024]{0:T(1024)S(1)} %bitcast.79, f32[512]{0:T(512)S(1)} %bitcast.93, f32[1024]{0:T(1024)S(1)} %bitcast.81, f32[512]{0:T(512)S(1)} %bitcast.91, f32[1024]{0:T(1024)S(1)} %bitcast.77, f32[512]{0:T(512)S(1)} %bitcast.89, f32[128,1024]{1,0:T(8,128)S(1)} %get-tuple-element.751, ...), kind=kOutput, calls=%fused_computation.37.clone.1 | convolution fusion | flops 813957120 | bytes 1329157 | tf_op jit(solution)/shard_map/while/body/eval_jaxpr/dot_general | solution.py:37
  145.9 1.7 fusion.76
  147.7 0.1 constant_dynamic-slice_fusion.7
  147.8 4.0 %convolution_add_fusion.4 = f32[128,1024]{1,0:T(8,128)S(1)} fusion(f32[1024]{0:T(1024)S(1)} %bitcast.79, f32[512]{0:T(512)S(1)} %bitcast.93, f32[1024]{0:T(1024)S(1)} %bitcast.81, f32[512]{0:T(512)S(1)} %bitcast.91, f32[1024]{0:T(1024)S(1)} %bitcast.77, f32[512]{0:T(512)S(1)} %bitcast.89, f32[128,1024]{1,0:T(8,128)S(1)} %get-tuple-element.751, ...), kind=kOutput, calls=%fused_computation.37.clone.1 | convolution fusion | flops 813957120 | bytes 1329157 | tf_op jit(solution)/shard_map/while/body/eval_jaxpr/dot_general | solution.py:37
  151.8 1.7 fusion.76
  153.5 1.0 copy.4
  154.6 0.0 reduce-scatter.12.cloned.1.call-start
  154.7 0.5 reduce-scatter.12.cloned.1.call-update
  155.2 0.0 all-gather.8.cloned.1.call-start
  155.2 21.2 %reduce-scatter.16.cloned.1.call-done = f32[256,1]{1,0:T(8,128)} async-done(((f32[1024,1]{1,0:T(8,128)}), f32[256,1]{1,0:T(8,128)}) %reduce-scatter.16.cloned.1.call-update) | async-done | bytes 1040
  176.4 0.9 multiply_bitcast_fusion.1
  177.3 0.1 copy.8
  177.4 21.0 %reduce-scatter.12.cloned.1.call-done = f32[128,256]{1,0:T(8,128)} async-done(((f32[128,1024]{1,0:T(8,128)}), f32[128,256]{1,0:T(8,128)}) %reduce-scatter.12.cloned.1.call-update) | async-done | bytes 131088 | tf_op jit(solution)/shard_map/reduce_scatter | solution.py:65
  198.4 1.6 fusion.54
  200.0 0.0 reduce-scatter.18.cloned.1.call-start
  200.1 21.9 %all-gather.8.cloned.1.call-done = f32[128,2048]{1,0:T(8,128)} async-done(((f32[128,256]{1,0:T(8,128)}), f32[128,2048]{1,0:T(8,128)}) %all-gather.8.cloned.1.call-update) | async-done | bytes 1048592 | tf_op jit(solution)/shard_map/all_gather | solution.py:62
  222.0 23.3 %while.54 = (s32[]{:T(128)}, f32[128,1024]{1,0:T(8,128)S(1)}, f32[1,1024]{1,0:T(1,128)S(1)}, f32[128,2048]{1,0:T(8,128)}, f32[3,2048]{1,0:T(4,128)S(1)}, /*index...) while((s32[]{:T(128)}, f32[128,1024]{1,0:T(8,128)S(1)}, ...), condition=%wide.region_10.0_spmd.clone, body=%wide.region_8.0_spmd.clone.sunk | while | flops 822871040 | bytes 1401046 | solution.py:45
  222.0 0.1 constant_dynamic-slice_fusion.8
  222.1 4.0 %convolution_add_fusion.5 = f32[128,1024]{1,0:T(8,128)S(1)} fusion(f32[1024]{0:T(1024)S(1)} %bitcast.85, f32[512]{0:T(512)S(1)} %bitcast.99, f32[1024]{0:T(1024)S(1)} %bitcast.87, f32[512]{0:T(512)S(1)} %bitcast.97, f32[1024]{0:T(1024)S(1)} %bitcast.83, f32[512]{0:T(512)S(1)} %bitcast.95, f32[128,1024]{1,0:T(8,128)S(1)} %get-tuple-element.787, ...), kind=kOutput, calls=%fused_computation.49.clone.1 | convolution fusion | flops 813957120 | bytes 1329157 | tf_op jit(solution)/shard_map/while/body/eval_jaxpr/dot_general | solution.py:37
  226.1 1.7 fusion.80
  227.8 0.1 constant_dynamic-slice_fusion.8
  228.0 4.0 %convolution_add_fusion.5 = f32[128,1024]{1,0:T(8,128)S(1)} fusion(f32[1024]{0:T(1024)S(1)} %bitcast.85, f32[512]{0:T(512)S(1)} %bitcast.99, f32[1024]{0:T(1024)S(1)} %bitcast.87, f32[512]{0:T(512)S(1)} %bitcast.97, f32[1024]{0:T(1024)S(1)} %bitcast.83, f32[512]{0:T(512)S(1)} %bitcast.95, f32[128,1024]{1,0:T(8,128)S(1)} %get-tuple-element.787, ...), kind=kOutput, calls=%fused_computation.49.clone.1 | convolution fusion | flops 813957120 | bytes 1329157 | tf_op jit(solution)/shard_map/while/body/eval_jaxpr/dot_general | solution.py:37
  231.9 1.7 fusion.80
  233.7 0.1 constant_dynamic-slice_fusion.8
  233.8 4.0 %convolution_add_fusion.5 = f32[128,1024]{1,0:T(8,128)S(1)} fusion(f32[1024]{0:T(1024)S(1)} %bitcast.85, f32[512]{0:T(512)S(1)} %bitcast.99, f32[1024]{0:T(1024)S(1)} %bitcast.87, f32[512]{0:T(512)S(1)} %bitcast.97, f32[1024]{0:T(1024)S(1)} %bitcast.83, f32[512]{0:T(512)S(1)} %bitcast.95, f32[128,1024]{1,0:T(8,128)S(1)} %get-tuple-element.787, ...), kind=kOutput, calls=%fused_computation.49.clone.1 | convolution fusion | flops 813957120 | bytes 1329157 | tf_op jit(solution)/shard_map/while/body/eval_jaxpr/dot_general | solution.py:37
  237.8 1.7 fusion.80
  239.5 0.1 constant_dynamic-slice_fusion.8
  239.6 4.0 %convolution_add_fusion.5 = f32[128,1024]{1,0:T(8,128)S(1)} fusion(f32[1024]{0:T(1024)S(1)} %bitcast.85, f32[512]{0:T(512)S(1)} %bitcast.99, f32[1024]{0:T(1024)S(1)} %bitcast.87, f32[512]{0:T(512)S(1)} %bitcast.97, f32[1024]{0:T(1024)S(1)} %bitcast.83, f32[512]{0:T(512)S(1)} %bitcast.95, f32[128,1024]{1,0:T(8,128)S(1)} %get-tuple-element.787, ...), kind=kOutput, calls=%fused_computation.49.clone.1 | convolution fusion | flops 813957120 | bytes 1329157 | tf_op jit(solution)/shard_map/while/body/eval_jaxpr/dot_general | solution.py:37
  243.6 1.7 fusion.80
  245.4 1.0 copy.6
  246.4 0.0 reduce-scatter.14.cloned.1.call-start
  246.5 0.7 reduce-scatter.14.cloned.1.call-update
  247.2 21.1 %reduce-scatter.18.cloned.1.call-done = f32[256,1]{1,0:T(8,128)} async-done(((f32[1024,1]{1,0:T(8,128)}), f32[256,1]{1,0:T(8,128)}) %reduce-scatter.18.cloned.1.call-update) | async-done | bytes 1040
  268.2 0.9 multiply_bitcast_fusion
  269.2 0.1 copy.9
  269.2 21.2 %reduce-scatter.14.cloned.1.call-done = f32[128,256]{1,0:T(8,128)} async-done(((f32[128,1024]{1,0:T(8,128)}), f32[128,256]{1,0:T(8,128)}) %reduce-scatter.14.cloned.1.call-update) | async-done | bytes 131088 | tf_op jit(solution)/shard_map/reduce_scatter | solution.py:65
  290.4 1.6 multiply_add_fusion
  (43 shorter events, 0.4 us)
Async XLA Ops:
  6.5 33.5 %all-gather.4.cloned.1.call-start = ((), (), s32[]{:S(2)}) async-start(), calls=%async_computation.5 | async-start | bytes 1310720 | tf_op jit(solution)/shard_map/all_gather | solution.py:53
  7.3 97.5 %reduce-scatter.10.cloned.1.call-start = ((), (), s32[]{:S(2)}) async-start(), calls=%async_computation.6 | async-start | bytes 1179648 | tf_op jit(solution)/shard_map/reduce_scatter | solution.py:59
  67.9 1.0 copy-start.2
  67.9 36.9 %copy-start.5 = (f32[3,256]{1,0:T(4,128)S(1)}, f32[3,256]{1,0:T(4,128)}, u32[]{:S(2)}) copy-start(f32[3,256]{1,0:T(4,128)} %param.11) | copy-start | bytes 9220
  68.9 61.2 %all-gather.6.cloned.1.call-start = ((), (), s32[]{:S(2)}) async-start(), calls=%async_computation.7 | async-start | bytes 1179648 | tf_op jit(solution)/shard_map/all_gather | solution.py:62
  104.7 71.7 %reduce-scatter.16.cloned.1.call-start = ((), (), s32[]{:S(2)}) async-start(), calls=%async_computation.11 | async-start | bytes 655360
  153.5 1.1 copy-start.3
  153.5 44.9 %copy-start = (f32[128,256]{1,0:T(8,128)S(1)}, f32[128,256]{1,0:T(8,128)}, u32[]{:S(2)}) copy-start(f32[128,256]{1,0:T(8,128)} %reduce-scatter.10.cloned.1.call-done) | copy-start | bytes 393220
  154.6 43.8 %reduce-scatter.12.cloned.1.call-start = ((), (), s32[]{:S(2)}) async-start(), calls=%async_computation.8 | async-start | bytes 655360 | tf_op jit(solution)/shard_map/reduce_scatter | solution.py:65
  155.2 66.8 %all-gather.8.cloned.1.call-start = ((), (), s32[]{:S(2)}) async-start(), calls=%async_computation.9 | async-start | bytes 1179648 | tf_op jit(solution)/shard_map/all_gather | solution.py:62
  200.0 68.2 %reduce-scatter.18.cloned.1.call-start = ((), (), s32[]{:S(2)}) async-start(), calls=%async_computation.12 | async-start | bytes 655360
  245.4 1.1 copy-start.4
  245.4 45.0 %copy-start.1 = (f32[128,256]{1,0:T(8,128)S(1)}, f32[128,256]{1,0:T(8,128)}, u32[]{:S(2)}) copy-start(f32[128,256]{1,0:T(8,128)} %fusion.54) | copy-start | bytes 393220
  246.4 44.0 %reduce-scatter.14.cloned.1.call-start = ((), (), s32[]{:S(2)}) async-start(), calls=%async_computation.10 | async-start | bytes 655360 | tf_op jit(solution)/shard_map/reduce_scatter | solution.py:65
Sparse Core Ops, SparseCore 0:
  8.9 31.0 all-gather.3
  69.1 35.6 reduce-scatter.9
  106.6 23.5 all-gather.5
  154.7 21.6 reduce-scatter.15
  178.5 19.8 reduce-scatter.11
  200.2 21.8 all-gather.7
  246.6 21.6 reduce-scatter.17
  270.5 19.8 reduce-scatter.13
where the time goes:
time: 299 us
  waiting for transfers between devices  164 us (55%)
  matrix products  59.2 us (20%)
  blocking collectives  37.8 us (13%)
  other arithmetic  18.8 us (6%)
  between operations  13.6 us (5%)
  local copies, waits for them, and re-layouts  4.36 us (1%)
    dot_general x12, matrix products, add(): jnp.dot(values, kernel_tile, precision=lax.Precision.HIGHEST, preferred_e...  59.2 us
    unnamed x10, waiting for transfers between devices  44.2 us
    reduce_scatter x2, waiting for transfers between devices, per_device(): lax.psum_scatter(product, 'tgt', scatter_dimension=1, tiled=True)  42.2 us
    reduce_scatter x1, waiting for transfers between devices, per_device(): lax.psum_scatter(partial_value, 'src', scatter_dimension=1, tiled=True)  35.7 us
    all_gather x2, waiting for transfers between devices, per_device(): columns = lax.all_gather(iterate, 'src', axis=1, tiled=True)  33.9 us
    all_gather x1, blocking collectives, per_device(): lax.all_gather(vol_coords, 'tgt', axis=1, tiled=True)  13.8 us
    reduce_sum x8, other arithmetic, add(): column_sums = column_sums + jnp.sum(kernel_tile, axis=0, keepdims=True)  13.6 us
    all_gather x1, blocking collectives, per_device(): lax.all_gather(ctrl_coords, 'tgt', axis=1, tiled=True)  13.4 us
  transfers between devices with their start and end apart: 8, of which 8 were waited for; matrix products, arithmetic and copies ran while one was open for 1% of the time, Pallas kernels for 0%

commit v1 on v0

v1 whole, which is shorter than its diff:
```python
import functools
import math

import jax
import jax.numpy as jnp
from jax import lax
from jax.experimental import pallas as pl
from jax.experimental.pallas import tpu as pltpu
from jax.sharding import PartitionSpec as P

STEPS = 2
COORDS = 8
FEATURES = 32
ONES = 16
KEPT_BYTES = 20 << 20

neighbours = 64.0
ridge_term = 1.0
omegas = [1.0 / (0.55 + 0.45 * math.cos(math.pi * (2 * k + 1) / 4.0)) for k in range(2)]

BF16 = jnp.bfloat16
F32 = jnp.float32


def parts_of(value, count):
    terms = []
    for _ in range(count):
        term = value.astype(BF16)
        terms.append(term)
        value = value - term.astype(F32)
    return terms


def point_features(points, inverse, as_rows):
    scaled = (points - 0.5) * inverse
    axes = [scaled[d : d + 1] for d in range(3)]
    norm = parts_of(axes[0] * axes[0] + axes[1] * axes[1] + axes[2] * axes[2], 3)
    one = jnp.ones_like(norm[0])
    found = []
    for axis in axes:
        if as_rows:
            a, b, c = parts_of(-2.0 * axis, 3)
            found += [a, a, b, b, a, c]
        else:
            a, b, c = parts_of(axis, 3)
            found += [a, b, a, b, c, a]
    found += norm + [one] * 3 if as_rows else [one] * 3 + norm
    found += [jnp.zeros_like(one)] * (FEATURES - len(found))
    return jnp.concatenate([f.astype(F32) for f in found], axis=0).astype(BF16)


def quarter_wendland(square):
    square = jnp.minimum(jnp.maximum(square, 1e-12), 1.0)
    distance = square * lax.rsqrt(square)
    falloff = 1.0 - distance
    falloff = falloff * falloff
    return (falloff * falloff) * (distance + 0.25)


def evaluate(rows, row_start, cols, high, low, high_start, sub):
    count, width = rows.shape[1], cols.shape[1]
    for at in range(0, count, sub):
        square = lax.dot_general(
            rows[:, at : at + sub], cols, (((0,), (0,)), ((), ())), preferred_element_type=F32
        )
        value = quarter_wendland(square)
        rounded = value.astype(BF16)
        high[row_start + at : row_start + at + sub, high_start : high_start + width] = rounded
        low[row_start + at : row_start + at + sub, high_start : high_start + width] = (
            value - rounded.astype(F32)
        ).astype(BF16)


def product(stacked, half, high, low):
    coarse = jnp.dot(stacked, high, preferred_element_type=F32)
    fine = jnp.dot(stacked[:half], low, preferred_element_type=F32)
    return coarse, fine


def pull_kernel(inverse, half, peers, first, *refs):
    refs = list(refs)
    block = refs.pop(0)
    if first:
        ctrl = [refs.pop(0) for _ in range(peers)]
    else:
        given = refs.pop(0)
        before = [refs.pop(0) for _ in range(peers)]
    if first:
        cols = refs.pop(0)
    after = [refs.pop(0) for _ in range(peers)]
    stacked, rows, high, low = refs
    width = after[0].shape[1]
    a, b = parts_of(block[:half] * 4.0, 2)
    stacked[:half] = a
    stacked[half:] = b
    rows[...] = point_features(block[half : half + 3], inverse, True)
    if first:
        for k in range(peers):
            cols[:, k * width : (k + 1) * width] = point_features(ctrl[k][...], inverse, False)
    else:
        cols = given
    step = 2 if peers % 2 == 0 else 1
    for k in range(0, peers, step):
        evaluate(rows, 0, cols[:, k * width : (k + step) * width], high, low, 0, 128)
        coarse, fine = product(stacked[...], half, high[...], low[...])
        total = coarse[:half] + coarse[half:] + fine
        for i in range(step):
            part = total[:, i * width : (i + 1) * width]
            after[k + i][...] = part if first else before[k + i][...] + part


def keep_kernel(inverse, peers, *refs):
    coords, cols, high, low, rows = refs[:peers], refs[peers], refs[peers + 1], refs[peers + 2], refs[peers + 3]
    count = coords[0].shape[1]
    width = 512 if cols.shape[1] % 512 == 0 else cols.shape[1]
    for k in range(peers):
        rows[...] = point_features(coords[k][3:6], inverse, True)
        for at in range(0, cols.shape[1], width):
            evaluate(rows, k * count, cols[:, at : at + width], high, low, at, 128)


def step_kernel(half, peers, with_sums, *refs):
    blocks, high, low = refs[:peers], refs[peers], refs[peers + 1]
    outs, stacked = refs[peers + 2 : 2 * peers + 2], refs[2 * peers + 2]
    count = blocks[0].shape[1]
    upper = half + (ONES if with_sums else 0)
    for k in range(peers):
        a, b = parts_of(blocks[k][...] * 4.0, 2)
        stacked[:half, k * count : (k + 1) * count] = a
        stacked[upper:, k * count : (k + 1) * count] = b
    if with_sums:
        stacked[half:upper, :] = jnp.full((ONES, stacked.shape[1]), 4.0, BF16)
    step = 2 if peers % 2 == 0 else 1
    for k in range(0, peers, step):
        span = slice(k * count, (k + step) * count)
        coarse, fine = product(stacked[...], upper, high[:, span], low[:, span])
        total = coarse[:half] + coarse[upper:] + fine[:half]
        for i in range(step):
            at = slice(i * count, (i + 1) * count)
            outs[k + i][:half] = total[:, at]
            if with_sums:
                outs[k + i][half:] = coarse[half : half + 8, at] + fine[half : half + 8, at]


def again_kernel(inverse, half, peers, with_sums, *refs):
    blocks, coords, cols = refs[:peers], refs[peers : 2 * peers], refs[2 * peers]
    outs = refs[2 * peers + 1 : 3 * peers + 1]
    stacked, rows, high, low = refs[3 * peers + 1 :]
    count = blocks[0].shape[1]
    upper = half + (ONES if with_sums else 0)
    if with_sums:
        stacked[half:upper, :] = jnp.full((ONES, count), 4.0, BF16)
    for k in range(peers):
        a, b = parts_of(blocks[k][...] * 4.0, 2)
        stacked[:half] = a
        stacked[upper:] = b
        rows[...] = point_features(coords[k][3:6], inverse, True)
        for j in range(peers):
            evaluate(rows, 0, cols[:, j * count : (j + 1) * count], high, low, 0, 128)
            coarse, fine = product(stacked[...], upper, high[...], low[...])
            total = coarse[:half] + coarse[upper:] + fine[:half]
            outs[j][:half] = total if k == 0 else outs[j][:half] + total
            if with_sums:
                sums = coarse[half : half + 8] + fine[half : half + 8]
                outs[j][half:] = sums if k == 0 else outs[j][half:] + sums


def vmem(count):
    return [pl.BlockSpec(memory_space=pltpu.VMEM)] * count


def params():
    return pltpu.CompilerParams(vmem_limit_bytes=24 << 20)


def cost(rows, cols, half, evaluated):
    return pl.CostEstimate(
        flops=rows * cols * (6 * half + (200 if evaluated else 0)), bytes_accessed=4 * rows * half, transcendentals=0
    )


def per_device(vol_grad, vol_coords, ctrl_coords):
    tgt, src = lax.axis_size("tgt"), lax.axis_size("src")
    chips = src // 2
    peers = tgt
    if chips != tgt or src % 2 or tgt & (tgt - 1):
        raise ValueError("unsupported mesh")
    half = vol_grad.shape[0] // 2
    volume, owned = vol_grad.shape[1], ctrl_coords.shape[1]
    overall = owned * tgt * src
    radius = (3.0 * neighbours / (4.0 * math.pi * overall)) ** (1.0 / 3.0)
    inverse = 1.0 / radius
    core = lax.axis_index("src") % 2
    first_core = core == 0

    sibling = [(i, i ^ 1) for i in range(src)]

    def moved(flip, gather):
        pairs = []
        for t in range(tgt):
            for c in range(chips):
                for r in range(2):
                    along_src = (r == 0) == gather
                    to_t, to_c = (t, c ^ flip) if along_src else (t ^ flip, c)
                    pairs.append(((t * chips + c) * 2 + r, (to_t * chips + to_c) * 2 + r))
        return pairs

    gather_pairs = [moved(k, True) for k in range(peers)]
    sum_pairs = [moved(k, False) for k in range(peers)]

    def exchange(value, pairs):
        return lax.ppermute(value, ("tgt", "src"), pairs)

    mine = jnp.where(first_core, vol_grad[:half], vol_grad[half:])
    other = jnp.where(first_core, vol_grad[half:], vol_grad[:half])
    coords = jnp.concatenate(
        [vol_coords, jnp.pad(ctrl_coords, ((0, 0), (0, volume - owned))), jnp.zeros((2, volume), F32)], axis=0
    )
    got = lax.ppermute(jnp.concatenate([other, coords], axis=0), "src", sibling)
    ctrl = jnp.concatenate([ctrl_coords, got[half + 3 : half + 6, :owned]], axis=1)
    chip_coords = jnp.concatenate(
        [
            jnp.concatenate([vol_coords, got[half : half + 3]], axis=1),
            jnp.pad(ctrl, ((0, 0), (0, 2 * (volume - owned)))),
            jnp.zeros((2, 2 * volume), F32),
        ],
        axis=0,
    )
    block = jnp.concatenate([jnp.concatenate([mine, got[:half]], axis=1), chip_coords], axis=0)

    col_ctrl = [ctrl] + [exchange(ctrl, sum_pairs[k]) for k in range(1, peers)]
    blocks = [block] + [exchange(block, gather_pairs[k]) for k in range(1, peers)]

    width = 2 * owned
    cols_shape = jax.ShapeDtypeStruct((FEATURES, peers * width), BF16)
    partial_shapes = [jax.ShapeDtypeStruct((half, width), F32)] * peers
    step = 2 if peers % 2 == 0 else 1
    pull_scratch = [
        pltpu.VMEM((2 * half, 2 * volume), BF16),
        pltpu.VMEM((FEATURES, 2 * volume), BF16),
        pltpu.VMEM((2 * volume, step * width), BF16),
        pltpu.VMEM((2 * volume, step * width), BF16),
    ]
    found = pl.pallas_call(
        functools.partial(pull_kernel, inverse, half, peers, True),
        out_shape=[cols_shape] + partial_shapes,
        in_specs=vmem(1 + peers),
        out_specs=vmem(1 + peers),
        scratch_shapes=pull_scratch,
        compiler_params=params(),
        cost_estimate=cost(2 * volume, peers * width, half, True),
    )(block, *col_ctrl)
    cols, partials = found[0], found[1:]
    for k in range(1, peers):
        partials = pl.pallas_call(
            functools.partial(pull_kernel, inverse, half, peers, False),
            out_shape=partial_shapes,
            in_specs=vmem(2 + peers),
            out_specs=vmem(peers),
            scratch_shapes=pull_scratch,
            input_output_aliases={2 + i: i for i in range(peers)},
            compiler_params=params(),
            cost_estimate=cost(2 * volume, peers * width, half, True),
        )(blocks[k], cols, *partials)

    def summed(values):
        total = values[0]
        for k in range(1, peers):
            total = total + exchange(values[k], sum_pairs[k])
        return total

    pullback = summed(partials)

    kept = (peers * width) ** 2 * 4 <= KEPT_BYTES
    coords_spec = [pl.BlockSpec((COORDS, width), lambda _: (half // COORDS, 0))] * peers
    if kept:
        high, low = pl.pallas_call(
            functools.partial(keep_kernel, inverse, peers),
            grid=(1,),
            out_shape=[pltpu.VMEM((peers * width, peers * width), BF16)] * 2,
            in_specs=coords_spec + vmem(1),
            out_specs=vmem(2),
            scratch_shapes=[pltpu.VMEM((FEATURES, width), BF16)],
            compiler_params=params(),
            cost_estimate=cost(peers * width, peers * width, 0, True),
        )(*blocks, cols)

    iterate = pullback
    for sweep in range(STEPS):
        arrived = [iterate] + [exchange(iterate, gather_pairs[k]) for k in range(1, peers)]
        with_sums = sweep == 0
        upper = half + (ONES if with_sums else 0)
        out_rows = half + (8 if with_sums else 0)
        out_shape = [jax.ShapeDtypeStruct((out_rows, width), F32)] * peers
        if kept:
            products = pl.pallas_call(
                functools.partial(step_kernel, half, peers, with_sums),
                out_shape=out_shape,
                in_specs=vmem(peers + 2),
                out_specs=vmem(peers),
                scratch_shapes=[pltpu.VMEM((upper + half, peers * width), BF16)],
                compiler_params=params(),
                cost_estimate=cost(peers * width, peers * width, half, False),
            )(
                *arrived,
                pltpu.with_memory_space_constraint(high, pltpu.VMEM),
                pltpu.with_memory_space_constraint(low, pltpu.VMEM),
            )
        else:
            products = pl.pallas_call(
                functools.partial(again_kernel, inverse, half, peers, with_sums),
                grid=(1,),
                out_shape=out_shape,
                in_specs=vmem(peers) + coords_spec + vmem(1),
                out_specs=vmem(peers),
                scratch_shapes=[
                    pltpu.VMEM((upper + half, width), BF16),
                    pltpu.VMEM((FEATURES, width), BF16),
                    pltpu.VMEM((width, width), BF16),
                    pltpu.VMEM((width, width), BF16),
                ],
                compiler_params=params(),
                cost_estimate=cost(peers * width, peers * width, half, True),
            )(*arrived, *blocks, cols)
        total = summed(products)
        if with_sums:
            scaling = 1.0 / (total[half : half + 1] + ridge_term)
        iterate = iterate + omegas[sweep] * scaling * (pullback - total[:half] - iterate)

    own, theirs = iterate[:, :owned], iterate[:, owned:]
    back = lax.ppermute(theirs, "src", sibling)
    return jnp.where(
        first_core, jnp.concatenate([own, back], axis=0), jnp.concatenate([back, own], axis=0)
    )


def solution(mesh):
    placed = (P(None, ("tgt", "src")), P(None, ("tgt", "src")), P(None, ("tgt", "src")))
    return jax.shard_map(
        per_device, mesh=mesh, in_specs=placed, out_specs=P(None, ("tgt", "src")), check_vma=False
    )
```

time: 299 us -> 103 us (0.34)
  waiting for transfers between devices: 164 us -> 33.4 us
  matrix products: 59.2 us -> 0 us
  blocking collectives: 37.8 us -> 0 us
  Pallas kernels: 0 us -> 32.7 us
  starting transfers between devices: 0.28 us -> 32.1 us
  other arithmetic: 18.8 us -> 4.13 us
  between operations: 13.6 us -> 0.19 us
  local copies, waits for them, and re-layouts: 4.36 us -> 0.1 us
    reduce_scatter x3 -> x0, waiting for transfers between devices: 77.9 us -> none  [the longest x2 42.2 us: per_device(): lax.psum_scatter(product, 'tgt', scatter_dimension=1, tiled=True)]
    dot_general x12 -> x0, matrix products: 59.2 us -> none  [add(): jnp.dot(values, kernel_tile, precision=lax.Precision.HIGHEST, preferred_e...]
    unnamed x10 -> x0, waiting for transfers between devices: 44.2 us -> none
    all_gather x3 -> x0, waiting for transfers between devices: 42.2 us -> none  [the longest x2 33.9 us: per_device(): columns = lax.all_gather(iterate, 'src', axis=1, tiled=True)]
    all_gather x3 -> x0, blocking collectives: 37.8 us -> none  [the longest x1 13.8 us: per_device(): lax.all_gather(vol_coords, 'tgt', axis=1, tiled=True)]
    ppermute x0 -> x23, waiting for transfers between devices: none -> 33.4 us  [the longest x21 31.2 us: exchange(): return lax.ppermute(value, ('tgt', 'src'), pairs)]
    pallas_call x0 -> x7, Pallas kernels: none -> 32.7 us  [the longest x3 14.4 us: per_device(): pl.pallas_call(functools.partial(pull_kernel, inverse, half, peers, False...]
    ppermute x0 -> x23, starting transfers between devices: none -> 32.1 us  [the longest x21 31.6 us: exchange(): return lax.ppermute(value, ('tgt', 'src'), pairs)]
  transfers between devices with their start and end apart: 8 -> 23, of which waited for: 8 -> 12; matrix products, arithmetic and copies ran while one was open for 1% -> 0% of each run, Pallas kernels for 0% -> 22%
where the time goes in v1:
time: 103 us
  waiting for transfers between devices  33.4 us (32%)
  Pallas kernels  32.7 us (32%)
  starting transfers between devices  32.1 us (31%)
  other arithmetic  4.13 us (4%)
    ppermute x21, starting transfers between devices, exchange(): return lax.ppermute(value, ('tgt', 'src'), pairs)  31.6 us
    ppermute x21, waiting for transfers between devices, exchange(): return lax.ppermute(value, ('tgt', 'src'), pairs)  31.2 us
    pallas_call x3, Pallas kernels, per_device(): pl.pallas_call(functools.partial(pull_kernel, inverse, half, peers, False...  14.4 us
    pallas_call x1, Pallas kernels, per_device(): pl.pallas_call(functools.partial(keep_kernel, inverse, peers), grid=(1,),...  7.94 us
    pallas_call x2, Pallas kernels, per_device(): pl.pallas_call(functools.partial(step_kernel, half, peers, with_sums), ou...  5.51 us
    pallas_call x1, Pallas kernels, per_device(): pl.pallas_call(functools.partial(pull_kernel, inverse, half, peers, True)...  4.77 us
  transfers between devices with their start and end apart: 23, of which 12 were waited for; matrix products, arithmetic and copies ran while one was open for 0% of the time, Pallas kernels for 22%

profile of v1, /device:TPU:0, one launch (start us, length us, event | category | flops | bytes accessed | tf_op | source)
XLA Modules:
  0.0 102.7 jit_solution(16931024494570271809)
XLA Ops:
  0.0 0.1 pad.25.clone
  0.1 1.0 slice_select_fusion.1
  1.1 0.8 fusion.2
  1.9 0.5 collective-permute-start
  2.4 1.0 collective-permute-done
  3.4 0.7 pad_maximum_fusion.refs_1_
  4.1 0.8 fusion.refs_0_
  4.9 2.9 %collective-permute-start.6 = (f32[72,1024]{1,0:T(8,128)S(1)}, f32[72,1024]{1,0:T(8,128)S(1)}, u32[]{:S(2)}, u32[]{:S(2)}) collective-permute-start(f32[72,1024]{1,0:T(8,128)S(1)} %fusion.refs_0_), channel_id=1, source_target_pairs={{0,2},{1,9},{2,0},{3,11},{4,6},{5,13},{6,4},{7,15},{8,10},{9,1},{1... | collective-permute-start | bytes 884744 | tf_op jit(solution)/shard_map/ppermute | solution.py:212
  7.8 1.5 %collective-permute-start.5 = (f32[72,1024]{1,0:T(8,128)S(1)}, f32[72,1024]{1,0:T(8,128)S(1)}, u32[]{:S(2)}, u32[]{:S(2)}) collective-permute-start(f32[72,1024]{1,0:T(8,128)S(1)} %fusion.refs_0_), channel_id=1, source_target_pairs={{0,4},{1,17},{2,6},{3,19},{4,0},{5,21},{6,2},{7,23},{8,12},{9,25},... | collective-permute-start | bytes 884744 | tf_op jit(solution)/shard_map/ppermute | solution.py:212
  9.3 3.6 %collective-permute-start.4 = (f32[3,512]{1,0:T(4,128)S(1)}, f32[3,512]{1,0:T(4,128)S(1)}, u32[]{:S(2)}, u32[]{:S(2)}) collective-permute-start(f32[3,512]{1,0:T(4,128)S(1)} %pad_maximum_fusion.refs_1_), channel_id=1, source_target_pairs={{0,24},{1,7},{2,26},{3,5},{4,28},{5,3},{6,30},{7,1},{8,16},{9,15},... | collective-permute-start | bytes 18440 | tf_op jit(solution)/shard_map/ppermute | solution.py:212
  12.9 0.0 collective-permute-start.3
  12.9 0.8 collective-permute-start.2
  13.7 1.3 %collective-permute-done.4.refs_4_ = f32[3,512]{1,0:T(4,128)S(1)} collective-permute-done((f32[3,512]{1,0:T(4,128)S(1)}, f32[3,512]{1,0:T(4,128)S(1)}, u32[]{:S(2)}, u32[]{:S(2)}) %collective-permute-start.4) | collective-permute-done | bytes 6176 | tf_op jit(solution)/shard_map/ppermute | solution.py:212
  15.0 0.2 collective-permute-start.1
  15.2 2.7 %collective-permute-done.3.refs_3_ = f32[3,512]{1,0:T(4,128)S(1)} collective-permute-done((f32[3,512]{1,0:T(4,128)S(1)}, f32[3,512]{1,0:T(4,128)S(1)}, u32[]{:S(2)}, u32[]{:S(2)}) %collective-permute-start.3) | collective-permute-done | bytes 6176 | tf_op jit(solution)/shard_map/ppermute | solution.py:212
  17.9 0.0 collective-permute-done.2.refs_2_
  17.9 4.8 %shard_map.37 = (bf16[32,2048]{1,0:T(8,128)(2,1)S(1)}, f32[64,512]{1,0:T(8,128)S(1)}, f32[64,512]{1,0:T(8,128)S(1)}, f32[64,512]{1,0:T(8,128)S(1)}, f32[64,512]{1,0:T(8,128)S(1)}) custom-call(f32[72,1024]{1,0:T(8,128)S(1)} %fusion.refs_0_, f32[3,512]{1,0:T(4,128)S(1)} %pad_maximum_fusion.refs_1_, f32[3,512]{1,0:T(4,128)S(1)} %collective-permute-done.2.refs_2_, ...), custom_call_target="tpu_custom_call" | custom-call | flops 1224736768 | bytes 262144 | tf_op jit(solution)/shard_map/pallas_call | solution.py:244
  22.7 0.0 collective-permute-done.6.refs_0_.refs_1_
  22.7 4.8 %shard_map.38 = (f32[64,512]{1,0:T(8,128)S(1)}, f32[64,512]{1,0:T(8,128)S(1)}, f32[64,512]{1,0:T(8,128)S(1)}, f32[64,512]{1,0:T(8,128)S(1)}) custom-call(f32[72,1024]{1,0:T(8,128)S(1)} %collective-permute-done.6.refs_0_.refs_1_, ...), custom_call_target="tpu_custom_call", output_to_operand_aliasing={{0}: (2, {}), {1}: (3, {}), {2}: (4, {}), {3}: (5, {})} | custom-call | flops 1224736768 | bytes 262144 | tf_op jit(solution)/shard_map/pallas_call | solution.py:255
  27.5 0.0 collective-permute-done.5.refs_0_.refs_2_
  27.5 4.9 %shard_map.39 = (f32[64,512]{1,0:T(8,128)S(1)}, f32[64,512]{1,0:T(8,128)S(1)}, f32[64,512]{1,0:T(8,128)S(1)}, f32[64,512]{1,0:T(8,128)S(1)}) custom-call(f32[72,1024]{1,0:T(8,128)S(1)} %collective-permute-done.5.refs_0_.refs_2_, ...), custom_call_target="tpu_custom_call", output_to_operand_aliasing={{0}: (2, {}), {1}: (3, {}), {2}: (4, {}), {3}: (5, {})} | custom-call | flops 1224736768 | bytes 262144 | tf_op jit(solution)/shard_map/pallas_call | solution.py:255
  32.4 0.0 collective-permute-done.1.refs_0_.refs_3_
  32.4 4.8 %shard_map.40 = (f32[64,512]{1,0:T(8,128)S(1)}, f32[64,512]{1,0:T(8,128)S(1)}, f32[64,512]{1,0:T(8,128)S(1)}, f32[64,512]{1,0:T(8,128)S(1)}) custom-call(f32[72,1024]{1,0:T(8,128)S(1)} %collective-permute-done.1.refs_0_.refs_3_, ...), custom_call_target="tpu_custom_call", output_to_operand_aliasing={{0}: (2, {}), {1}: (3, {}), {2}: (4, {}), {3}: (5, {})} | custom-call | flops 1224736768 | bytes 262144 | tf_op jit(solution)/shard_map/pallas_call | solution.py:255
  37.2 0.1 collective-permute-start.7
  37.3 5.2 %collective-permute-start.8 = (f32[64,512]{1,0:T(8,128)S(1)}, f32[64,512]{1,0:T(8,128)S(1)}, u32[]{:S(2)}, u32[]{:S(2)}) collective-permute-start(f32[64,512]{1,0:T(8,128)S(1)} %get-tuple-element.47), channel_id=1, source_target_pairs={{0,16},{1,5},{2,18},{3,7},{4,20},{5,1},{6,22},{7,3},{8,24},{9,13},... | collective-permute-start | bytes 393224 | tf_op jit(solution)/shard_map/ppermute | solution.py:212
  42.5 0.0 collective-permute-start.9
  42.5 0.0 collective-permute-done.7
  42.5 9.9 %collective-permute-done.8 = f32[64,512]{1,0:T(8,128)S(1)} collective-permute-done((f32[64,512]{1,0:T(8,128)S(1)}, f32[64,512]{1,0:T(8,128)S(1)}, u32[]{:S(2)}, u32[]{:S(2)}) %collective-permute-start.8) | collective-permute-done | bytes 131104 | tf_op jit(solution)/shard_map/ppermute | solution.py:212
  52.4 0.0 collective-permute-done.9
  52.5 2.8 %collective-permute-start.12 = (f32[64,512]{1,0:T(8,128)S(1)}, f32[64,512]{1,0:T(8,128)S(1)}, u32[]{:S(2)}, u32[]{:S(2)}) collective-permute-start(f32[64,512]{1,0:T(8,128)S(1)} %add_add_fusion.1.refs_0_), channel_id=1, source_target_pairs={{0,6},{1,25},{2,4},{3,27},{4,2},{5,29},{6,0},{7,31},{8,14},{9,17},... | collective-permute-start | bytes 393224 | tf_op jit(solution)/shard_map/ppermute | solution.py:212
  55.3 0.0 collective-permute-start.11
  55.3 0.7 collective-permute-start.10
  56.0 7.9 %shard_map.41 = (bf16[2048,2048]{1,0:T(8,128)(2,1)S(1)}, bf16[2048,2048]{1,0:T(8,128)(2,1)S(1)}) custom-call(f32[72,1024]{1,0:T(8,128)S(1)} %fusion.refs_0_, f32[72,1024]{1,0:T(8,128)S(1)} %collective-permute-done.6.refs_0_.refs_1_, f32[72,1024]{1,0:T(8,128)S(1)} %collective-permute-done.5.refs_0_.refs_2_, ...), custom_call_target="tpu_custom_call" | custom-call | flops 838860800 | tf_op jit(solution)/shard_map/pallas_call | solution.py:277
  64.0 0.0 collective-permute-done.12.refs_3_
  64.0 0.0 collective-permute-done.11.refs_2_
  64.0 0.0 collective-permute-done.10.refs_1_
  64.0 2.8 %shard_map.42 = (f32[72,512]{1,0:T(8,128)S(1)}, f32[72,512]{1,0:T(8,128)S(1)}, f32[72,512]{1,0:T(8,128)S(1)}, f32[72,512]{1,0:T(8,128)S(1)}) custom-call(f32[64,512]{1,0:T(8,128)S(1)} %add_add_fusion.1.refs_0_, f32[64,512]{1,0:T(8,128)S(1)} %collective-permute-done.10.refs_1_, f32[64,512]{1,0:T(8,128)S(1)} %collective-permute-done.11.refs_2_, ...), custom_call_target="tpu_custom_call" | custom-call | flops 1610612736 | bytes 524288 | tf_op jit(solution)/shard_map/pallas_call | solution.py:296
  66.8 3.0 %collective-permute-start.13 = (f32[72,512]{1,0:T(8,128)S(1)}, f32[72,512]{1,0:T(8,128)S(1)}, u32[]{:S(2)}, u32[]{:S(2)}) collective-permute-start(f32[72,512]{1,0:T(8,128)S(1)} %get-tuple-element.52), channel_id=1, source_target_pairs={{0,8},{1,3},{2,10},{3,1},{4,12},{5,7},{6,14},{7,5},{8,0},{9,11},{1... | collective-permute-start | bytes 442376 | tf_op jit(solution)/shard_map/ppermute | solution.py:212
  69.8 0.5 collective-permute-start.14
  70.4 1.9 %collective-permute-start.15 = (f32[72,512]{1,0:T(8,128)S(1)}, f32[72,512]{1,0:T(8,128)S(1)}, u32[]{:S(2)}, u32[]{:S(2)}) collective-permute-start(f32[72,512]{1,0:T(8,128)S(1)} %get-tuple-element.54), channel_id=1, source_target_pairs={{0,24},{1,7},{2,26},{3,5},{4,28},{5,3},{6,30},{7,1},{8,16},{9,15},... | collective-permute-start | bytes 442376 | tf_op jit(solution)/shard_map/ppermute | solution.py:212
  72.3 3.1 %collective-permute-done.13 = f32[72,512]{1,0:T(8,128)S(1)} collective-permute-done((f32[72,512]{1,0:T(8,128)S(1)}, f32[72,512]{1,0:T(8,128)S(1)}, u32[]{:S(2)}, u32[]{:S(2)}) %collective-permute-start.13) | collective-permute-done | bytes 147488 | tf_op jit(solution)/shard_map/ppermute | solution.py:212
  75.4 3.6 %collective-permute-done.14 = f32[72,512]{1,0:T(8,128)S(1)} collective-permute-done((f32[72,512]{1,0:T(8,128)S(1)}, f32[72,512]{1,0:T(8,128)S(1)}, u32[]{:S(2)}, u32[]{:S(2)}) %collective-permute-start.14) | collective-permute-done | bytes 147488 | tf_op jit(solution)/shard_map/ppermute | solution.py:212
  79.1 0.0 collective-permute-done.15
  79.2 1.7 %collective-permute-start.18 = (f32[64,512]{1,0:T(8,128)S(1)}, f32[64,512]{1,0:T(8,128)S(1)}, u32[]{:S(2)}, u32[]{:S(2)}) collective-permute-start(f32[64,512]{1,0:T(8,128)S(1)} %fusion.5.refs_0_), channel_id=1, source_target_pairs={{0,6},{1,25},{2,4},{3,27},{4,2},{5,29},{6,0},{7,31},{8,14},{9,17},... | collective-permute-start | bytes 393224 | tf_op jit(solution)/shard_map/ppermute | solution.py:212
  80.8 1.2 %collective-permute-start.17 = (f32[64,512]{1,0:T(8,128)S(1)}, f32[64,512]{1,0:T(8,128)S(1)}, u32[]{:S(2)}, u32[]{:S(2)}) collective-permute-start(f32[64,512]{1,0:T(8,128)S(1)} %fusion.5.refs_0_), channel_id=1, source_target_pairs={{0,4},{1,17},{2,6},{3,19},{4,0},{5,21},{6,2},{7,23},{8,12},{9,25},... | collective-permute-start | bytes 393224 | tf_op jit(solution)/shard_map/ppermute | solution.py:212
  82.0 0.7 collective-permute-start.16
  82.7 2.4 %collective-permute-done.18.refs_3_ = f32[64,512]{1,0:T(8,128)S(1)} collective-permute-done((f32[64,512]{1,0:T(8,128)S(1)}, f32[64,512]{1,0:T(8,128)S(1)}, u32[]{:S(2)}, u32[]{:S(2)}) %collective-permute-start.18) | collective-permute-done | bytes 131104 | tf_op jit(solution)/shard_map/ppermute | solution.py:212
  85.2 1.3 %collective-permute-done.17.refs_2_ = f32[64,512]{1,0:T(8,128)S(1)} collective-permute-done((f32[64,512]{1,0:T(8,128)S(1)}, f32[64,512]{1,0:T(8,128)S(1)}, u32[]{:S(2)}, u32[]{:S(2)}) %collective-permute-start.17) | collective-permute-done | bytes 131104 | tf_op jit(solution)/shard_map/ppermute | solution.py:212
  86.5 0.5 collective-permute-done.16.refs_1_
  87.0 2.7 %shard_map.43 = (f32[64,512]{1,0:T(8,128)S(1)}, f32[64,512]{1,0:T(8,128)S(1)}, f32[64,512]{1,0:T(8,128)S(1)}, f32[64,512]{1,0:T(8,128)S(1)}) custom-call(f32[64,512]{1,0:T(8,128)S(1)} %fusion.5.refs_0_, f32[64,512]{1,0:T(8,128)S(1)} %collective-permute-done.16.refs_1_, f32[64,512]{1,0:T(8,128)S(1)} %collective-permute-done.17.refs_2_, ...), custom_call_target="tpu_custom_call" | custom-call | flops 1610612736 | bytes 524288 | tf_op jit(solution)/shard_map/pallas_call | solution.py:296
  89.7 2.2 %collective-permute-start.19 = (f32[64,512]{1,0:T(8,128)S(1)}, f32[64,512]{1,0:T(8,128)S(1)}, u32[]{:S(2)}, u32[]{:S(2)}) collective-permute-start(f32[64,512]{1,0:T(8,128)S(1)} %get-tuple-element.56), channel_id=1, source_target_pairs={{0,8},{1,3},{2,10},{3,1},{4,12},{5,7},{6,14},{7,5},{8,0},{9,11},{1... | collective-permute-start | bytes 393224 | tf_op jit(solution)/shard_map/ppermute | solution.py:212
  91.9 0.1 collective-permute-start.20
  92.1 2.3 %collective-permute-start.21 = (f32[64,512]{1,0:T(8,128)S(1)}, f32[64,512]{1,0:T(8,128)S(1)}, u32[]{:S(2)}, u32[]{:S(2)}) collective-permute-start(f32[64,512]{1,0:T(8,128)S(1)} %get-tuple-element.58), channel_id=1, source_target_pairs={{0,24},{1,7},{2,26},{3,5},{4,28},{5,3},{6,30},{7,1},{8,16},{9,15},... | collective-permute-start | bytes 393224 | tf_op jit(solution)/shard_map/ppermute | solution.py:212
  94.4 0.5 collective-permute-done.19
  94.9 5.7 %collective-permute-done.20 = f32[64,512]{1,0:T(8,128)S(1)} collective-permute-done((f32[64,512]{1,0:T(8,128)S(1)}, f32[64,512]{1,0:T(8,128)S(1)}, u32[]{:S(2)}, u32[]{:S(2)}) %collective-permute-start.20) | collective-permute-done | bytes 131104 | tf_op jit(solution)/shard_map/ppermute | solution.py:212
  100.6 0.0 collective-permute-done.21
  100.6 0.1 multiply_add_fusion
  100.7 0.1 collective-permute-start.22
  100.8 1.2 %collective-permute-done.22 = f32[64,256]{1,0:T(8,128)S(1)} collective-permute-done((f32[64,256]{1,0:T(8,128)S(1)}, f32[64,256]{1,0:T(8,128)S(1)}, u32[]{:S(2)}, u32[]{:S(2)}) %collective-permute-start.22) | collective-permute-done | bytes 65568 | tf_op jit(solution)/shard_map/ppermute | solution.py:331
  102.0 0.7 maximum_select_fusion
  (10 shorter events, 0.2 us)
Async XLA Ops:
  1.9 1.5 %collective-permute-start = (f32[72,512]{1,0:T(8,128)S(1)}, f32[72,512]{1,0:T(8,128)S(1)}, u32[]{:S(2)}, u32[]{:S(2)}) collective-permute-start(f32[72,512]{1,0:T(8,128)S(1)} %fusion.2), channel_id=1, source_target_pairs={{0,1},{1,0},{2,3},{3,2},{4,5},{5,4},{6,7},{7,6},{8,9},{9,8},{10,11... | collective-permute-start | bytes 442376 | tf_op jit(solution)/shard_map/ppermute | solution.py:219
  4.9 17.8 %collective-permute-start.6 = (f32[72,1024]{1,0:T(8,128)S(1)}, f32[72,1024]{1,0:T(8,128)S(1)}, u32[]{:S(2)}, u32[]{:S(2)}) collective-permute-start(f32[72,1024]{1,0:T(8,128)S(1)} %fusion.refs_0_), channel_id=1, source_target_pairs={{0,2},{1,9},{2,0},{3,11},{4,6},{5,13},{6,4},{7,15},{8,10},{9,1},{1... | collective-permute-start | bytes 884744 | tf_op jit(solution)/shard_map/ppermute | solution.py:212
  7.8 19.7 %collective-permute-start.5 = (f32[72,1024]{1,0:T(8,128)S(1)}, f32[72,1024]{1,0:T(8,128)S(1)}, u32[]{:S(2)}, u32[]{:S(2)}) collective-permute-start(f32[72,1024]{1,0:T(8,128)S(1)} %fusion.refs_0_), channel_id=1, source_target_pairs={{0,4},{1,17},{2,6},{3,19},{4,0},{5,21},{6,2},{7,23},{8,12},{9,25},... | collective-permute-start | bytes 884744 | tf_op jit(solution)/shard_map/ppermute | solution.py:212
  9.3 5.7 %collective-permute-start.4 = (f32[3,512]{1,0:T(4,128)S(1)}, f32[3,512]{1,0:T(4,128)S(1)}, u32[]{:S(2)}, u32[]{:S(2)}) collective-permute-start(f32[3,512]{1,0:T(4,128)S(1)} %pad_maximum_fusion.refs_1_), channel_id=1, source_target_pairs={{0,24},{1,7},{2,26},{3,5},{4,28},{5,3},{6,30},{7,1},{8,16},{9,15},... | collective-permute-start | bytes 18440 | tf_op jit(solution)/shard_map/ppermute | solution.py:212
  12.9 5.0 %collective-permute-start.3 = (f32[3,512]{1,0:T(4,128)S(1)}, f32[3,512]{1,0:T(4,128)S(1)}, u32[]{:S(2)}, u32[]{:S(2)}) collective-permute-start(f32[3,512]{1,0:T(4,128)S(1)} %pad_maximum_fusion.refs_1_), channel_id=1, source_target_pairs={{0,16},{1,5},{2,18},{3,7},{4,20},{5,1},{6,22},{7,3},{8,24},{9,13},... | collective-permute-start | bytes 18440 | tf_op jit(solution)/shard_map/ppermute | solution.py:212
  12.9 5.0 %collective-permute-start.2 = (f32[3,512]{1,0:T(4,128)S(1)}, f32[3,512]{1,0:T(4,128)S(1)}, u32[]{:S(2)}, u32[]{:S(2)}) collective-permute-start(f32[3,512]{1,0:T(4,128)S(1)} %pad_maximum_fusion.refs_1_), channel_id=1, source_target_pairs={{0,8},{1,3},{2,10},{3,1},{4,12},{5,7},{6,14},{7,5},{8,0},{9,11},{1... | collective-permute-start | bytes 18440 | tf_op jit(solution)/shard_map/ppermute | solution.py:212
  15.0 17.4 %collective-permute-start.1 = (f32[72,1024]{1,0:T(8,128)S(1)}, f32[72,1024]{1,0:T(8,128)S(1)}, u32[]{:S(2)}, u32[]{:S(2)}) collective-permute-start(f32[72,1024]{1,0:T(8,128)S(1)} %fusion.refs_0_), channel_id=1, source_target_pairs={{0,6},{1,25},{2,4},{3,27},{4,2},{5,29},{6,0},{7,31},{8,14},{9,17},... | collective-permute-start | bytes 884744 | tf_op jit(solution)/shard_map/ppermute | solution.py:212
  37.2 5.3 %collective-permute-start.7 = (f32[64,512]{1,0:T(8,128)S(1)}, f32[64,512]{1,0:T(8,128)S(1)}, u32[]{:S(2)}, u32[]{:S(2)}) collective-permute-start(f32[64,512]{1,0:T(8,128)S(1)} %get-tuple-element.46), channel_id=1, source_target_pairs={{0,8},{1,3},{2,10},{3,1},{4,12},{5,7},{6,14},{7,5},{8,0},{9,11},{1... | collective-permute-start | bytes 393224 | tf_op jit(solution)/shard_map/ppermute | solution.py:212
  37.3 15.1 %collective-permute-start.8 = (f32[64,512]{1,0:T(8,128)S(1)}, f32[64,512]{1,0:T(8,128)S(1)}, u32[]{:S(2)}, u32[]{:S(2)}) collective-permute-start(f32[64,512]{1,0:T(8,128)S(1)} %get-tuple-element.47), channel_id=1, source_target_pairs={{0,16},{1,5},{2,18},{3,7},{4,20},{5,1},{6,22},{7,3},{8,24},{9,13},... | collective-permute-start | bytes 393224 | tf_op jit(solution)/shard_map/ppermute | solution.py:212
  42.5 9.9 %collective-permute-start.9 = (f32[64,512]{1,0:T(8,128)S(1)}, f32[64,512]{1,0:T(8,128)S(1)}, u32[]{:S(2)}, u32[]{:S(2)}) collective-permute-start(f32[64,512]{1,0:T(8,128)S(1)} %get-tuple-element.48), channel_id=1, source_target_pairs={{0,24},{1,7},{2,26},{3,5},{4,28},{5,3},{6,30},{7,1},{8,16},{9,15},... | collective-permute-start | bytes 393224 | tf_op jit(solution)/shard_map/ppermute | solution.py:212
  52.5 11.5 %collective-permute-start.12 = (f32[64,512]{1,0:T(8,128)S(1)}, f32[64,512]{1,0:T(8,128)S(1)}, u32[]{:S(2)}, u32[]{:S(2)}) collective-permute-start(f32[64,512]{1,0:T(8,128)S(1)} %add_add_fusion.1.refs_0_), channel_id=1, source_target_pairs={{0,6},{1,25},{2,4},{3,27},{4,2},{5,29},{6,0},{7,31},{8,14},{9,17},... | collective-permute-start | bytes 393224 | tf_op jit(solution)/shard_map/ppermute | solution.py:212
  55.3 8.7 %collective-permute-start.11 = (f32[64,512]{1,0:T(8,128)S(1)}, f32[64,512]{1,0:T(8,128)S(1)}, u32[]{:S(2)}, u32[]{:S(2)}) collective-permute-start(f32[64,512]{1,0:T(8,128)S(1)} %add_add_fusion.1.refs_0_), channel_id=1, source_target_pairs={{0,4},{1,17},{2,6},{3,19},{4,0},{5,21},{6,2},{7,23},{8,12},{9,25},... | collective-permute-start | bytes 393224 | tf_op jit(solution)/shard_map/ppermute | solution.py:212
  55.3 8.7 %collective-permute-start.10 = (f32[64,512]{1,0:T(8,128)S(1)}, f32[64,512]{1,0:T(8,128)S(1)}, u32[]{:S(2)}, u32[]{:S(2)}) collective-permute-start(f32[64,512]{1,0:T(8,128)S(1)} %add_add_fusion.1.refs_0_), channel_id=1, source_target_pairs={{0,2},{1,9},{2,0},{3,11},{4,6},{5,13},{6,4},{7,15},{8,10},{9,1},{1... | collective-permute-start | bytes 393224 | tf_op jit(solution)/shard_map/ppermute | solution.py:212
  66.8 8.6 %collective-permute-start.13 = (f32[72,512]{1,0:T(8,128)S(1)}, f32[72,512]{1,0:T(8,128)S(1)}, u32[]{:S(2)}, u32[]{:S(2)}) collective-permute-start(f32[72,512]{1,0:T(8,128)S(1)} %get-tuple-element.52), channel_id=1, source_target_pairs={{0,8},{1,3},{2,10},{3,1},{4,12},{5,7},{6,14},{7,5},{8,0},{9,11},{1... | collective-permute-start | bytes 442376 | tf_op jit(solution)/shard_map/ppermute | solution.py:212
  69.8 9.2 %collective-permute-start.14 = (f32[72,512]{1,0:T(8,128)S(1)}, f32[72,512]{1,0:T(8,128)S(1)}, u32[]{:S(2)}, u32[]{:S(2)}) collective-permute-start(f32[72,512]{1,0:T(8,128)S(1)} %get-tuple-element.53), channel_id=1, source_target_pairs={{0,16},{1,5},{2,18},{3,7},{4,20},{5,1},{6,22},{7,3},{8,24},{9,13},... | collective-permute-start | bytes 442376 | tf_op jit(solution)/shard_map/ppermute | solution.py:212
  70.4 8.7 %collective-permute-start.15 = (f32[72,512]{1,0:T(8,128)S(1)}, f32[72,512]{1,0:T(8,128)S(1)}, u32[]{:S(2)}, u32[]{:S(2)}) collective-permute-start(f32[72,512]{1,0:T(8,128)S(1)} %get-tuple-element.54), channel_id=1, source_target_pairs={{0,24},{1,7},{2,26},{3,5},{4,28},{5,3},{6,30},{7,1},{8,16},{9,15},... | collective-permute-start | bytes 442376 | tf_op jit(solution)/shard_map/ppermute | solution.py:212
  79.2 6.0 %collective-permute-start.18 = (f32[64,512]{1,0:T(8,128)S(1)}, f32[64,512]{1,0:T(8,128)S(1)}, u32[]{:S(2)}, u32[]{:S(2)}) collective-permute-start(f32[64,512]{1,0:T(8,128)S(1)} %fusion.5.refs_0_), channel_id=1, source_target_pairs={{0,6},{1,25},{2,4},{3,27},{4,2},{5,29},{6,0},{7,31},{8,14},{9,17},... | collective-permute-start | bytes 393224 | tf_op jit(solution)/shard_map/ppermute | solution.py:212
  80.8 5.7 %collective-permute-start.17 = (f32[64,512]{1,0:T(8,128)S(1)}, f32[64,512]{1,0:T(8,128)S(1)}, u32[]{:S(2)}, u32[]{:S(2)}) collective-permute-start(f32[64,512]{1,0:T(8,128)S(1)} %fusion.5.refs_0_), channel_id=1, source_target_pairs={{0,4},{1,17},{2,6},{3,19},{4,0},{5,21},{6,2},{7,23},{8,12},{9,25},... | collective-permute-start | bytes 393224 | tf_op jit(solution)/shard_map/ppermute | solution.py:212
  82.0 5.0 %collective-permute-start.16 = (f32[64,512]{1,0:T(8,128)S(1)}, f32[64,512]{1,0:T(8,128)S(1)}, u32[]{:S(2)}, u32[]{:S(2)}) collective-permute-start(f32[64,512]{1,0:T(8,128)S(1)} %fusion.5.refs_0_), channel_id=1, source_target_pairs={{0,2},{1,9},{2,0},{3,11},{4,6},{5,13},{6,4},{7,15},{8,10},{9,1},{1... | collective-permute-start | bytes 393224 | tf_op jit(solution)/shard_map/ppermute | solution.py:212
  89.7 5.2 %collective-permute-start.19 = (f32[64,512]{1,0:T(8,128)S(1)}, f32[64,512]{1,0:T(8,128)S(1)}, u32[]{:S(2)}, u32[]{:S(2)}) collective-permute-start(f32[64,512]{1,0:T(8,128)S(1)} %get-tuple-element.56), channel_id=1, source_target_pairs={{0,8},{1,3},{2,10},{3,1},{4,12},{5,7},{6,14},{7,5},{8,0},{9,11},{1... | collective-permute-start | bytes 393224 | tf_op jit(solution)/shard_map/ppermute | solution.py:212
  91.9 8.7 %collective-permute-start.20 = (f32[64,512]{1,0:T(8,128)S(1)}, f32[64,512]{1,0:T(8,128)S(1)}, u32[]{:S(2)}, u32[]{:S(2)}) collective-permute-start(f32[64,512]{1,0:T(8,128)S(1)} %get-tuple-element.57), channel_id=1, source_target_pairs={{0,16},{1,5},{2,18},{3,7},{4,20},{5,1},{6,22},{7,3},{8,24},{9,13},... | collective-permute-start | bytes 393224 | tf_op jit(solution)/shard_map/ppermute | solution.py:212
  92.1 8.5 %collective-permute-start.21 = (f32[64,512]{1,0:T(8,128)S(1)}, f32[64,512]{1,0:T(8,128)S(1)}, u32[]{:S(2)}, u32[]{:S(2)}) collective-permute-start(f32[64,512]{1,0:T(8,128)S(1)} %get-tuple-element.58), channel_id=1, source_target_pairs={{0,24},{1,7},{2,26},{3,5},{4,28},{5,3},{6,30},{7,1},{8,16},{9,15},... | collective-permute-start | bytes 393224 | tf_op jit(solution)/shard_map/ppermute | solution.py:212
  100.7 1.3 %collective-permute-start.22 = (f32[64,256]{1,0:T(8,128)S(1)}, f32[64,256]{1,0:T(8,128)S(1)}, u32[]{:S(2)}, u32[]{:S(2)}) collective-permute-start(f32[64,256]{1,0:T(8,128)S(1)} %get-tuple-element.64), channel_id=1, source_target_pairs={{0,1},{1,0},{2,3},{3,2},{4,5},{5,4},{6,7},{7,6},{8,9},{9,8},{10,11... | collective-permute-start | bytes 196616 | tf_op jit(solution)/shard_map/ppermute | solution.py:331

commit v2 on v1

v2 whole, which is shorter than its diff:
```python
import functools
import math

import jax
import jax.numpy as jnp
from jax import lax
from jax.experimental import pallas as pl
from jax.experimental.pallas import tpu as pltpu
from jax.sharding import PartitionSpec as P

STEPS = 2
COORDS = 8
FEATURES = 32
ONES = 16
KEPT_BYTES = 20 << 20

neighbours = 64.0
ridge_term = 1.0
omegas = [1.0 / (0.55 + 0.45 * math.cos(math.pi * (2 * k + 1) / 4.0)) for k in range(2)]

BF16 = jnp.bfloat16
F32 = jnp.float32


def parts_of(value, count):
    terms = []
    for _ in range(count):
        term = value.astype(BF16)
        terms.append(term)
        value = value - term.astype(F32)
    return terms


def point_features(points, inverse, as_rows):
    scaled = (points - 0.5) * inverse
    axes = [scaled[d : d + 1] for d in range(3)]
    norm = parts_of(axes[0] * axes[0] + axes[1] * axes[1] + axes[2] * axes[2], 3)
    one = jnp.ones_like(norm[0])
    found = []
    for axis in axes:
        if as_rows:
            a, b, c = parts_of(-2.0 * axis, 3)
            found += [a, a, b, b, a, c]
        else:
            a, b, c = parts_of(axis, 3)
            found += [a, b, a, b, c, a]
    found += norm + [one] * 3 if as_rows else [one] * 3 + norm
    found += [jnp.zeros_like(one)] * (FEATURES - len(found))
    return jnp.concatenate([f.astype(F32) for f in found], axis=0).astype(BF16)


def quarter_wendland(square):
    square = jnp.minimum(jnp.maximum(square, 1e-12), 1.0)
    distance = square * lax.rsqrt(square)
    falloff = 1.0 - distance
    falloff = falloff * falloff
    return (falloff * falloff) * (distance + 0.25)


def evaluate(rows, row_start, cols, high, low, high_start, sub):
    count, width = rows.shape[1], cols.shape[1]
    for at in range(0, count, sub):
        square = lax.dot_general(
            rows[:, at : at + sub], cols, (((0,), (0,)), ((), ())), preferred_element_type=F32
        )
        value = quarter_wendland(square)
        rounded = value.astype(BF16)
        high[row_start + at : row_start + at + sub, high_start : high_start + width] = rounded
        low[row_start + at : row_start + at + sub, high_start : high_start + width] = (
            value - rounded.astype(F32)
        ).astype(BF16)


def product(stacked, half, high, low):
    coarse = jnp.dot(stacked, high, preferred_element_type=F32)
    fine = jnp.dot(stacked[:half], low, preferred_element_type=F32)
    return coarse, fine


def pull_kernel(inverse, full, spans, first, last, *refs):
    refs = list(refs)
    core = refs.pop(0)
    block = refs.pop(0)
    if first:
        sources = [refs.pop(0) for _ in spans]
        cols, after = refs.pop(0), refs.pop(0)
    else:
        cols, before = refs.pop(0), refs.pop(0)
        after = [refs.pop(0) for _ in range(len(spans) + 1)] if last else refs.pop(0)
    stacked, rows, high, low = refs
    half, width = full // 2, cols.shape[1] // (len(spans) * (2 if last else 1))
    a, b = parts_of(block[:full] * 4.0, 2)
    stacked[:full] = a
    stacked[full:] = b
    rows[...] = point_features(block[full : full + 3], inverse, True)
    if first:
        for k in spans:
            cols[:, k * width : (k + 1) * width] = point_features(sources[k][...], inverse, False)
    step = 2 if len(spans) % 2 == 0 else 1
    for k in range(0, len(spans), step):
        at = slice(spans[k] * width, (spans[k] + step) * width)
        evaluate(rows, 0, cols[:, at], high, low, 0, 128)
        coarse, fine = product(stacked[...], full, high[...], low[...])
        total = coarse[:full] + coarse[full:] + fine
        if not first:
            total = before[:, at] + total
        if not last:
            after[:, at] = total
            continue
        mine = jnp.where(core[0] == 0, total[:half], total[half:])
        for i in range(step):
            after[k + i][...] = mine[:, i * width : (i + 1) * width]
        after[-1][:, k * width : (k + step) * width] = jnp.where(core[0] == 0, total[half:], total[:half])


def keep_kernel(inverse, row_points, col_points, high, low, zero, rows, cols):
    zero[...] = jnp.zeros_like(zero)
    rows[...] = point_features(row_points[...], inverse, True)
    cols[...] = point_features(col_points[...], inverse, False)
    count, width = rows.shape[1], math.gcd(cols.shape[1], 1024)

    def tile(which, carry):
        at = pl.ds(pl.multiple_of(which * width, width), width)
        wide = cols[:, at]
        for row in range(0, count, 256):
            square = lax.dot_general(
                rows[:, row : row + 256], wide, (((0,), (0,)), ((), ())), preferred_element_type=F32
            )
            value = quarter_wendland(square)
            rounded = value.astype(BF16)
            high[row : row + 256, at] = rounded
            low[row : row + 256, at] = (value - rounded.astype(F32)).astype(BF16)
        return carry

    lax.fori_loop(0, cols.shape[1] // width, tile, 0)


def step_kernel(half, peers, spans, with_sums, *refs):
    blocks, high, low = refs[:peers], refs[peers], refs[peers + 1]
    outs, stacked = refs[peers + 2 : -1], refs[-1]
    count = blocks[0].shape[1]
    upper = half + (ONES if with_sums else 0)
    for k in range(peers):
        a, b = parts_of(blocks[k][...] * 4.0, 2)
        stacked[:half, k * count : (k + 1) * count] = a
        stacked[upper:, k * count : (k + 1) * count] = b
    if with_sums:
        stacked[half:upper, :] = jnp.full((ONES, stacked.shape[1]), 4.0, BF16)
    step = 2 if len(spans) % 2 == 0 else 1
    for k in range(0, len(spans), step):
        span = slice(spans[k] * count, (spans[k] + step) * count)
        coarse, fine = product(stacked[...], upper, high[:, span], low[:, span])
        total = coarse[:half] + coarse[upper:] + fine[:half]
        for i in range(step):
            at = slice(i * count, (i + 1) * count)
            outs[k + i][:half] = total[:, at]
            if with_sums:
                outs[k + i][half:] = coarse[half : half + 8, at] + fine[half : half + 8, at]


def again_kernel(inverse, half, peers, with_sums, *refs):
    blocks, row_points, col_points = refs[:peers], refs[peers], refs[peers + 1]
    outs = refs[peers + 2 : 2 * peers + 2]
    stacked, rows, cols, high, low = refs[2 * peers + 2 :]
    count = blocks[0].shape[1]
    upper = half + (ONES if with_sums else 0)
    rows[...] = point_features(row_points[...], inverse, True)
    cols[...] = point_features(col_points[...], inverse, False)
    if with_sums:
        stacked[half:upper, :] = jnp.full((ONES, count), 4.0, BF16)
    for k in range(peers):
        a, b = parts_of(blocks[k][...] * 4.0, 2)
        stacked[:half] = a
        stacked[upper:] = b
        for j in range(peers):
            mine = rows[:, k * count : (k + 1) * count]
            evaluate(mine, 0, cols[:, j * count : (j + 1) * count], high, low, 0, 128)
            coarse, fine = product(stacked[...], upper, high[...], low[...])
            total = coarse[:half] + coarse[upper:] + fine[:half]
            outs[j][:half] = total if k == 0 else outs[j][:half] + total
            if with_sums:
                sums = coarse[half : half + 8] + fine[half : half + 8]
                outs[j][half:] = sums if k == 0 else outs[j][half:] + sums


def vmem(count):
    return [pl.BlockSpec(memory_space=pltpu.VMEM)] * count


def params():
    return pltpu.CompilerParams(vmem_limit_bytes=24 << 20)


def cost(rows, cols, half, evaluated):
    return pl.CostEstimate(
        flops=rows * cols * (6 * half + (200 if evaluated else 0)), bytes_accessed=4 * rows * half, transcendentals=0
    )


def per_device(vol_grad, vol_coords, ctrl_coords):
    tgt, src = lax.axis_size("tgt"), lax.axis_size("src")
    chips = src // 2
    peers = tgt
    if chips != tgt or src % 2 or tgt & (tgt - 1):
        raise ValueError("unsupported mesh")
    half = vol_grad.shape[0] // 2
    volume, owned = vol_grad.shape[1], ctrl_coords.shape[1]
    overall = owned * tgt * src
    radius = (3.0 * neighbours / (4.0 * math.pi * overall)) ** (1.0 / 3.0)
    inverse = 1.0 / radius
    core = lax.axis_index("src") % 2
    first_core = core == 0

    sibling = [(i, i ^ 1) for i in range(src)]

    def moved(flips):
        return [
            ((t * chips + c) * 2 + r, ((t ^ flips[r][0]) * chips + (c ^ flips[r][1])) * 2 + r)
            for t in range(tgt)
            for c in range(chips)
            for r in range(2)
        ]

    along_src = [moved(((0, k), (0, k))) for k in range(peers)]
    along_tgt = [moved(((k, 0), (k, 0))) for k in range(peers)]
    gather_pairs = [moved(((0, k), (k, 0))) for k in range(peers)]
    sum_pairs = [moved(((k, 0), (0, k))) for k in range(peers)]

    def exchange(value, pairs):
        return lax.ppermute(value, ("tgt", "src"), pairs)

    def ordered(mine, other, axis):
        return jnp.where(
            first_core, jnp.concatenate([mine, other], axis=axis), jnp.concatenate([other, mine], axis=axis)
        )

    block = jnp.concatenate(
        [
            vol_grad,
            vol_coords,
            jnp.pad(ctrl_coords, ((0, 0), (0, volume - owned))),
            jnp.zeros((COORDS - 6, volume), F32),
        ],
        axis=0,
    )
    ctrl = ordered(ctrl_coords, lax.ppermute(ctrl_coords, "src", sibling), 1)
    blocks = [block] + [exchange(block, along_src[k]) for k in range(1, peers)]
    tgt_ctrl = [ctrl] + [exchange(ctrl, along_tgt[k]) for k in range(1, peers)]

    width, full = 2 * owned, 2 * half
    total_width = peers * width
    core_of = jnp.reshape(core, (1,)).astype(jnp.int32)
    scalar = [pl.BlockSpec(memory_space=pltpu.SMEM)]
    span_step = 2 if peers % 4 == 0 else 1
    pull_scratch = [
        pltpu.VMEM((2 * full, volume), BF16),
        pltpu.VMEM((FEATURES, volume), BF16),
        pltpu.VMEM((volume, span_step * width), BF16),
        pltpu.VMEM((volume, span_step * width), BF16),
    ]

    def pull(which, spans, cols, before, last):
        first = which == 0
        sums = pltpu.VMEM((full, total_width), F32)
        if last:
            shapes = [jax.ShapeDtypeStruct((half, width), F32)] * len(spans)
            shapes.append(jax.ShapeDtypeStruct((half, len(spans) * width), F32))
        else:
            shapes = [pltpu.VMEM((FEATURES, total_width), BF16), sums] if first else [sums]
        if first:
            inputs = [core_of, blocks[which], *tgt_ctrl]
        else:
            inputs = [core_of, blocks[which]]
            inputs += [pltpu.with_memory_space_constraint(value, pltpu.VMEM) for value in (cols, before)]
        return pl.pallas_call(
            functools.partial(pull_kernel, inverse, full, spans, first, last),
            out_shape=shapes,
            in_specs=scalar + vmem(len(inputs) - 1),
            out_specs=vmem(len(shapes)),
            scratch_shapes=pull_scratch,
            input_output_aliases={} if first or last else {3: 0},
            compiler_params=params(),
            cost_estimate=cost(volume, len(spans) * width, full, True),
        )(*inputs)

    near, far = list(range(peers // 2)), list(range(peers // 2, peers))
    cols, sofar = pull(0, near + far, None, None, False)
    for k in range(1, peers - 1):
        (sofar,) = pull(k, near + far, cols, sofar, False)
    sums = [None] * peers
    for spans in (far, near):
        *mine, other = pull(peers - 1, spans, cols, sofar, True)
        other = lax.ppermute(other, "src", sibling)
        for i, k in enumerate(spans):
            sums[k] = mine[i] + other[:, i * width : (i + 1) * width]

    def summed(values):
        total = values[0]
        for k in range(1, peers):
            total = total + exchange(values[k], sum_pairs[k])
        return total

    theirs = jnp.concatenate([b[full + 3 : full + 6, :owned] for b in blocks[1:]], axis=1)
    others = lax.ppermute(theirs, "src", sibling)
    src_points = [ctrl]
    for k in range(peers - 1):
        at = slice(k * owned, (k + 1) * owned)
        src_points.append(ordered(theirs[:, at], others[:, at], 1))
    src_points = jnp.concatenate(src_points, axis=1)
    tgt_points = jnp.concatenate(tgt_ctrl, axis=1)
    row_points = jnp.where(first_core, src_points, tgt_points)
    col_points = jnp.where(first_core, tgt_points, src_points)

    kept = (peers * width) ** 2 * 4 <= KEPT_BYTES
    pullback = sums[0]
    if kept:
        high, low, zero = pl.pallas_call(
            functools.partial(keep_kernel, inverse),
            out_shape=[pltpu.VMEM((peers * width, peers * width), BF16)] * 2 + [jax.ShapeDtypeStruct((8, 128), F32)],
            in_specs=vmem(2),
            out_specs=vmem(3),
            scratch_shapes=[pltpu.VMEM((FEATURES, peers * width), BF16)] * 2,
            compiler_params=params(),
            cost_estimate=cost(peers * width, peers * width, 0, True),
        )(row_points, col_points)
        pullback = pullback + zero[0, 0]
    for k in range(1, peers):
        pullback = pullback + exchange(sums[k], along_tgt[k])

    iterate = pullback
    for sweep in range(STEPS):
        arrived = [iterate] + [exchange(iterate, gather_pairs[k]) for k in range(1, peers)]
        with_sums = sweep == 0
        upper = half + (ONES if with_sums else 0)
        out_rows = half + (8 if with_sums else 0)
        products = [None] * peers
        if kept:
            for spans in (far, near):
                found = pl.pallas_call(
                    functools.partial(step_kernel, half, peers, spans, with_sums),
                    out_shape=[jax.ShapeDtypeStruct((out_rows, width), F32)] * len(spans),
                    in_specs=vmem(peers + 2),
                    out_specs=vmem(len(spans)),
                    scratch_shapes=[pltpu.VMEM((upper + half, peers * width), BF16)],
                    compiler_params=params(),
                    cost_estimate=cost(peers * width, len(spans) * width, half, False),
                )(
                    *arrived,
                    pltpu.with_memory_space_constraint(high, pltpu.VMEM),
                    pltpu.with_memory_space_constraint(low, pltpu.VMEM),
                )
                for k, value in zip(spans, found):
                    products[k] = value
        else:
            products = pl.pallas_call(
                functools.partial(again_kernel, inverse, half, peers, with_sums),
                out_shape=[jax.ShapeDtypeStruct((out_rows, width), F32)] * peers,
                in_specs=vmem(peers + 2),
                out_specs=vmem(peers),
                scratch_shapes=[
                    pltpu.VMEM((upper + half, width), BF16),
                    pltpu.VMEM((FEATURES, peers * width), BF16),
                    pltpu.VMEM((FEATURES, peers * width), BF16),
                    pltpu.VMEM((width, width), BF16),
                    pltpu.VMEM((width, width), BF16),
                ],
                compiler_params=params(),
                cost_estimate=cost(peers * width, peers * width, half, True),
            )(*arrived, row_points, col_points)
        total = summed(products)
        if with_sums:
            scaling = 1.0 / (total[half : half + 1] + ridge_term)
        iterate = iterate + omegas[sweep] * scaling * (pullback - total[:half] - iterate)

    own = jnp.where(first_core, iterate[:, :owned], iterate[:, owned:])
    theirs = jnp.where(first_core, iterate[:, owned:], iterate[:, :owned])
    back = lax.ppermute(theirs, "src", sibling)
    return jnp.where(
        first_core, jnp.concatenate([own, back], axis=0), jnp.concatenate([back, own], axis=0)
    )


def solution(mesh):
    placed = (P(None, ("tgt", "src")), P(None, ("tgt", "src")), P(None, ("tgt", "src")))
    return jax.shard_map(
        per_device, mesh=mesh, in_specs=placed, out_specs=P(None, ("tgt", "src")), check_vma=False
    )
```

time: 103 us -> 86 us (0.83)
  Pallas kernels: 32.7 us -> 24.7 us
  waiting for transfers between devices: 33.4 us -> 27.7 us
  starting transfers between devices: 32.1 us -> 29 us
    pallas_call x7 -> x10, Pallas kernels: 32.7 us -> 24.7 us  [the longest x5 10.6 us: pull(): pl.pallas_call(functools.partial(pull_kernel, inverse, full, spans, first...]
    ppermute x21, waiting for transfers between devices: 31.2 us -> 25 us  [exchange(): return lax.ppermute(value, ('tgt', 'src'), pairs)]
    ppermute x21, starting transfers between devices: 31.6 us -> 28.2 us  [exchange(): return lax.ppermute(value, ('tgt', 'src'), pairs)]
    concatenate x3 -> x2, other arithmetic: 2.27 us -> 1.07 us  [the longest x1 1.06 us: per_device(): jnp.concatenate([vol_grad, vol_coords, jnp.pad(ctrl_coords, ((0, 0), (0,...]
  transfers between devices with their start and end apart: 23 -> 26, of which waited for: 12 -> 17; matrix products, arithmetic and copies ran while one was open for 0% -> 2% of each run, Pallas kernels for 22% -> 25%
where the time goes in v2:
time: 86 us; the launch traced here: 85.7 us
  starting transfers between devices  29 us (34%)
  waiting for transfers between devices  27.7 us (32%)
  Pallas kernels  24.7 us (29%)
  other arithmetic  3.45 us (4%)
    ppermute x21, starting transfers between devices, exchange(): return lax.ppermute(value, ('tgt', 'src'), pairs)  28.2 us
    ppermute x21, waiting for transfers between devices, exchange(): return lax.ppermute(value, ('tgt', 'src'), pairs)  25 us
    pallas_call x5, Pallas kernels, pull(): pl.pallas_call(functools.partial(pull_kernel, inverse, full, spans, first...  10.6 us
    pallas_call x1, Pallas kernels, per_device(): pl.pallas_call(functools.partial(keep_kernel, inverse), out_shape=[pltpu....  8.33 us
    pallas_call x4, Pallas kernels, per_device(): pl.pallas_call(functools.partial(step_kernel, half, peers, spans, with_su...  5.75 us
  transfers between devices with their start and end apart: 26, of which 17 were waited for; matrix products, arithmetic and copies ran while one was open for 2% of the time, Pallas kernels for 25%

profile of v2, /device:TPU:0, one launch (start us, length us, event | category | flops | bytes accessed | tf_op | source)
XLA Modules:
  0.0 85.7 jit_solution(5698505699307678653)
XLA Ops:
  0.0 0.1 pad.39.clone
  0.1 1.1 %fusion.refs_1_ = f32[136,512]{1,0:T(8,128)S(1)} fusion(f32[3,256]{1,0:T(4,128)} %param.5, f32[3,512]{1,0:T(4,128)} %param.4, f32[128,512]{1,0:T(8,128)} %param.3, f32[136]{0:T(256)S(1)} %pad.39.clone), kind=kLoop, calls=%fused_computation.3 | loop fusion | flops 487424 | bytes 550432 | tf_op jit(solution)/shard_map/concatenate | solution.py:237
  1.2 3.0 %collective-permute-start.6 = (f32[136,512]{1,0:T(8,128)S(1)}, f32[136,512]{1,0:T(8,128)S(1)}, u32[]{:S(2)}, u32[]{:S(2)}) collective-permute-start(f32[136,512]{1,0:T(8,128)S(1)} %fusion.refs_1_), channel_id=1, source_target_pairs={{0,2},{1,3},{2,0},{3,1},{4,6},{5,7},{6,4},{7,5},{8,10},{9,11},{10,... | collective-permute-start | bytes 835592 | tf_op jit(solution)/shard_map/ppermute | solution.py:230
  4.2 1.5 %collective-permute-start.5 = (f32[136,512]{1,0:T(8,128)S(1)}, f32[136,512]{1,0:T(8,128)S(1)}, u32[]{:S(2)}, u32[]{:S(2)}) collective-permute-start(f32[136,512]{1,0:T(8,128)S(1)} %fusion.refs_1_), channel_id=1, source_target_pairs={{0,4},{1,5},{2,6},{3,7},{4,0},{5,1},{6,2},{7,3},{8,12},{9,13},{10,... | collective-permute-start | bytes 835592 | tf_op jit(solution)/shard_map/ppermute | solution.py:230
  5.7 0.0 collective-permute-start
  5.7 0.0 collective-permute-start.1
  5.7 1.4 %collective-permute-done.1 = f32[3,256]{1,0:T(4,128)S(1)} collective-permute-done((f32[3,256]{1,0:T(4,128)}, f32[3,256]{1,0:T(4,128)S(1)}, u32[]{:S(2)}, u32[]{:S(2)}) %collective-permute-start.1) | collective-permute-done | bytes 3104 | tf_op jit(solution)/shard_map/ppermute | solution.py:246
  7.1 0.8 maximum_select_fusion.1.refs_2_
  7.8 4.1 %collective-permute-start.4 = (f32[3,512]{1,0:T(4,128)S(1)}, f32[3,512]{1,0:T(4,128)S(1)}, u32[]{:S(2)}, u32[]{:S(2)}) collective-permute-start(f32[3,512]{1,0:T(4,128)S(1)} %maximum_select_fusion.1.refs_2_), channel_id=1, source_target_pairs={{0,24},{1,25},{2,26},{3,27},{4,28},{5,29},{6,30},{7,31},{8,16},{9,... | collective-permute-start | bytes 18440 | tf_op jit(solution)/shard_map/ppermute | solution.py:230
  11.9 1.6 %collective-permute-done.4.refs_5_ = f32[3,512]{1,0:T(4,128)S(1)} collective-permute-done((f32[3,512]{1,0:T(4,128)S(1)}, f32[3,512]{1,0:T(4,128)S(1)}, u32[]{:S(2)}, u32[]{:S(2)}) %collective-permute-start.4) | collective-permute-done | bytes 6176 | tf_op jit(solution)/shard_map/ppermute | solution.py:230
  13.5 0.0 collective-permute-start.2
  13.5 2.9 %collective-permute-done.3.refs_4_ = f32[3,512]{1,0:T(4,128)S(1)} collective-permute-done((f32[3,512]{1,0:T(4,128)S(1)}, f32[3,512]{1,0:T(4,128)S(1)}, u32[]{:S(2)}, u32[]{:S(2)}) %collective-permute-start.3) | collective-permute-done | bytes 6176 | tf_op jit(solution)/shard_map/ppermute | solution.py:230
  16.5 0.7 collective-permute-done.2.refs_3_
  17.2 2.6 %shard_map.37 = (bf16[32,2048]{1,0:T(8,128)(2,1)S(1)}, f32[128,2048]{1,0:T(8,128)S(1)}) custom-call(s32[1]{0:T(128)} %bitcast.refs_0_, f32[136,512]{1,0:T(8,128)S(1)} %fusion.refs_1_, f32[3,512]{1,0:T(4,128)S(1)} %maximum_select_fusion.1.refs_2_, f32[3,512]{1,0:T(4,128)S(1)} %collective-permute-done.2.refs_3_, f32[3,512]{1,0:T(4,128)S(1)} %collective-permute-done.3.refs_4_, ...), custom_call_target="tpu_custom_call" | custom-call | flops 1015021568 | bytes 262144 | tf_op jit(solution)/shard_map/pallas_call | solution.py:275
  19.8 0.0 collective-permute-done.6.refs_1_
  19.8 0.0 collective-permute-done.5.refs_1_
  19.9 0.1 collective-permute-start.8
  20.0 2.6 %shard_map.38.refs_3_ = f32[128,2048]{1,0:T(8,128)S(1)} custom-call(s32[1]{0:T(128)} %bitcast.refs_0_, f32[136,512]{1,0:T(8,128)S(1)} %collective-permute-done.6.refs_1_, bf16[32,2048]{1,0:T(8,128)(2,1)S(1)} %get-tuple-element.24.refs_2_, f32[128,2048]{1,0:T(8,128)S(1)} %get-tuple-element.25.refs_3_), custom_call_target="tpu_custom_call", output_to_operand_aliasing={{}: (3, {})} | custom-call | flops 1015021568 | bytes 262144 | tf_op jit(solution)/shard_map/pallas_call | solution.py:275
  22.6 2.6 %shard_map.39.refs_3_ = f32[128,2048]{1,0:T(8,128)S(1)} custom-call(s32[1]{0:T(128)} %bitcast.refs_0_, f32[136,512]{1,0:T(8,128)S(1)} %collective-permute-done.5.refs_1_, bf16[32,2048]{1,0:T(8,128)(2,1)S(1)} %get-tuple-element.24.refs_2_, f32[128,2048]{1,0:T(8,128)S(1)} %shard_map.38.refs_3_), custom_call_target="tpu_custom_call", output_to_operand_aliasing={{}: (3, {})} | custom-call | flops 1015021568 | bytes 262144 | tf_op jit(solution)/shard_map/pallas_call | solution.py:275
  25.2 1.4 %shard_map.42 = (f32[64,512]{1,0:T(8,128)S(1)}, f32[64,512]{1,0:T(8,128)S(1)}, f32[64,1024]{1,0:T(8,128)S(1)}) custom-call(s32[1]{0:T(128)} %bitcast.refs_0_, f32[136,512]{1,0:T(8,128)S(1)} %collective-permute-done.refs_1_, bf16[32,2048]{1,0:T(8,128)(2,1)S(1)} %get-tuple-element.24.refs_2_, f32[128,2048]{1,0:T(8,128)S(1)} %shard_map.39.refs_3_), custom_call_target="tpu_custom_call" | custom-call | flops 507510784 | bytes 262144 | tf_op jit(solution)/shard_map/pallas_call | solution.py:275
  26.6 0.6 collective-permute-start.10
  27.2 1.4 %shard_map.40 = (f32[64,512]{1,0:T(8,128)S(1)}, f32[64,512]{1,0:T(8,128)S(1)}, f32[64,1024]{1,0:T(8,128)S(1)}) custom-call(s32[1]{0:T(128)} %bitcast.refs_0_, f32[136,512]{1,0:T(8,128)S(1)} %collective-permute-done.refs_1_, bf16[32,2048]{1,0:T(8,128)(2,1)S(1)} %get-tuple-element.24.refs_2_, f32[128,2048]{1,0:T(8,128)S(1)} %shard_map.39.refs_3_), custom_call_target="tpu_custom_call" | custom-call | flops 507510784 | bytes 262144 | tf_op jit(solution)/shard_map/pallas_call | solution.py:275
  28.6 0.1 collective-permute-start.7
  28.7 0.0 collective-permute-done.8
  28.8 2.4 %collective-permute-start.11 = (f32[64,512]{1,0:T(8,128)S(1)}, f32[64,512]{1,0:T(8,128)S(1)}, u32[]{:S(2)}, u32[]{:S(2)}) collective-permute-start(f32[64,512]{1,0:T(8,128)S(1)} %get-tuple-element.45), channel_id=1, source_target_pairs={{0,16},{1,17},{2,18},{3,19},{4,20},{5,21},{6,22},{7,23},{8,24},{9,... | collective-permute-start | bytes 393224 | tf_op jit(solution)/shard_map/ppermute | solution.py:230
  31.2 1.5 %collective-permute-start.12 = (f32[64,512]{1,0:T(8,128)S(1)}, f32[64,512]{1,0:T(8,128)S(1)}, u32[]{:S(2)}, u32[]{:S(2)}) collective-permute-start(f32[64,512]{1,0:T(8,128)S(1)} %get-tuple-element.46), channel_id=1, source_target_pairs={{0,24},{1,25},{2,26},{3,27},{4,28},{5,29},{6,30},{7,31},{8,16},{9,... | collective-permute-start | bytes 393224 | tf_op jit(solution)/shard_map/ppermute | solution.py:230
  32.7 0.0 collective-permute-done.7
  32.8 0.6 collective-permute-start.9
  33.3 8.3 %shard_map.41 = (bf16[2048,2048]{1,0:T(8,128)(2,1)S(1)}, bf16[2048,2048]{1,0:T(8,128)(2,1)S(1)}, f32[8,128]{1,0:T(8,128)S(1)}) custom-call(f32[3,2048]{1,0:T(4,128)S(1)} %get-tuple-element.50.row_points, f32[3,2048]{1,0:T(4,128)S(1)} %get-tuple-element.49.col_points), custom_call_target="tpu_custom_call" | custom-call | flops 838860800 | tf_op jit(solution)/shard_map/pallas_call | solution.py:317
  41.7 0.5 slice.54
  42.2 0.6 collective-permute-done.9
  42.8 0.7 fusion.7.refs_0_
  43.5 2.7 %collective-permute-start.15 = (f32[64,512]{1,0:T(8,128)S(1)}, f32[64,512]{1,0:T(8,128)S(1)}, u32[]{:S(2)}, u32[]{:S(2)}) collective-permute-start(f32[64,512]{1,0:T(8,128)S(1)} %fusion.7.refs_0_), channel_id=1, source_target_pairs={{0,6},{1,25},{2,4},{3,27},{4,2},{5,29},{6,0},{7,31},{8,14},{9,17},... | collective-permute-start | bytes 393224 | tf_op jit(solution)/shard_map/ppermute | solution.py:230
  46.2 0.5 collective-permute-start.14
  46.7 0.3 collective-permute-start.13
  47.0 2.4 %collective-permute-done.15.refs_3_ = f32[64,512]{1,0:T(8,128)S(1)} collective-permute-done((f32[64,512]{1,0:T(8,128)S(1)}, f32[64,512]{1,0:T(8,128)S(1)}, u32[]{:S(2)}, u32[]{:S(2)}) %collective-permute-start.15) | collective-permute-done | bytes 131104 | tf_op jit(solution)/shard_map/ppermute | solution.py:230
  49.4 1.8 %collective-permute-done.14.refs_2_ = f32[64,512]{1,0:T(8,128)S(1)} collective-permute-done((f32[64,512]{1,0:T(8,128)S(1)}, f32[64,512]{1,0:T(8,128)S(1)}, u32[]{:S(2)}, u32[]{:S(2)}) %collective-permute-start.14) | collective-permute-done | bytes 131104 | tf_op jit(solution)/shard_map/ppermute | solution.py:230
  51.2 0.5 collective-permute-done.13.refs_1_
  51.7 1.5 %shard_map.44 = (f32[72,512]{1,0:T(8,128)S(1)}, f32[72,512]{1,0:T(8,128)S(1)}) custom-call(f32[64,512]{1,0:T(8,128)S(1)} %fusion.7.refs_0_, f32[64,512]{1,0:T(8,128)S(1)} %collective-permute-done.13.refs_1_, f32[64,512]{1,0:T(8,128)S(1)} %collective-permute-done.14.refs_2_, f32[64,512]{1,0:T(8,128)S(1)} %collective-permute-done.15.refs_3_, ...), custom_call_target="tpu_custom_call" | custom-call | flops 805306368 | bytes 524288 | tf_op jit(solution)/shard_map/pallas_call | solution.py:339
  53.2 3.5 %collective-permute-start.17 = (f32[72,512]{1,0:T(8,128)S(1)}, f32[72,512]{1,0:T(8,128)S(1)}, u32[]{:S(2)}, u32[]{:S(2)}) collective-permute-start(f32[72,512]{1,0:T(8,128)S(1)} %get-tuple-element.37), channel_id=1, source_target_pairs={{0,16},{1,5},{2,18},{3,7},{4,20},{5,1},{6,22},{7,3},{8,24},{9,13},... | collective-permute-start | bytes 442376 | tf_op jit(solution)/shard_map/ppermute | solution.py:230
  56.7 0.8 collective-permute-start.18
  57.5 1.5 %shard_map.43 = (f32[72,512]{1,0:T(8,128)S(1)}, f32[72,512]{1,0:T(8,128)S(1)}) custom-call(f32[64,512]{1,0:T(8,128)S(1)} %fusion.7.refs_0_, f32[64,512]{1,0:T(8,128)S(1)} %collective-permute-done.13.refs_1_, f32[64,512]{1,0:T(8,128)S(1)} %collective-permute-done.14.refs_2_, f32[64,512]{1,0:T(8,128)S(1)} %collective-permute-done.15.refs_3_, ...), custom_call_target="tpu_custom_call" | custom-call | flops 805306368 | bytes 524288 | tf_op jit(solution)/shard_map/pallas_call | solution.py:339
  58.9 0.1 collective-permute-start.16
  59.0 2.4 %collective-permute-done.17 = f32[72,512]{1,0:T(8,128)S(1)} collective-permute-done((f32[72,512]{1,0:T(8,128)S(1)}, f32[72,512]{1,0:T(8,128)S(1)}, u32[]{:S(2)}, u32[]{:S(2)}) %collective-permute-start.17) | collective-permute-done | bytes 147488 | tf_op jit(solution)/shard_map/ppermute | solution.py:230
  61.4 2.4 %collective-permute-done.18 = f32[72,512]{1,0:T(8,128)S(1)} collective-permute-done((f32[72,512]{1,0:T(8,128)S(1)}, f32[72,512]{1,0:T(8,128)S(1)}, u32[]{:S(2)}, u32[]{:S(2)}) %collective-permute-start.18) | collective-permute-done | bytes 147488 | tf_op jit(solution)/shard_map/ppermute | solution.py:230
  63.8 1.5 %collective-permute-done.16 = f32[72,512]{1,0:T(8,128)S(1)} collective-permute-done((f32[72,512]{1,0:T(8,128)S(1)}, f32[72,512]{1,0:T(8,128)S(1)}, u32[]{:S(2)}, u32[]{:S(2)}) %collective-permute-start.16) | collective-permute-done | bytes 147488 | tf_op jit(solution)/shard_map/ppermute | solution.py:230
  65.4 1.5 %collective-permute-start.21 = (f32[64,512]{1,0:T(8,128)S(1)}, f32[64,512]{1,0:T(8,128)S(1)}, u32[]{:S(2)}, u32[]{:S(2)}) collective-permute-start(f32[64,512]{1,0:T(8,128)S(1)} %fusion.3.refs_0_), channel_id=1, source_target_pairs={{0,6},{1,25},{2,4},{3,27},{4,2},{5,29},{6,0},{7,31},{8,14},{9,17},... | collective-permute-start | bytes 393224 | tf_op jit(solution)/shard_map/ppermute | solution.py:230
  67.0 0.9 %collective-permute-start.20 = (f32[64,512]{1,0:T(8,128)S(1)}, f32[64,512]{1,0:T(8,128)S(1)}, u32[]{:S(2)}, u32[]{:S(2)}) collective-permute-start(f32[64,512]{1,0:T(8,128)S(1)} %fusion.3.refs_0_), channel_id=1, source_target_pairs={{0,4},{1,17},{2,6},{3,19},{4,0},{5,21},{6,2},{7,23},{8,12},{9,25},... | collective-permute-start | bytes 393224 | tf_op jit(solution)/shard_map/ppermute | solution.py:230
  67.9 1.1 %collective-permute-start.19 = (f32[64,512]{1,0:T(8,128)S(1)}, f32[64,512]{1,0:T(8,128)S(1)}, u32[]{:S(2)}, u32[]{:S(2)}) collective-permute-start(f32[64,512]{1,0:T(8,128)S(1)} %fusion.3.refs_0_), channel_id=1, source_target_pairs={{0,2},{1,9},{2,0},{3,11},{4,6},{5,13},{6,4},{7,15},{8,10},{9,1},{1... | collective-permute-start | bytes 393224 | tf_op jit(solution)/shard_map/ppermute | solution.py:230
  69.0 2.5 %collective-permute-done.21.refs_3_ = f32[64,512]{1,0:T(8,128)S(1)} collective-permute-done((f32[64,512]{1,0:T(8,128)S(1)}, f32[64,512]{1,0:T(8,128)S(1)}, u32[]{:S(2)}, u32[]{:S(2)}) %collective-permute-start.21) | collective-permute-done | bytes 131104 | tf_op jit(solution)/shard_map/ppermute | solution.py:230
  71.4 1.3 %collective-permute-done.20.refs_2_ = f32[64,512]{1,0:T(8,128)S(1)} collective-permute-done((f32[64,512]{1,0:T(8,128)S(1)}, f32[64,512]{1,0:T(8,128)S(1)}, u32[]{:S(2)}, u32[]{:S(2)}) %collective-permute-start.20) | collective-permute-done | bytes 131104 | tf_op jit(solution)/shard_map/ppermute | solution.py:230
  72.8 0.1 collective-permute-done.19.refs_1_
  72.9 1.4 %shard_map.46 = (f32[64,512]{1,0:T(8,128)S(1)}, f32[64,512]{1,0:T(8,128)S(1)}) custom-call(f32[64,512]{1,0:T(8,128)S(1)} %fusion.3.refs_0_, f32[64,512]{1,0:T(8,128)S(1)} %collective-permute-done.19.refs_1_, f32[64,512]{1,0:T(8,128)S(1)} %collective-permute-done.20.refs_2_, f32[64,512]{1,0:T(8,128)S(1)} %collective-permute-done.21.refs_3_, ...), custom_call_target="tpu_custom_call" | custom-call | flops 805306368 | bytes 524288 | tf_op jit(solution)/shard_map/pallas_call | solution.py:339
  74.3 1.0 %collective-permute-start.23 = (f32[64,512]{1,0:T(8,128)S(1)}, f32[64,512]{1,0:T(8,128)S(1)}, u32[]{:S(2)}, u32[]{:S(2)}) collective-permute-start(f32[64,512]{1,0:T(8,128)S(1)} %get-tuple-element.41), channel_id=1, source_target_pairs={{0,16},{1,5},{2,18},{3,7},{4,20},{5,1},{6,22},{7,3},{8,24},{9,13},... | collective-permute-start | bytes 393224 | tf_op jit(solution)/shard_map/ppermute | solution.py:230
  75.2 1.3 %collective-permute-start.24 = (f32[64,512]{1,0:T(8,128)S(1)}, f32[64,512]{1,0:T(8,128)S(1)}, u32[]{:S(2)}, u32[]{:S(2)}) collective-permute-start(f32[64,512]{1,0:T(8,128)S(1)} %get-tuple-element.42), channel_id=1, source_target_pairs={{0,24},{1,7},{2,26},{3,5},{4,28},{5,3},{6,30},{7,1},{8,16},{9,15},... | collective-permute-start | bytes 393224 | tf_op jit(solution)/shard_map/ppermute | solution.py:230
  76.5 1.4 %shard_map.45 = (f32[64,512]{1,0:T(8,128)S(1)}, f32[64,512]{1,0:T(8,128)S(1)}) custom-call(f32[64,512]{1,0:T(8,128)S(1)} %fusion.3.refs_0_, f32[64,512]{1,0:T(8,128)S(1)} %collective-permute-done.19.refs_1_, f32[64,512]{1,0:T(8,128)S(1)} %collective-permute-done.20.refs_2_, f32[64,512]{1,0:T(8,128)S(1)} %collective-permute-done.21.refs_3_, ...), custom_call_target="tpu_custom_call" | custom-call | flops 805306368 | bytes 524288 | tf_op jit(solution)/shard_map/pallas_call | solution.py:339
  77.9 1.4 %collective-permute-start.22 = (f32[64,512]{1,0:T(8,128)S(1)}, f32[64,512]{1,0:T(8,128)S(1)}, u32[]{:S(2)}, u32[]{:S(2)}) collective-permute-start(f32[64,512]{1,0:T(8,128)S(1)} %get-tuple-element.40), channel_id=1, source_target_pairs={{0,8},{1,3},{2,10},{3,1},{4,12},{5,7},{6,14},{7,5},{8,0},{9,11},{1... | collective-permute-start | bytes 393224 | tf_op jit(solution)/shard_map/ppermute | solution.py:230
  79.3 3.0 %collective-permute-done.23 = f32[64,512]{1,0:T(8,128)S(1)} collective-permute-done((f32[64,512]{1,0:T(8,128)S(1)}, f32[64,512]{1,0:T(8,128)S(1)}, u32[]{:S(2)}, u32[]{:S(2)}) %collective-permute-start.23) | collective-permute-done | bytes 131104 | tf_op jit(solution)/shard_map/ppermute | solution.py:230
  82.3 0.0 collective-permute-done.24
  82.3 1.3 %collective-permute-done.22 = f32[64,512]{1,0:T(8,128)S(1)} collective-permute-done((f32[64,512]{1,0:T(8,128)S(1)}, f32[64,512]{1,0:T(8,128)S(1)}, u32[]{:S(2)}, u32[]{:S(2)}) %collective-permute-start.22) | collective-permute-done | bytes 131104 | tf_op jit(solution)/shard_map/ppermute | solution.py:230
  83.7 0.1 multiply_add_fusion
  83.7 0.1 collective-permute-start.25
  83.8 1.2 %collective-permute-done.25 = f32[64,256]{1,0:T(8,128)S(1)} collective-permute-done((f32[64,256]{1,0:T(8,128)S(1)}, f32[64,256]{1,0:T(8,128)S(1)}, u32[]{:S(2)}, u32[]{:S(2)}) %collective-permute-start.25) | collective-permute-done | bytes 65568 | tf_op jit(solution)/shard_map/ppermute | solution.py:377
  85.1 0.7 maximum_select_fusion
  (22 shorter events, 0.2 us)
Async XLA Ops:
  1.2 18.6 %collective-permute-start.6 = (f32[136,512]{1,0:T(8,128)S(1)}, f32[136,512]{1,0:T(8,128)S(1)}, u32[]{:S(2)}, u32[]{:S(2)}) collective-permute-start(f32[136,512]{1,0:T(8,128)S(1)} %fusion.refs_1_), channel_id=1, source_target_pairs={{0,2},{1,3},{2,0},{3,1},{4,6},{5,7},{6,4},{7,5},{8,10},{9,11},{10,... | collective-permute-start | bytes 835592 | tf_op jit(solution)/shard_map/ppermute | solution.py:230
  4.2 15.7 %collective-permute-start.5 = (f32[136,512]{1,0:T(8,128)S(1)}, f32[136,512]{1,0:T(8,128)S(1)}, u32[]{:S(2)}, u32[]{:S(2)}) collective-permute-start(f32[136,512]{1,0:T(8,128)S(1)} %fusion.refs_1_), channel_id=1, source_target_pairs={{0,4},{1,5},{2,6},{3,7},{4,0},{5,1},{6,2},{7,3},{8,12},{9,13},{10,... | collective-permute-start | bytes 835592 | tf_op jit(solution)/shard_map/ppermute | solution.py:230
  5.7 14.2 %collective-permute-start = (f32[136,512]{1,0:T(8,128)S(1)}, f32[136,512]{1,0:T(8,128)S(1)}, u32[]{:S(2)}, u32[]{:S(2)}) collective-permute-start(f32[136,512]{1,0:T(8,128)S(1)} %fusion.refs_1_), channel_id=1, source_target_pairs={{0,6},{1,7},{2,4},{3,5},{4,2},{5,3},{6,0},{7,1},{8,14},{9,15},{10,... | collective-permute-start | bytes 835592 | tf_op jit(solution)/shard_map/ppermute | solution.py:230
  5.7 1.4 %collective-permute-start.1 = (f32[3,256]{1,0:T(4,128)}, f32[3,256]{1,0:T(4,128)S(1)}, u32[]{:S(2)}, u32[]{:S(2)}) collective-permute-start(f32[3,256]{1,0:T(4,128)} %param.5), channel_id=1, source_target_pairs={{0,1},{1,0},{2,3},{3,2},{4,5},{5,4},{6,7},{7,6},{8,9},{9,8},{10,11... | collective-permute-start | bytes 9224 | tf_op jit(solution)/shard_map/ppermute | solution.py:246
  7.8 5.7 %collective-permute-start.4 = (f32[3,512]{1,0:T(4,128)S(1)}, f32[3,512]{1,0:T(4,128)S(1)}, u32[]{:S(2)}, u32[]{:S(2)}) collective-permute-start(f32[3,512]{1,0:T(4,128)S(1)} %maximum_select_fusion.1.refs_2_), channel_id=1, source_target_pairs={{0,24},{1,25},{2,26},{3,27},{4,28},{5,29},{6,30},{7,31},{8,16},{9,... | collective-permute-start | bytes 18440 | tf_op jit(solution)/shard_map/ppermute | solution.py:230
  11.9 4.5 %collective-permute-start.3 = (f32[3,512]{1,0:T(4,128)S(1)}, f32[3,512]{1,0:T(4,128)S(1)}, u32[]{:S(2)}, u32[]{:S(2)}) collective-permute-start(f32[3,512]{1,0:T(4,128)S(1)} %maximum_select_fusion.1.refs_2_), channel_id=1, source_target_pairs={{0,16},{1,17},{2,18},{3,19},{4,20},{5,21},{6,22},{7,23},{8,24},{9,... | collective-permute-start | bytes 18440 | tf_op jit(solution)/shard_map/ppermute | solution.py:230
  13.5 3.7 %collective-permute-start.2 = (f32[3,512]{1,0:T(4,128)S(1)}, f32[3,512]{1,0:T(4,128)S(1)}, u32[]{:S(2)}, u32[]{:S(2)}) collective-permute-start(f32[3,512]{1,0:T(4,128)S(1)} %maximum_select_fusion.1.refs_2_), channel_id=1, source_target_pairs={{0,8},{1,9},{2,10},{3,11},{4,12},{5,13},{6,14},{7,15},{8,0},{9,1},... | collective-permute-start | bytes 18440 | tf_op jit(solution)/shard_map/ppermute | solution.py:230
  19.9 8.8 %collective-permute-start.8 = (f32[3,768]{1,0:T(4,128)S(1)}, f32[3,768]{1,0:T(4,128)S(1)}, u32[]{:S(2)}, u32[]{:S(2)}) collective-permute-start(f32[3,768]{1,0:T(4,128)S(1)} %pad_maximum_fusion.2), channel_id=1, source_target_pairs={{0,1},{1,0},{2,3},{3,2},{4,5},{5,4},{6,7},{7,6},{8,9},{9,8},{10,11... | collective-permute-start | bytes 27656 | tf_op jit(solution)/shard_map/ppermute | solution.py:304
  26.6 2.1 %collective-permute-start.10 = (f32[64,1024]{1,0:T(8,128)S(1)}, f32[64,1024]{1,0:T(8,128)S(1)}, u32[]{:S(2)}, u32[]{:S(2)}) collective-permute-start(f32[64,1024]{1,0:T(8,128)S(1)} %get-tuple-element.31), channel_id=1, source_target_pairs={{0,1},{1,0},{2,3},{3,2},{4,5},{5,4},{6,7},{7,6},{8,9},{9,8},{10,11... | collective-permute-start | bytes 786440 | tf_op jit(solution)/shard_map/ppermute | solution.py:293
  28.6 4.2 %collective-permute-start.7 = (f32[64,1024]{1,0:T(8,128)S(1)}, f32[64,1024]{1,0:T(8,128)S(1)}, u32[]{:S(2)}, u32[]{:S(2)}) collective-permute-start(f32[64,1024]{1,0:T(8,128)S(1)} %get-tuple-element.27), channel_id=1, source_target_pairs={{0,1},{1,0},{2,3},{3,2},{4,5},{5,4},{6,7},{7,6},{8,9},{9,8},{10,11... | collective-permute-start | bytes 786440 | tf_op jit(solution)/shard_map/ppermute | solution.py:293
  28.8 13.4 %collective-permute-start.11 = (f32[64,512]{1,0:T(8,128)S(1)}, f32[64,512]{1,0:T(8,128)S(1)}, u32[]{:S(2)}, u32[]{:S(2)}) collective-permute-start(f32[64,512]{1,0:T(8,128)S(1)} %get-tuple-element.45), channel_id=1, source_target_pairs={{0,16},{1,17},{2,18},{3,19},{4,20},{5,21},{6,22},{7,23},{8,24},{9,... | collective-permute-start | bytes 393224 | tf_op jit(solution)/shard_map/ppermute | solution.py:230
  31.2 11.0 %collective-permute-start.12 = (f32[64,512]{1,0:T(8,128)S(1)}, f32[64,512]{1,0:T(8,128)S(1)}, u32[]{:S(2)}, u32[]{:S(2)}) collective-permute-start(f32[64,512]{1,0:T(8,128)S(1)} %get-tuple-element.46), channel_id=1, source_target_pairs={{0,24},{1,25},{2,26},{3,27},{4,28},{5,29},{6,30},{7,31},{8,16},{9,... | collective-permute-start | bytes 393224 | tf_op jit(solution)/shard_map/ppermute | solution.py:230
  32.8 10.0 %collective-permute-start.9 = (f32[64,512]{1,0:T(8,128)S(1)}, f32[64,512]{1,0:T(8,128)S(1)}, u32[]{:S(2)}, u32[]{:S(2)}) collective-permute-start(f32[64,512]{1,0:T(8,128)S(1)} %slice_add_fusion.2), channel_id=1, source_target_pairs={{0,8},{1,9},{2,10},{3,11},{4,12},{5,13},{6,14},{7,15},{8,0},{9,1},... | collective-permute-start | bytes 393224 | tf_op jit(solution)/shard_map/ppermute | solution.py:230
  43.5 5.9 %collective-permute-start.15 = (f32[64,512]{1,0:T(8,128)S(1)}, f32[64,512]{1,0:T(8,128)S(1)}, u32[]{:S(2)}, u32[]{:S(2)}) collective-permute-start(f32[64,512]{1,0:T(8,128)S(1)} %fusion.7.refs_0_), channel_id=1, source_target_pairs={{0,6},{1,25},{2,4},{3,27},{4,2},{5,29},{6,0},{7,31},{8,14},{9,17},... | collective-permute-start | bytes 393224 | tf_op jit(solution)/shard_map/ppermute | solution.py:230
  46.2 5.0 %collective-permute-start.14 = (f32[64,512]{1,0:T(8,128)S(1)}, f32[64,512]{1,0:T(8,128)S(1)}, u32[]{:S(2)}, u32[]{:S(2)}) collective-permute-start(f32[64,512]{1,0:T(8,128)S(1)} %fusion.7.refs_0_), channel_id=1, source_target_pairs={{0,4},{1,17},{2,6},{3,19},{4,0},{5,21},{6,2},{7,23},{8,12},{9,25},... | collective-permute-start | bytes 393224 | tf_op jit(solution)/shard_map/ppermute | solution.py:230
  46.7 5.0 %collective-permute-start.13 = (f32[64,512]{1,0:T(8,128)S(1)}, f32[64,512]{1,0:T(8,128)S(1)}, u32[]{:S(2)}, u32[]{:S(2)}) collective-permute-start(f32[64,512]{1,0:T(8,128)S(1)} %fusion.7.refs_0_), channel_id=1, source_target_pairs={{0,2},{1,9},{2,0},{3,11},{4,6},{5,13},{6,4},{7,15},{8,10},{9,1},{1... | collective-permute-start | bytes 393224 | tf_op jit(solution)/shard_map/ppermute | solution.py:230
  53.2 8.2 %collective-permute-start.17 = (f32[72,512]{1,0:T(8,128)S(1)}, f32[72,512]{1,0:T(8,128)S(1)}, u32[]{:S(2)}, u32[]{:S(2)}) collective-permute-start(f32[72,512]{1,0:T(8,128)S(1)} %get-tuple-element.37), channel_id=1, source_target_pairs={{0,16},{1,5},{2,18},{3,7},{4,20},{5,1},{6,22},{7,3},{8,24},{9,13},... | collective-permute-start | bytes 442376 | tf_op jit(solution)/shard_map/ppermute | solution.py:230
  56.7 7.1 %collective-permute-start.18 = (f32[72,512]{1,0:T(8,128)S(1)}, f32[72,512]{1,0:T(8,128)S(1)}, u32[]{:S(2)}, u32[]{:S(2)}) collective-permute-start(f32[72,512]{1,0:T(8,128)S(1)} %get-tuple-element.38), channel_id=1, source_target_pairs={{0,24},{1,7},{2,26},{3,5},{4,28},{5,3},{6,30},{7,1},{8,16},{9,15},... | collective-permute-start | bytes 442376 | tf_op jit(solution)/shard_map/ppermute | solution.py:230
  58.9 6.4 %collective-permute-start.16 = (f32[72,512]{1,0:T(8,128)S(1)}, f32[72,512]{1,0:T(8,128)S(1)}, u32[]{:S(2)}, u32[]{:S(2)}) collective-permute-start(f32[72,512]{1,0:T(8,128)S(1)} %get-tuple-element.36), channel_id=1, source_target_pairs={{0,8},{1,3},{2,10},{3,1},{4,12},{5,7},{6,14},{7,5},{8,0},{9,11},{1... | collective-permute-start | bytes 442376 | tf_op jit(solution)/shard_map/ppermute | solution.py:230
  65.4 6.0 %collective-permute-start.21 = (f32[64,512]{1,0:T(8,128)S(1)}, f32[64,512]{1,0:T(8,128)S(1)}, u32[]{:S(2)}, u32[]{:S(2)}) collective-permute-start(f32[64,512]{1,0:T(8,128)S(1)} %fusion.3.refs_0_), channel_id=1, source_target_pairs={{0,6},{1,25},{2,4},{3,27},{4,2},{5,29},{6,0},{7,31},{8,14},{9,17},... | collective-permute-start | bytes 393224 | tf_op jit(solution)/shard_map/ppermute | solution.py:230
  67.0 5.8 %collective-permute-start.20 = (f32[64,512]{1,0:T(8,128)S(1)}, f32[64,512]{1,0:T(8,128)S(1)}, u32[]{:S(2)}, u32[]{:S(2)}) collective-permute-start(f32[64,512]{1,0:T(8,128)S(1)} %fusion.3.refs_0_), channel_id=1, source_target_pairs={{0,4},{1,17},{2,6},{3,19},{4,0},{5,21},{6,2},{7,23},{8,12},{9,25},... | collective-permute-start | bytes 393224 | tf_op jit(solution)/shard_map/ppermute | solution.py:230
  67.9 5.0 %collective-permute-start.19 = (f32[64,512]{1,0:T(8,128)S(1)}, f32[64,512]{1,0:T(8,128)S(1)}, u32[]{:S(2)}, u32[]{:S(2)}) collective-permute-start(f32[64,512]{1,0:T(8,128)S(1)} %fusion.3.refs_0_), channel_id=1, source_target_pairs={{0,2},{1,9},{2,0},{3,11},{4,6},{5,13},{6,4},{7,15},{8,10},{9,1},{1... | collective-permute-start | bytes 393224 | tf_op jit(solution)/shard_map/ppermute | solution.py:230
  74.3 8.1 %collective-permute-start.23 = (f32[64,512]{1,0:T(8,128)S(1)}, f32[64,512]{1,0:T(8,128)S(1)}, u32[]{:S(2)}, u32[]{:S(2)}) collective-permute-start(f32[64,512]{1,0:T(8,128)S(1)} %get-tuple-element.41), channel_id=1, source_target_pairs={{0,16},{1,5},{2,18},{3,7},{4,20},{5,1},{6,22},{7,3},{8,24},{9,13},... | collective-permute-start | bytes 393224 | tf_op jit(solution)/shard_map/ppermute | solution.py:230
  75.2 7.1 %collective-permute-start.24 = (f32[64,512]{1,0:T(8,128)S(1)}, f32[64,512]{1,0:T(8,128)S(1)}, u32[]{:S(2)}, u32[]{:S(2)}) collective-permute-start(f32[64,512]{1,0:T(8,128)S(1)} %get-tuple-element.42), channel_id=1, source_target_pairs={{0,24},{1,7},{2,26},{3,5},{4,28},{5,3},{6,30},{7,1},{8,16},{9,15},... | collective-permute-start | bytes 393224 | tf_op jit(solution)/shard_map/ppermute | solution.py:230
  77.9 5.7 %collective-permute-start.22 = (f32[64,512]{1,0:T(8,128)S(1)}, f32[64,512]{1,0:T(8,128)S(1)}, u32[]{:S(2)}, u32[]{:S(2)}) collective-permute-start(f32[64,512]{1,0:T(8,128)S(1)} %get-tuple-element.40), channel_id=1, source_target_pairs={{0,8},{1,3},{2,10},{3,1},{4,12},{5,7},{6,14},{7,5},{8,0},{9,11},{1... | collective-permute-start | bytes 393224 | tf_op jit(solution)/shard_map/ppermute | solution.py:230
  83.7 1.3 %collective-permute-start.25 = (f32[64,256]{1,0:T(8,128)S(1)}, f32[64,256]{1,0:T(8,128)S(1)}, u32[]{:S(2)}, u32[]{:S(2)}) collective-permute-start(f32[64,256]{1,0:T(8,128)S(1)} %get-tuple-element.48), channel_id=1, source_target_pairs={{0,1},{1,0},{2,3},{3,2},{4,5},{5,4},{6,7},{7,6},{8,9},{9,8},{10,11... | collective-permute-start | bytes 196616 | tf_op jit(solution)/shard_map/ppermute | solution.py:377

commit v3 on v2

--- a/solution.py
+++ b/solution.py
@@ -77,85 +77,109 @@
     return coarse, fine
 
 
-def pull_kernel(inverse, full, spans, first, last, *refs):
+def pull_kernel(inverse, full, width, count, spans, skip, first, last, after_other, *refs):
     refs = list(refs)
     core = refs.pop(0)
-    block = refs.pop(0)
-    if first:
-        sources = [refs.pop(0) for _ in spans]
+    blocks = [refs.pop(0) for _ in range(count)]
+    if first == "features":
+        sources = [refs.pop(0) for _ in range(after_other)]
         cols, after = refs.pop(0), refs.pop(0)
     else:
-        cols, before = refs.pop(0), refs.pop(0)
+        cols = refs.pop(0)
+        before = None if first else refs.pop(0)
+        del refs[:after_other]
         after = [refs.pop(0) for _ in range(len(spans) + 1)] if last else refs.pop(0)
     stacked, rows, high, low = refs
-    half, width = full // 2, cols.shape[1] // (len(spans) * (2 if last else 1))
-    a, b = parts_of(block[:full] * 4.0, 2)
-    stacked[:full] = a
-    stacked[full:] = b
-    rows[...] = point_features(block[full : full + 3], inverse, True)
-    if first:
-        for k in spans:
-            cols[:, k * width : (k + 1) * width] = point_features(sources[k][...], inverse, False)
+    half = full // 2
+    if first == "features":
+        for k, source in enumerate(sources):
+            cols[:, k * width : (k + 1) * width] = point_features(source[...], inverse, False)
     step = 2 if len(spans) % 2 == 0 else 1
-    for k in range(0, len(spans), step):
-        at = slice(spans[k] * width, (spans[k] + step) * width)
-        evaluate(rows, 0, cols[:, at], high, low, 0, 128)
-        coarse, fine = product(stacked[...], full, high[...], low[...])
-        total = coarse[:full] + coarse[full:] + fine
-        if not first:
-            total = before[:, at] + total
-        if not last:
-            after[:, at] = total
-            continue
-        mine = jnp.where(core[0] == 0, total[:half], total[half:])
-        for i in range(step):
-            after[k + i][...] = mine[:, i * width : (i + 1) * width]
-        after[-1][:, k * width : (k + step) * width] = jnp.where(core[0] == 0, total[half:], total[:half])
-
-
-def keep_kernel(inverse, row_points, col_points, high, low, zero, rows, cols):
+    sums = [None] * len(spans)
+    for n in range(count):
+        a, b = parts_of(blocks[n][:full] * 4.0, 2)
+        stacked[:full] = a
+        stacked[full:] = b
+        rows[...] = point_features(blocks[n][full : full + 3], inverse, True)
+        for k in range(0, len(spans), step):
+            evaluate(rows, 0, cols[:, spans[k] * width : (spans[k] + step) * width], high, low, 0, 128)
+            coarse, fine = product(stacked[...], full, high[...], low[...])
+            total = coarse[:full] + coarse[full:] + fine
+            at = slice(k * width, (k + step) * width)
+            if n:
+                total = sums[k] + total
+            elif not first:
+                total = before[:, skip + at.start : skip + at.stop] + total
+            sums[k] = total
+            if n < count - 1:
+                continue
+            if not last:
+                after[:, at] = total
+                continue
+            mine = jnp.where(core[0] == 0, total[:half], total[half:])
+            for i in range(step):
+                after[k + i][...] = mine[:, i * width : (i + 1) * width]
+            after[-1][:, at] = jnp.where(core[0] == 0, total[half:], total[:half])
+
+
+def keep_kernel(inverse, start, row_points, col_points, high, low, zero, rows, cols):
     zero[...] = jnp.zeros_like(zero)
-    rows[...] = point_features(row_points[...], inverse, True)
+    rows[...] = point_features(row_points[:, start : start + rows.shape[1]], inverse, True)
     cols[...] = point_features(col_points[...], inverse, False)
     count, width = rows.shape[1], math.gcd(cols.shape[1], 1024)
+    sub = math.gcd(count, 256)
 
     def tile(which, carry):
         at = pl.ds(pl.multiple_of(which * width, width), width)
         wide = cols[:, at]
-        for row in range(0, count, 256):
+        for row in range(0, count, sub):
             square = lax.dot_general(
-                rows[:, row : row + 256], wide, (((0,), (0,)), ((), ())), preferred_element_type=F32
+                rows[:, row : row + sub], wide, (((0,), (0,)), ((), ())), preferred_element_type=F32
             )
             value = quarter_wendland(square)
             rounded = value.astype(BF16)
-            high[row : row + 256, at] = rounded
-            low[row : row + 256, at] = (value - rounded.astype(F32)).astype(BF16)
+            high[row : row + sub, at] = rounded
+            low[row : row + sub, at] = (value - rounded.astype(F32)).astype(BF16)
         return carry
 
     lax.fori_loop(0, cols.shape[1] // width, tile, 0)
 
 
-def step_kernel(half, peers, spans, with_sums, *refs):
-    blocks, high, low = refs[:peers], refs[peers], refs[peers + 1]
-    outs, stacked = refs[peers + 2 : -1], refs[-1]
-    count = blocks[0].shape[1]
+def step_kernel(half, start, count, spans, with_sums, first, last, *refs):
+    refs = list(refs)
+    blocks = [refs.pop(0) for _ in range(count)]
+    high, low = refs.pop(0), refs.pop(0)
+    before = None if first else refs.pop(0)
+    del refs[:1]
+    stacked, outs = refs[-1], refs[:-1]
+    size = blocks[0].shape[1]
     upper = half + (ONES if with_sums else 0)
-    for k in range(peers):
+    for k in range(count):
         a, b = parts_of(blocks[k][...] * 4.0, 2)
-        stacked[:half, k * count : (k + 1) * count] = a
-        stacked[upper:, k * count : (k + 1) * count] = b
+        stacked[:half, k * size : (k + 1) * size] = a
+        stacked[upper:, k * size : (k + 1) * size] = b
     if with_sums:
         stacked[half:upper, :] = jnp.full((ONES, stacked.shape[1]), 4.0, BF16)
     step = 2 if len(spans) % 2 == 0 else 1
+    along = slice(start * size, (start + count) * size)
     for k in range(0, len(spans), step):
-        span = slice(spans[k] * count, (spans[k] + step) * count)
-        coarse, fine = product(stacked[...], upper, high[:, span], low[:, span])
+        span = slice(spans[k] * size, (spans[k] + step) * size)
+        coarse, fine = product(stacked[...], upper, high[along, span], low[along, span])
         total = coarse[:half] + coarse[upper:] + fine[:half]
+        sums = coarse[half : half + 8] + fine[half : half + 8] if with_sums else None
+        if not first:
+            total = before[:half, span] + total
+            sums = before[half:, span] + sums if with_sums else None
+        if not last:
+            outs[0][:half, span] = total
+            if with_sums:
+                outs[0][half:, span] = sums
+            continue
         for i in range(step):
-            at = slice(i * count, (i + 1) * count)
+            at = slice(i * size, (i + 1) * size)
             outs[k + i][:half] = total[:, at]
             if with_sums:
-                outs[k + i][half:] = coarse[half : half + 8, at] + fine[half : half + 8, at]
+                outs[k + i][half:] = sums[:, at]
 
 
 def again_kernel(inverse, half, peers, with_sums, *refs):
@@ -191,10 +215,8 @@
     return pltpu.CompilerParams(vmem_limit_bytes=24 << 20)
 
 
-def cost(rows, cols, half, evaluated):
-    return pl.CostEstimate(
-        flops=rows * cols * (6 * half + (200 if evaluated else 0)), bytes_accessed=4 * rows * half, transcendentals=0
-    )
+def cost(rows, half, weight=1):
+    return pl.CostEstimate(flops=rows * half * weight, bytes_accessed=half, transcendentals=0)
 
 
 def per_device(vol_grad, vol_coords, ctrl_coords):
@@ -243,7 +265,9 @@
         ],
         axis=0,
     )
-    ctrl = ordered(ctrl_coords, lax.ppermute(ctrl_coords, "src", sibling), 1)
+    got = lax.ppermute(ctrl_coords, "src", sibling)
+    block, got = lax.optimization_barrier((block, got))
+    ctrl = ordered(ctrl_coords, got, 1)
     blocks = [block] + [exchange(block, along_src[k]) for k in range(1, peers)]
     tgt_ctrl = [ctrl] + [exchange(ctrl, along_tgt[k]) for k in range(1, peers)]
 
@@ -251,54 +275,49 @@
     total_width = peers * width
     core_of = jnp.reshape(core, (1,)).astype(jnp.int32)
     scalar = [pl.BlockSpec(memory_space=pltpu.SMEM)]
-    span_step = 2 if peers % 4 == 0 else 1
-    pull_scratch = [
-        pltpu.VMEM((2 * full, volume), BF16),
-        pltpu.VMEM((FEATURES, volume), BF16),
-        pltpu.VMEM((volume, span_step * width), BF16),
-        pltpu.VMEM((volume, span_step * width), BF16),
-    ]
-
-    def pull(which, spans, cols, before, last):
-        first = which == 0
-        sums = pltpu.VMEM((full, total_width), F32)
+    anywhere = [pl.BlockSpec(memory_space=pl.ANY)]
+    def pull(which, spans, cols, before, last, skip=0, other=(), weight=1):
+        first = before is None
+        step = 2 if len(spans) % 2 == 0 else 1
         if last:
             shapes = [jax.ShapeDtypeStruct((half, width), F32)] * len(spans)
             shapes.append(jax.ShapeDtypeStruct((half, len(spans) * width), F32))
         else:
-            shapes = [pltpu.VMEM((FEATURES, total_width), BF16), sums] if first else [sums]
-        if first:
-            inputs = [core_of, blocks[which], *tgt_ctrl]
+            shapes = [pltpu.VMEM((full, len(spans) * width), F32)]
+        inputs = [core_of, *[blocks[k] for k in which]]
+        if cols is None:
+            first = "features"
+            shapes = [pltpu.VMEM((FEATURES, total_width), BF16)] + shapes
+            inputs += tgt_ctrl
         else:
-            inputs = [core_of, blocks[which]]
-            inputs += [pltpu.with_memory_space_constraint(value, pltpu.VMEM) for value in (cols, before)]
+            inputs.append(pltpu.with_memory_space_constraint(cols, pltpu.VMEM))
+        if not first:
+            inputs.append(pltpu.with_memory_space_constraint(before, pltpu.VMEM))
+        in_specs = scalar + vmem(len(inputs) - 1) + anywhere * len(other)
+        inputs += other
+        extra = len(tgt_ctrl) if cols is None else len(other)
         return pl.pallas_call(
-            functools.partial(pull_kernel, inverse, full, spans, first, last),
+            functools.partial(
+                pull_kernel, inverse, full, width, len(which), spans, skip, first, last, extra
+            ),
             out_shape=shapes,
-            in_specs=scalar + vmem(len(inputs) - 1),
+            in_specs=in_specs,
             out_specs=vmem(len(shapes)),
-            scratch_shapes=pull_scratch,
-            input_output_aliases={} if first or last else {3: 0},
+            scratch_shapes=[
+                pltpu.VMEM((2 * full, volume), BF16),
+                pltpu.VMEM((FEATURES, volume), BF16),
+                pltpu.VMEM((volume, step * width), BF16),
+                pltpu.VMEM((volume, step * width), BF16),
+            ],
             compiler_params=params(),
-            cost_estimate=cost(volume, len(spans) * width, full, True),
+            cost_estimate=cost(len(which) * volume, full, weight),
         )(*inputs)
 
     near, far = list(range(peers // 2)), list(range(peers // 2, peers))
-    cols, sofar = pull(0, near + far, None, None, False)
-    for k in range(1, peers - 1):
-        (sofar,) = pull(k, near + far, cols, sofar, False)
+    cols, far_sofar = pull([0], far, None, None, False)
+    (near_sofar,) = pull([0], near, cols, None, False)
     sums = [None] * peers
-    for spans in (far, near):
-        *mine, other = pull(peers - 1, spans, cols, sofar, True)
-        other = lax.ppermute(other, "src", sibling)
-        for i, k in enumerate(spans):
-            sums[k] = mine[i] + other[:, i * width : (i + 1) * width]
-
-    def summed(values):
-        total = values[0]
-        for k in range(1, peers):
-            total = total + exchange(values[k], sum_pairs[k])
-        return total
+    arriving = list(range(1, peers))
 
     theirs = jnp.concatenate([b[full + 3 : full + 6, :owned] for b in blocks[1:]], axis=1)
     others = lax.ppermute(theirs, "src", sibling)
@@ -311,19 +330,70 @@
     row_points = jnp.where(first_core, src_points, tgt_points)
     col_points = jnp.where(first_core, tgt_points, src_points)
 
+    def added(spans, mine, other, pieces=1):
+        rows = half // pieces
+        other = [lax.ppermute(other[i * rows : (i + 1) * rows], "src", sibling) for i in range(pieces)]
+        other = jnp.concatenate(other, axis=0)
+        for i, k in enumerate(spans):
+            sums[k] = mine[i] + other[:, i * width : (i + 1) * width]
+
+    *mine, other = pull(arriving, far, cols, far_sofar, True, weight=8 * width)
+    added(far, mine, other)
+    if near[1:]:
+        *mine, other = pull(arriving, near[1:], cols, near_sofar, True, width, [other], 4 * width)
+        added(near[1:], mine, other)
+    *mine, other = pull(arriving, near[:1], cols, near_sofar, True, 0, [sums[k] for k in range(1, peers)] + [row_points, col_points])
+    added(near[:1], mine, other, 2)
+
+    def summed(values):
+        order = [peers // 2] + [k for k in range(1, peers) if k != peers // 2]
+        got = {k: exchange(values[k], sum_pairs[k]) for k in order}
+        total = values[0]
+        for k in order:
+            total = total + got[k]
+        return total
+
     kept = (peers * width) ** 2 * 4 <= KEPT_BYTES
     pullback = sums[0]
-    if kept:
-        high, low, zero = pl.pallas_call(
-            functools.partial(keep_kernel, inverse),
-            out_shape=[pltpu.VMEM((peers * width, peers * width), BF16)] * 2 + [jax.ShapeDtypeStruct((8, 128), F32)],
+    def keep(start, count):
+        return pl.pallas_call(
+            functools.partial(keep_kernel, inverse, start * width),
+            out_shape=[pltpu.VMEM((count * width, total_width), BF16)] * 2
+            + [jax.ShapeDtypeStruct((1, width), F32)],
             in_specs=vmem(2),
             out_specs=vmem(3),
-            scratch_shapes=[pltpu.VMEM((FEATURES, peers * width), BF16)] * 2,
+            scratch_shapes=[pltpu.VMEM((FEATURES, count * width), BF16), pltpu.VMEM((FEATURES, total_width), BF16)],
             compiler_params=params(),
-            cost_estimate=cost(peers * width, peers * width, 0, True),
+            cost_estimate=cost(total_width, half),
         )(row_points, col_points)
-        pullback = pullback + zero[0, 0]
+
+    if kept:
+        *early, zero = keep(0, peers - 1)
+        *final, after_final = keep(peers - 1, 1)
+        pullback = pullback + zero
+
+    def step(these, part, start, spans, before, with_sums, last, other):
+        out_rows = half + (8 if with_sums else 0)
+        if last:
+            shapes = [jax.ShapeDtypeStruct((out_rows, width), F32)] * len(spans)
+        else:
+            shapes = [pltpu.VMEM((out_rows, total_width), F32)]
+        inputs = these + [pltpu.with_memory_space_constraint(value, pltpu.VMEM) for value in part]
+        if before is not None:
+            inputs.append(pltpu.with_memory_space_constraint(before, pltpu.VMEM))
+        upper = half + (ONES if with_sums else 0)
+        return pl.pallas_call(
+            functools.partial(
+                step_kernel, half, start, len(these), spans, with_sums, before is None, last
+            ),
+            out_shape=shapes,
+            in_specs=vmem(len(inputs)) + anywhere,
+            out_specs=vmem(len(shapes)),
+            scratch_shapes=[pltpu.VMEM((upper + half, len(these) * width), BF16)],
+            compiler_params=params(),
+            cost_estimate=cost(total_width, half),
+        )(*inputs, other)
+
     for k in range(1, peers):
         pullback = pullback + exchange(sums[k], along_tgt[k])
 
@@ -331,27 +401,17 @@
     for sweep in range(STEPS):
         arrived = [iterate] + [exchange(iterate, gather_pairs[k]) for k in range(1, peers)]
         with_sums = sweep == 0
-        upper = half + (ONES if with_sums else 0)
-        out_rows = half + (8 if with_sums else 0)
-        products = [None] * peers
         if kept:
-            for spans in (far, near):
-                found = pl.pallas_call(
-                    functools.partial(step_kernel, half, peers, spans, with_sums),
-                    out_shape=[jax.ShapeDtypeStruct((out_rows, width), F32)] * len(spans),
-                    in_specs=vmem(peers + 2),
-                    out_specs=vmem(len(spans)),
-                    scratch_shapes=[pltpu.VMEM((upper + half, peers * width), BF16)],
-                    compiler_params=params(),
-                    cost_estimate=cost(peers * width, len(spans) * width, half, False),
-                )(
-                    *arrived,
-                    pltpu.with_memory_space_constraint(high, pltpu.VMEM),
-                    pltpu.with_memory_space_constraint(low, pltpu.VMEM),
-                )
-                for k, value in zip(spans, found):
-                    products[k] = value
+            spans = near + far
+            (sofar,) = step(arrived[:1], early, 0, spans, None, with_sums, False, after_final)
+            if peers > 2:
+                (sofar,) = step(arrived[1:-1], early, 1, spans, sofar, with_sums, False, after_final)
+            far_ones = step(arrived[-1:], final, 0, far, sofar, with_sums, True, after_final)
+            near_ones = step(arrived[-1:], final, 0, near, sofar, with_sums, True, far_ones[0])
+            products = [*near_ones, *far_ones]
         else:
+            upper = half + (ONES if with_sums else 0)
+            out_rows = half + (8 if with_sums else 0)
             products = pl.pallas_call(
                 functools.partial(again_kernel, inverse, half, peers, with_sums),
                 out_shape=[jax.ShapeDtypeStruct((out_rows, width), F32)] * peers,
@@ -365,7 +425,7 @@
                     pltpu.VMEM((width, width), BF16),
                 ],
                 compiler_params=params(),
-                cost_estimate=cost(peers * width, peers * width, half, True),
+                cost_estimate=cost(total_width, half),
             )(*arrived, row_points, col_points)
         total = summed(products)
         if with_sums:

time: 86 us -> 83.7 us (0.973)
  waiting for transfers between devices: 27.7 us -> 19.3 us
  starting transfers between devices: 29 us -> 35.1 us
  Pallas kernels: 24.7 us -> 25.9 us
    ppermute x21, waiting for transfers between devices: 25 us -> 16.8 us  [exchange(): return lax.ppermute(value, ('tgt', 'src'), pairs)]
    ppermute x21, starting transfers between devices: 28.2 us -> 33.3 us  [exchange(): return lax.ppermute(value, ('tgt', 'src'), pairs)]
    pallas_call x10 -> x15, Pallas kernels: 24.7 us -> 25.9 us  [the longest x5 10.8 us: pull(): pl.pallas_call(functools.partial(pull_kernel, inverse, full, width, len(w...]
    ppermute x3 -> x5, starting transfers between devices: 0.65 us -> 1.67 us  [the longest x4 1.22 us: added(): lax.ppermute(other[i * rows:(i + 1) * rows], 'src', sibling)]
  transfers between devices with their start and end apart: 26 -> 28, of which waited for: 17 -> 12; matrix products, arithmetic and copies ran while one was open for 2% -> 2% of each run, Pallas kernels for 25% -> 30%
where the time goes in v3:
time: 83.7 us; the launch traced here: 83.6 us
  starting transfers between devices  35.1 us (42%)
  Pallas kernels  25.9 us (31%)
  waiting for transfers between devices  19.3 us (23%)
  other arithmetic  2.83 us (3%)
    ppermute x21, starting transfers between devices, exchange(): return lax.ppermute(value, ('tgt', 'src'), pairs)  33.3 us
    ppermute x21, waiting for transfers between devices, exchange(): return lax.ppermute(value, ('tgt', 'src'), pairs)  16.8 us
    pallas_call x5, Pallas kernels, pull(): pl.pallas_call(functools.partial(pull_kernel, inverse, full, width, len(w...  10.8 us
    pallas_call x2, Pallas kernels, keep(): pl.pallas_call(functools.partial(keep_kernel, inverse, start * width), ou...  8.69 us
    pallas_call x8, Pallas kernels, step(): pl.pallas_call(functools.partial(step_kernel, half, start, len(these), sp...  6.42 us
  transfers between devices with their start and end apart: 28, of which 12 were waited for; matrix products, arithmetic and copies ran while one was open for 2% of the time, Pallas kernels for 30%

profile of v3, /device:TPU:0, one launch (start us, length us, event | category | flops | bytes accessed | tf_op | source)
XLA Modules:
  0.0 83.6 jit_solution(13925747423978258243)
XLA Ops:
  0.0 0.5 collective-permute-start
  0.5 0.1 pad.41.clone
  0.5 1.1 %fusion.refs_1_ = f32[136,512]{1,0:T(8,128)S(1)} fusion(f32[3,256]{1,0:T(4,128)} %param.5, f32[3,512]{1,0:T(4,128)} %param.4, f32[128,512]{1,0:T(8,128)} %param.3, f32[136]{0:T(256)S(1)} %pad.41.clone), kind=kLoop, calls=%fused_computation.3 | loop fusion | flops 487424 | bytes 550432 | tf_op jit(solution)/shard_map/concatenate | solution.py:259
  1.6 2.7 %collective-permute-start.1 = (f32[136,512]{1,0:T(8,128)S(1)}, f32[136,512]{1,0:T(8,128)S(1)}, u32[]{:S(2)}, u32[]{:S(2)}) collective-permute-start(f32[136,512]{1,0:T(8,128)S(1)} %fusion.refs_1_), channel_id=1, source_target_pairs={{0,2},{1,3},{2,0},{3,1},{4,6},{5,7},{6,4},{7,5},{8,10},{9,11},{10,... | collective-permute-start | bytes 835592 | tf_op jit(solution)/shard_map/ppermute | solution.py:252
  4.3 1.5 %collective-permute-start.2 = (f32[136,512]{1,0:T(8,128)S(1)}, f32[136,512]{1,0:T(8,128)S(1)}, u32[]{:S(2)}, u32[]{:S(2)}) collective-permute-start(f32[136,512]{1,0:T(8,128)S(1)} %fusion.refs_1_), channel_id=1, source_target_pairs={{0,4},{1,5},{2,6},{3,7},{4,0},{5,1},{6,2},{7,3},{8,12},{9,13},{10,... | collective-permute-start | bytes 835592 | tf_op jit(solution)/shard_map/ppermute | solution.py:252
  5.9 0.8 maximum_select_fusion.1.refs_2_
  6.6 2.1 %collective-permute-start.4 = (f32[3,512]{1,0:T(4,128)S(1)}, f32[3,512]{1,0:T(4,128)S(1)}, u32[]{:S(2)}, u32[]{:S(2)}) collective-permute-start(f32[3,512]{1,0:T(4,128)S(1)} %maximum_select_fusion.1.refs_2_), channel_id=1, source_target_pairs={{0,8},{1,9},{2,10},{3,11},{4,12},{5,13},{6,14},{7,15},{8,0},{9,1},... | collective-permute-start | bytes 18440 | tf_op jit(solution)/shard_map/ppermute | solution.py:252
  8.7 2.6 %collective-permute-start.5 = (f32[3,512]{1,0:T(4,128)S(1)}, f32[3,512]{1,0:T(4,128)S(1)}, u32[]{:S(2)}, u32[]{:S(2)}) collective-permute-start(f32[3,512]{1,0:T(4,128)S(1)} %maximum_select_fusion.1.refs_2_), channel_id=1, source_target_pairs={{0,16},{1,17},{2,18},{3,19},{4,20},{5,21},{6,22},{7,23},{8,24},{9,... | collective-permute-start | bytes 18440 | tf_op jit(solution)/shard_map/ppermute | solution.py:252
  11.3 0.0 collective-permute-done.4.refs_3_
  11.3 3.1 %collective-permute-start.6 = (f32[3,512]{1,0:T(4,128)S(1)}, f32[3,512]{1,0:T(4,128)S(1)}, u32[]{:S(2)}, u32[]{:S(2)}) collective-permute-start(f32[3,512]{1,0:T(4,128)S(1)} %maximum_select_fusion.1.refs_2_), channel_id=1, source_target_pairs={{0,24},{1,25},{2,26},{3,27},{4,28},{5,29},{6,30},{7,31},{8,16},{9,... | collective-permute-start | bytes 18440 | tf_op jit(solution)/shard_map/ppermute | solution.py:252
  14.4 0.0 collective-permute-done.5.refs_4_
  14.4 2.4 %collective-permute-done.6.refs_5_ = f32[3,512]{1,0:T(4,128)S(1)} collective-permute-done((f32[3,512]{1,0:T(4,128)S(1)}, f32[3,512]{1,0:T(4,128)S(1)}, u32[]{:S(2)}, u32[]{:S(2)}) %collective-permute-start.6) | collective-permute-done | bytes 6176 | tf_op jit(solution)/shard_map/ppermute | solution.py:252
  16.7 1.4 %shard_map.37 = (bf16[32,2048]{1,0:T(8,128)(2,1)S(1)}, f32[128,1024]{1,0:T(8,128)S(1)}) custom-call(s32[1]{0:T(128)} %bitcast.refs_0_, f32[136,512]{1,0:T(8,128)S(1)} %fusion.refs_1_, f32[3,512]{1,0:T(4,128)S(1)} %maximum_select_fusion.1.refs_2_, f32[3,512]{1,0:T(4,128)S(1)} %collective-permute-done.4.refs_3_, f32[3,512]{1,0:T(4,128)S(1)} %collective-permute-done.5.refs_4_, ...), custom_call_target="tpu_custom_call" | custom-call | flops 65536 | bytes 128 | tf_op jit(solution)/shard_map/pallas_call | solution.py:299
  18.2 1.4 %shard_map.38.refs_5_ = f32[128,1024]{1,0:T(8,128)S(1)} custom-call(s32[1]{0:T(128)} %bitcast.refs_0_, f32[136,512]{1,0:T(8,128)S(1)} %fusion.refs_1_, bf16[32,2048]{1,0:T(8,128)(2,1)S(1)} %get-tuple-element.32.refs_2_.refs_4_), custom_call_target="tpu_custom_call" | custom-call | flops 65536 | bytes 128 | tf_op jit(solution)/shard_map/pallas_call | solution.py:299
  19.6 0.0 collective-permute-done.3.refs_3_
  19.6 0.1 collective-permute-start.9
  19.7 3.7 %shard_map.39 = (f32[64,512]{1,0:T(8,128)S(1)}, f32[64,512]{1,0:T(8,128)S(1)}, f32[64,1024]{1,0:T(8,128)S(1)}) custom-call(s32[1]{0:T(128)} %bitcast.refs_0_, f32[136,512]{1,0:T(8,128)S(1)} %collective-permute-done.1.refs_1_, f32[136,512]{1,0:T(8,128)S(1)} %collective-permute-done.2.refs_2_, f32[136,512]{1,0:T(8,128)S(1)} %collective-permute-done.3.refs_3_, ...), custom_call_target="tpu_custom_call" | custom-call | flops 805306368 | bytes 128 | tf_op jit(solution)/shard_map/pallas_call | solution.py:299
  23.4 0.6 collective-permute-start.8
  23.9 2.2 %shard_map.40 = (f32[64,512]{1,0:T(8,128)S(1)}, f32[64,512]{1,0:T(8,128)S(1)}) custom-call(s32[1]{0:T(128)} %bitcast.refs_0_, f32[136,512]{1,0:T(8,128)S(1)} %collective-permute-done.1.refs_1_, f32[136,512]{1,0:T(8,128)S(1)} %collective-permute-done.2.refs_2_, f32[136,512]{1,0:T(8,128)S(1)} %collective-permute-done.3.refs_3_, ...), custom_call_target="tpu_custom_call" | custom-call | flops 402653184 | bytes 128 | tf_op jit(solution)/shard_map/pallas_call | solution.py:299
  26.1 0.1 collective-permute-start.7
  26.2 0.0 collective-permute-done.9
  26.3 1.3 %collective-permute-done.7 = f32[64,512]{1,0:T(8,128)S(1)} collective-permute-done((f32[64,512]{1,0:T(8,128)S(1)}, f32[64,512]{1,0:T(8,128)S(1)}, u32[]{:S(2)}, u32[]{:S(2)}) %collective-permute-start.7) | collective-permute-done | bytes 131104 | tf_op jit(solution)/shard_map/ppermute | solution.py:335
  27.6 1.0 %collective-permute-start.12 = (f32[64,512]{1,0:T(8,128)S(1)}, f32[64,512]{1,0:T(8,128)S(1)}, u32[]{:S(2)}, u32[]{:S(2)}) collective-permute-start(f32[64,512]{1,0:T(8,128)S(1)} %add.65.refs_6_), channel_id=1, source_target_pairs={{0,8},{1,9},{2,10},{3,11},{4,12},{5,13},{6,14},{7,15},{8,0},{9,1},... | collective-permute-start | bytes 393224 | tf_op jit(solution)/shard_map/ppermute | solution.py:252
  28.6 2.8 %collective-permute-start.13 = (f32[64,512]{1,0:T(8,128)S(1)}, f32[64,512]{1,0:T(8,128)S(1)}, u32[]{:S(2)}, u32[]{:S(2)}) collective-permute-start(f32[64,512]{1,0:T(8,128)S(1)} %get-tuple-element.57.refs_7_), channel_id=1, source_target_pairs={{0,16},{1,17},{2,18},{3,19},{4,20},{5,21},{6,22},{7,23},{8,24},{9,... | collective-permute-start | bytes 393224 | tf_op jit(solution)/shard_map/ppermute | solution.py:252
  31.4 0.7 collective-permute-start.14
  32.1 2.2 %shard_map.41 = (f32[64,512]{1,0:T(8,128)S(1)}, f32[64,512]{1,0:T(8,128)S(1)}) custom-call(s32[1]{0:T(128)} %bitcast.refs_0_, f32[136,512]{1,0:T(8,128)S(1)} %collective-permute-done.1.refs_1_, f32[136,512]{1,0:T(8,128)S(1)} %collective-permute-done.2.refs_2_, f32[136,512]{1,0:T(8,128)S(1)} %collective-permute-done.3.refs_3_, ...), custom_call_target="tpu_custom_call" | custom-call | flops 196608 | bytes 128 | tf_op jit(solution)/shard_map/pallas_call | solution.py:299
  34.3 0.1 collective-permute-start.10
  34.4 0.5 collective-permute-start.11
  34.9 6.3 %shard_map.42 = (bf16[1536,2048]{1,0:T(8,128)(2,1)S(1)}, bf16[1536,2048]{1,0:T(8,128)(2,1)S(1)}, f32[1,512]{1,0:T(1,128)S(1)}) custom-call(f32[3,2048]{1,0:T(4,128)S(1)} %get-tuple-element.64.refs_9_.row_points, f32[3,2048]{1,0:T(4,128)S(1)} %get-tuple-element.63.refs_10_.col_points), custom_call_target="tpu_custom_call" | custom-call | flops 131072 | bytes 64 | tf_op jit(solution)/shard_map/pallas_call | solution.py:359
  41.3 0.3 collective-permute-done.13
  41.5 0.1 fusion.7.refs_0_
  41.6 1.4 %collective-permute-start.16 = (f32[64,512]{1,0:T(8,128)S(1)}, f32[64,512]{1,0:T(8,128)S(1)}, u32[]{:S(2)}, u32[]{:S(2)}) collective-permute-start(f32[64,512]{1,0:T(8,128)S(1)} %fusion.7.refs_0_), channel_id=1, source_target_pairs={{0,2},{1,9},{2,0},{3,11},{4,6},{5,13},{6,4},{7,15},{8,10},{9,1},{1... | collective-permute-start | bytes 393224 | tf_op jit(solution)/shard_map/ppermute | solution.py:252
  43.0 1.5 %collective-permute-start.17 = (f32[64,512]{1,0:T(8,128)S(1)}, f32[64,512]{1,0:T(8,128)S(1)}, u32[]{:S(2)}, u32[]{:S(2)}) collective-permute-start(f32[64,512]{1,0:T(8,128)S(1)} %fusion.7.refs_0_), channel_id=1, source_target_pairs={{0,4},{1,17},{2,6},{3,19},{4,0},{5,21},{6,2},{7,23},{8,12},{9,25},... | collective-permute-start | bytes 393224 | tf_op jit(solution)/shard_map/ppermute | solution.py:252
  44.5 0.7 collective-permute-start.15
  45.2 2.4 %shard_map.43 = (bf16[512,2048]{1,0:T(8,128)(2,1)S(1)}, bf16[512,2048]{1,0:T(8,128)(2,1)S(1)}, f32[1,512]{1,0:T(1,128)S(1)}) custom-call(f32[3,2048]{1,0:T(4,128)S(1)} %get-tuple-element.64.refs_9_.row_points, f32[3,2048]{1,0:T(4,128)S(1)} %get-tuple-element.63.refs_10_.col_points), custom_call_target="tpu_custom_call" | custom-call | flops 131072 | bytes 64 | tf_op jit(solution)/shard_map/pallas_call | solution.py:359
  47.5 0.8 shard_map.44.refs_4_
  48.4 1.5 %shard_map.45.refs_3_ = f32[72,2048]{1,0:T(8,128)S(1)} custom-call(f32[64,512]{1,0:T(8,128)S(1)} %collective-permute-done.16.refs_0_, f32[64,512]{1,0:T(8,128)S(1)} %collective-permute-done.17.refs_1_, bf16[1536,2048]{1,0:T(8,128)(2,1)S(1)} %get-tuple-element.44.refs_1_.refs_2_, bf16[1536,2048]{1,0:T(8,128)(2,1)S(1)} %get-tuple-element.45.refs_2_.refs_3_, ...), custom_call_target="tpu_custom_call" | custom-call | flops 131072 | bytes 64 | tf_op jit(solution)/shard_map/pallas_call | solution.py:385
  49.9 0.5 collective-permute-done.15.refs_0_
  50.4 0.5 shard_map.46
  50.8 3.6 %collective-permute-start.18 = (f32[72,512]{1,0:T(8,128)S(1)}, f32[72,512]{1,0:T(8,128)S(1)}, u32[]{:S(2)}, u32[]{:S(2)}) collective-permute-start(f32[72,512]{1,0:T(8,128)S(1)} %get-tuple-element.47.refs_4_), channel_id=1, source_target_pairs={{0,16},{1,5},{2,18},{3,7},{4,20},{5,1},{6,22},{7,3},{8,24},{9,13},... | collective-permute-start | bytes 442376 | tf_op jit(solution)/shard_map/ppermute | solution.py:252
  54.4 0.5 shard_map.47
  54.9 0.1 collective-permute-start.19
  55.0 1.5 %collective-permute-start.20 = (f32[72,512]{1,0:T(8,128)S(1)}, f32[72,512]{1,0:T(8,128)S(1)}, u32[]{:S(2)}, u32[]{:S(2)}) collective-permute-start(f32[72,512]{1,0:T(8,128)S(1)} %get-tuple-element.50), channel_id=1, source_target_pairs={{0,24},{1,7},{2,26},{3,5},{4,28},{5,3},{6,30},{7,1},{8,16},{9,15},... | collective-permute-start | bytes 442376 | tf_op jit(solution)/shard_map/ppermute | solution.py:252
  56.5 3.7 %collective-permute-done.19 = f32[72,512]{1,0:T(8,128)S(1)} collective-permute-done((f32[72,512]{1,0:T(8,128)S(1)}, f32[72,512]{1,0:T(8,128)S(1)}, u32[]{:S(2)}, u32[]{:S(2)}) %collective-permute-start.19) | collective-permute-done | bytes 147488 | tf_op jit(solution)/shard_map/ppermute | solution.py:252
  60.1 2.1 %collective-permute-done.20 = f32[72,512]{1,0:T(8,128)S(1)} collective-permute-done((f32[72,512]{1,0:T(8,128)S(1)}, f32[72,512]{1,0:T(8,128)S(1)}, u32[]{:S(2)}, u32[]{:S(2)}) %collective-permute-start.20) | collective-permute-done | bytes 147488 | tf_op jit(solution)/shard_map/ppermute | solution.py:252
  62.4 0.9 %collective-permute-start.22 = (f32[64,512]{1,0:T(8,128)S(1)}, f32[64,512]{1,0:T(8,128)S(1)}, u32[]{:S(2)}, u32[]{:S(2)}) collective-permute-start(f32[64,512]{1,0:T(8,128)S(1)} %fusion.3.refs_0_), channel_id=1, source_target_pairs={{0,2},{1,9},{2,0},{3,11},{4,6},{5,13},{6,4},{7,15},{8,10},{9,1},{1... | collective-permute-start | bytes 393224 | tf_op jit(solution)/shard_map/ppermute | solution.py:252
  63.3 1.5 %collective-permute-start.23 = (f32[64,512]{1,0:T(8,128)S(1)}, f32[64,512]{1,0:T(8,128)S(1)}, u32[]{:S(2)}, u32[]{:S(2)}) collective-permute-start(f32[64,512]{1,0:T(8,128)S(1)} %fusion.3.refs_0_), channel_id=1, source_target_pairs={{0,4},{1,17},{2,6},{3,19},{4,0},{5,21},{6,2},{7,23},{8,12},{9,25},... | collective-permute-start | bytes 393224 | tf_op jit(solution)/shard_map/ppermute | solution.py:252
  64.8 1.1 %collective-permute-start.21 = (f32[64,512]{1,0:T(8,128)S(1)}, f32[64,512]{1,0:T(8,128)S(1)}, u32[]{:S(2)}, u32[]{:S(2)}) collective-permute-start(f32[64,512]{1,0:T(8,128)S(1)} %fusion.3.refs_0_), channel_id=1, source_target_pairs={{0,6},{1,25},{2,4},{3,27},{4,2},{5,29},{6,0},{7,31},{8,14},{9,17},... | collective-permute-start | bytes 393224 | tf_op jit(solution)/shard_map/ppermute | solution.py:252
  66.0 0.8 shard_map.48.refs_4_
  66.7 0.7 collective-permute-done.22.refs_0_
  67.4 0.9 %collective-permute-done.23.refs_1_ = f32[64,512]{1,0:T(8,128)S(1)} collective-permute-done((f32[64,512]{1,0:T(8,128)S(1)}, f32[64,512]{1,0:T(8,128)S(1)}, u32[]{:S(2)}, u32[]{:S(2)}) %collective-permute-start.23) | collective-permute-done | bytes 131104 | tf_op jit(solution)/shard_map/ppermute | solution.py:252
  68.3 1.4 %shard_map.49.refs_3_ = f32[64,2048]{1,0:T(8,128)S(1)} custom-call(f32[64,512]{1,0:T(8,128)S(1)} %collective-permute-done.22.refs_0_, f32[64,512]{1,0:T(8,128)S(1)} %collective-permute-done.23.refs_1_, bf16[1536,2048]{1,0:T(8,128)(2,1)S(1)} %get-tuple-element.44.refs_1_.refs_2_, bf16[1536,2048]{1,0:T(8,128)(2,1)S(1)} %get-tuple-element.45.refs_2_.refs_3_, ...), custom_call_target="tpu_custom_call" | custom-call | flops 131072 | bytes 64 | tf_op jit(solution)/shard_map/pallas_call | solution.py:385
  69.7 1.0 %collective-permute-done.21.refs_0_ = f32[64,512]{1,0:T(8,128)S(1)} collective-permute-done((f32[64,512]{1,0:T(8,128)S(1)}, f32[64,512]{1,0:T(8,128)S(1)}, u32[]{:S(2)}, u32[]{:S(2)}) %collective-permute-start.21) | collective-permute-done | bytes 131104 | tf_op jit(solution)/shard_map/ppermute | solution.py:252
  70.7 0.5 shard_map.50
  71.2 1.6 %collective-permute-start.24 = (f32[64,512]{1,0:T(8,128)S(1)}, f32[64,512]{1,0:T(8,128)S(1)}, u32[]{:S(2)}, u32[]{:S(2)}) collective-permute-start(f32[64,512]{1,0:T(8,128)S(1)} %get-tuple-element.51.refs_4_), channel_id=1, source_target_pairs={{0,16},{1,5},{2,18},{3,7},{4,20},{5,1},{6,22},{7,3},{8,24},{9,13},... | collective-permute-start | bytes 393224 | tf_op jit(solution)/shard_map/ppermute | solution.py:252
  72.7 0.4 shard_map.51
  73.2 1.5 %collective-permute-start.25 = (f32[64,512]{1,0:T(8,128)S(1)}, f32[64,512]{1,0:T(8,128)S(1)}, u32[]{:S(2)}, u32[]{:S(2)}) collective-permute-start(f32[64,512]{1,0:T(8,128)S(1)} %get-tuple-element.53), channel_id=1, source_target_pairs={{0,8},{1,3},{2,10},{3,1},{4,12},{5,7},{6,14},{7,5},{8,0},{9,11},{1... | collective-permute-start | bytes 393224 | tf_op jit(solution)/shard_map/ppermute | solution.py:252
  74.7 1.4 %collective-permute-start.26 = (f32[64,512]{1,0:T(8,128)S(1)}, f32[64,512]{1,0:T(8,128)S(1)}, u32[]{:S(2)}, u32[]{:S(2)}) collective-permute-start(f32[64,512]{1,0:T(8,128)S(1)} %get-tuple-element.54), channel_id=1, source_target_pairs={{0,24},{1,7},{2,26},{3,5},{4,28},{5,3},{6,30},{7,1},{8,16},{9,15},... | collective-permute-start | bytes 393224 | tf_op jit(solution)/shard_map/ppermute | solution.py:252
  76.1 2.5 %collective-permute-done.25 = f32[64,512]{1,0:T(8,128)S(1)} collective-permute-done((f32[64,512]{1,0:T(8,128)S(1)}, f32[64,512]{1,0:T(8,128)S(1)}, u32[]{:S(2)}, u32[]{:S(2)}) %collective-permute-start.25) | collective-permute-done | bytes 131104 | tf_op jit(solution)/shard_map/ppermute | solution.py:252
  78.7 2.8 %collective-permute-done.26 = f32[64,512]{1,0:T(8,128)S(1)} collective-permute-done((f32[64,512]{1,0:T(8,128)S(1)}, f32[64,512]{1,0:T(8,128)S(1)}, u32[]{:S(2)}, u32[]{:S(2)}) %collective-permute-start.26) | collective-permute-done | bytes 131104 | tf_op jit(solution)/shard_map/ppermute | solution.py:252
  81.5 0.1 multiply_add_fusion
  81.6 0.1 collective-permute-start.27
  81.7 1.2 %collective-permute-done.27 = f32[64,256]{1,0:T(8,128)S(1)} collective-permute-done((f32[64,256]{1,0:T(8,128)S(1)}, f32[64,256]{1,0:T(8,128)S(1)}, u32[]{:S(2)}, u32[]{:S(2)}) %collective-permute-start.27) | collective-permute-done | bytes 65568 | tf_op jit(solution)/shard_map/ppermute | solution.py:437
  82.9 0.7 maximum_select_fusion
  (30 shorter events, 0.3 us)
Async XLA Ops:
  0.0 1.6 %collective-permute-start = (f32[3,256]{1,0:T(4,128)}, f32[3,256]{1,0:T(4,128)S(1)}, u32[]{:S(2)}, u32[]{:S(2)}) collective-permute-start(f32[3,256]{1,0:T(4,128)} %param.5), channel_id=1, source_target_pairs={{0,1},{1,0},{2,3},{3,2},{4,5},{5,4},{6,7},{7,6},{8,9},{9,8},{10,11... | collective-permute-start | bytes 9224 | tf_op jit(solution)/shard_map/ppermute | solution.py:268
  1.6 17.9 %collective-permute-start.1 = (f32[136,512]{1,0:T(8,128)S(1)}, f32[136,512]{1,0:T(8,128)S(1)}, u32[]{:S(2)}, u32[]{:S(2)}) collective-permute-start(f32[136,512]{1,0:T(8,128)S(1)} %fusion.refs_1_), channel_id=1, source_target_pairs={{0,2},{1,3},{2,0},{3,1},{4,6},{5,7},{6,4},{7,5},{8,10},{9,11},{10,... | collective-permute-start | bytes 835592 | tf_op jit(solution)/shard_map/ppermute | solution.py:252
  4.3 15.2 %collective-permute-start.2 = (f32[136,512]{1,0:T(8,128)S(1)}, f32[136,512]{1,0:T(8,128)S(1)}, u32[]{:S(2)}, u32[]{:S(2)}) collective-permute-start(f32[136,512]{1,0:T(8,128)S(1)} %fusion.refs_1_), channel_id=1, source_target_pairs={{0,4},{1,5},{2,6},{3,7},{4,0},{5,1},{6,2},{7,3},{8,12},{9,13},{10,... | collective-permute-start | bytes 835592 | tf_op jit(solution)/shard_map/ppermute | solution.py:252
  5.9 13.7 %collective-permute-start.3 = (f32[136,512]{1,0:T(8,128)S(1)}, f32[136,512]{1,0:T(8,128)S(1)}, u32[]{:S(2)}, u32[]{:S(2)}) collective-permute-start(f32[136,512]{1,0:T(8,128)S(1)} %fusion.refs_1_), channel_id=1, source_target_pairs={{0,6},{1,7},{2,4},{3,5},{4,2},{5,3},{6,0},{7,1},{8,14},{9,15},{10,... | collective-permute-start | bytes 835592 | tf_op jit(solution)/shard_map/ppermute | solution.py:252
  6.6 4.6 %collective-permute-start.4 = (f32[3,512]{1,0:T(4,128)S(1)}, f32[3,512]{1,0:T(4,128)S(1)}, u32[]{:S(2)}, u32[]{:S(2)}) collective-permute-start(f32[3,512]{1,0:T(4,128)S(1)} %maximum_select_fusion.1.refs_2_), channel_id=1, source_target_pairs={{0,8},{1,9},{2,10},{3,11},{4,12},{5,13},{6,14},{7,15},{8,0},{9,1},... | collective-permute-start | bytes 18440 | tf_op jit(solution)/shard_map/ppermute | solution.py:252
  8.7 5.7 %collective-permute-start.5 = (f32[3,512]{1,0:T(4,128)S(1)}, f32[3,512]{1,0:T(4,128)S(1)}, u32[]{:S(2)}, u32[]{:S(2)}) collective-permute-start(f32[3,512]{1,0:T(4,128)S(1)} %maximum_select_fusion.1.refs_2_), channel_id=1, source_target_pairs={{0,16},{1,17},{2,18},{3,19},{4,20},{5,21},{6,22},{7,23},{8,24},{9,... | collective-permute-start | bytes 18440 | tf_op jit(solution)/shard_map/ppermute | solution.py:252
  11.3 5.4 %collective-permute-start.6 = (f32[3,512]{1,0:T(4,128)S(1)}, f32[3,512]{1,0:T(4,128)S(1)}, u32[]{:S(2)}, u32[]{:S(2)}) collective-permute-start(f32[3,512]{1,0:T(4,128)S(1)} %maximum_select_fusion.1.refs_2_), channel_id=1, source_target_pairs={{0,24},{1,25},{2,26},{3,27},{4,28},{5,29},{6,30},{7,31},{8,16},{9,... | collective-permute-start | bytes 18440 | tf_op jit(solution)/shard_map/ppermute | solution.py:252
  19.6 6.6 %collective-permute-start.9 = (f32[3,768]{1,0:T(4,128)S(1)}, f32[3,768]{1,0:T(4,128)S(1)}, u32[]{:S(2)}, u32[]{:S(2)}) collective-permute-start(f32[3,768]{1,0:T(4,128)S(1)} %pad_maximum_fusion.2), channel_id=1, source_target_pairs={{0,1},{1,0},{2,3},{3,2},{4,5},{5,4},{6,7},{7,6},{8,9},{9,8},{10,11... | collective-permute-start | bytes 27656 | tf_op jit(solution)/shard_map/ppermute | solution.py:323
  23.4 5.2 %collective-permute-start.8 = (f32[64,1024]{1,0:T(8,128)S(1)}, f32[64,1024]{1,0:T(8,128)S(1)}, u32[]{:S(2)}, u32[]{:S(2)}) collective-permute-start(f32[64,1024]{1,0:T(8,128)S(1)} %get-tuple-element.34.refs_6_), channel_id=1, source_target_pairs={{0,1},{1,0},{2,3},{3,2},{4,5},{5,4},{6,7},{7,6},{8,9},{9,8},{10,11... | collective-permute-start | bytes 786440 | tf_op jit(solution)/shard_map/ppermute | solution.py:335
  26.1 1.4 %collective-permute-start.7 = (f32[64,512]{1,0:T(8,128)S(1)}, f32[64,512]{1,0:T(8,128)S(1)}, u32[]{:S(2)}, u32[]{:S(2)}) collective-permute-start(f32[64,512]{1,0:T(8,128)S(1)} %get-tuple-element.36), channel_id=1, source_target_pairs={{0,1},{1,0},{2,3},{3,2},{4,5},{5,4},{6,7},{7,6},{8,9},{9,8},{10,11... | collective-permute-start | bytes 393224 | tf_op jit(solution)/shard_map/ppermute | solution.py:335
  27.6 13.7 %collective-permute-start.12 = (f32[64,512]{1,0:T(8,128)S(1)}, f32[64,512]{1,0:T(8,128)S(1)}, u32[]{:S(2)}, u32[]{:S(2)}) collective-permute-start(f32[64,512]{1,0:T(8,128)S(1)} %add.65.refs_6_), channel_id=1, source_target_pairs={{0,8},{1,9},{2,10},{3,11},{4,12},{5,13},{6,14},{7,15},{8,0},{9,1},... | collective-permute-start | bytes 393224 | tf_op jit(solution)/shard_map/ppermute | solution.py:252
  28.6 13.0 %collective-permute-start.13 = (f32[64,512]{1,0:T(8,128)S(1)}, f32[64,512]{1,0:T(8,128)S(1)}, u32[]{:S(2)}, u32[]{:S(2)}) collective-permute-start(f32[64,512]{1,0:T(8,128)S(1)} %get-tuple-element.57.refs_7_), channel_id=1, source_target_pairs={{0,16},{1,17},{2,18},{3,19},{4,20},{5,21},{6,22},{7,23},{8,24},{9,... | collective-permute-start | bytes 393224 | tf_op jit(solution)/shard_map/ppermute | solution.py:252
  31.4 10.2 %collective-permute-start.14 = (f32[64,512]{1,0:T(8,128)S(1)}, f32[64,512]{1,0:T(8,128)S(1)}, u32[]{:S(2)}, u32[]{:S(2)}) collective-permute-start(f32[64,512]{1,0:T(8,128)S(1)} %get-tuple-element.58.refs_8_), channel_id=1, source_target_pairs={{0,24},{1,25},{2,26},{3,27},{4,28},{5,29},{6,30},{7,31},{8,16},{9,... | collective-permute-start | bytes 393224 | tf_op jit(solution)/shard_map/ppermute | solution.py:252
  34.3 6.9 %collective-permute-start.10 = (f32[32,512]{1,0:T(8,128)S(1)}, f32[32,512]{1,0:T(8,128)S(1)}, u32[]{:S(2)}, u32[]{:S(2)}) collective-permute-start(f32[32,512]{1,0:T(8,128)S(1)} %get-tuple-element.61), channel_id=1, source_target_pairs={{0,1},{1,0},{2,3},{3,2},{4,5},{5,4},{6,7},{7,6},{8,9},{9,8},{10,11... | collective-permute-start | bytes 196616 | tf_op jit(solution)/shard_map/ppermute | solution.py:335
  34.4 6.9 %collective-permute-start.11 = (f32[32,512]{1,0:T(8,128)S(1)}, f32[32,512]{1,0:T(8,128)S(1)}, u32[]{:S(2)}, u32[]{:S(2)}) collective-permute-start(f32[32,512]{1,0:T(8,128)S(1)} %get-tuple-element.62), channel_id=1, source_target_pairs={{0,1},{1,0},{2,3},{3,2},{4,5},{5,4},{6,7},{7,6},{8,9},{9,8},{10,11... | collective-permute-start | bytes 196616 | tf_op jit(solution)/shard_map/ppermute | solution.py:335
  41.6 6.7 %collective-permute-start.16 = (f32[64,512]{1,0:T(8,128)S(1)}, f32[64,512]{1,0:T(8,128)S(1)}, u32[]{:S(2)}, u32[]{:S(2)}) collective-permute-start(f32[64,512]{1,0:T(8,128)S(1)} %fusion.7.refs_0_), channel_id=1, source_target_pairs={{0,2},{1,9},{2,0},{3,11},{4,6},{5,13},{6,4},{7,15},{8,10},{9,1},{1... | collective-permute-start | bytes 393224 | tf_op jit(solution)/shard_map/ppermute | solution.py:252
  43.0 5.4 %collective-permute-start.17 = (f32[64,512]{1,0:T(8,128)S(1)}, f32[64,512]{1,0:T(8,128)S(1)}, u32[]{:S(2)}, u32[]{:S(2)}) collective-permute-start(f32[64,512]{1,0:T(8,128)S(1)} %fusion.7.refs_0_), channel_id=1, source_target_pairs={{0,4},{1,17},{2,6},{3,19},{4,0},{5,21},{6,2},{7,23},{8,12},{9,25},... | collective-permute-start | bytes 393224 | tf_op jit(solution)/shard_map/ppermute | solution.py:252
  44.5 5.9 %collective-permute-start.15 = (f32[64,512]{1,0:T(8,128)S(1)}, f32[64,512]{1,0:T(8,128)S(1)}, u32[]{:S(2)}, u32[]{:S(2)}) collective-permute-start(f32[64,512]{1,0:T(8,128)S(1)} %fusion.7.refs_0_), channel_id=1, source_target_pairs={{0,6},{1,25},{2,4},{3,27},{4,2},{5,29},{6,0},{7,31},{8,14},{9,17},... | collective-permute-start | bytes 393224 | tf_op jit(solution)/shard_map/ppermute | solution.py:252
  50.8 9.3 %collective-permute-start.18 = (f32[72,512]{1,0:T(8,128)S(1)}, f32[72,512]{1,0:T(8,128)S(1)}, u32[]{:S(2)}, u32[]{:S(2)}) collective-permute-start(f32[72,512]{1,0:T(8,128)S(1)} %get-tuple-element.47.refs_4_), channel_id=1, source_target_pairs={{0,16},{1,5},{2,18},{3,7},{4,20},{5,1},{6,22},{7,3},{8,24},{9,13},... | collective-permute-start | bytes 442376 | tf_op jit(solution)/shard_map/ppermute | solution.py:252
  54.9 5.3 %collective-permute-start.19 = (f32[72,512]{1,0:T(8,128)S(1)}, f32[72,512]{1,0:T(8,128)S(1)}, u32[]{:S(2)}, u32[]{:S(2)}) collective-permute-start(f32[72,512]{1,0:T(8,128)S(1)} %get-tuple-element.49), channel_id=1, source_target_pairs={{0,8},{1,3},{2,10},{3,1},{4,12},{5,7},{6,14},{7,5},{8,0},{9,11},{1... | collective-permute-start | bytes 442376 | tf_op jit(solution)/shard_map/ppermute | solution.py:252
  55.0 7.3 %collective-permute-start.20 = (f32[72,512]{1,0:T(8,128)S(1)}, f32[72,512]{1,0:T(8,128)S(1)}, u32[]{:S(2)}, u32[]{:S(2)}) collective-permute-start(f32[72,512]{1,0:T(8,128)S(1)} %get-tuple-element.50), channel_id=1, source_target_pairs={{0,24},{1,7},{2,26},{3,5},{4,28},{5,3},{6,30},{7,1},{8,16},{9,15},... | collective-permute-start | bytes 442376 | tf_op jit(solution)/shard_map/ppermute | solution.py:252
  62.4 5.0 %collective-permute-start.22 = (f32[64,512]{1,0:T(8,128)S(1)}, f32[64,512]{1,0:T(8,128)S(1)}, u32[]{:S(2)}, u32[]{:S(2)}) collective-permute-start(f32[64,512]{1,0:T(8,128)S(1)} %fusion.3.refs_0_), channel_id=1, source_target_pairs={{0,2},{1,9},{2,0},{3,11},{4,6},{5,13},{6,4},{7,15},{8,10},{9,1},{1... | collective-permute-start | bytes 393224 | tf_op jit(solution)/shard_map/ppermute | solution.py:252
  63.3 5.0 %collective-permute-start.23 = (f32[64,512]{1,0:T(8,128)S(1)}, f32[64,512]{1,0:T(8,128)S(1)}, u32[]{:S(2)}, u32[]{:S(2)}) collective-permute-start(f32[64,512]{1,0:T(8,128)S(1)} %fusion.3.refs_0_), channel_id=1, source_target_pairs={{0,4},{1,17},{2,6},{3,19},{4,0},{5,21},{6,2},{7,23},{8,12},{9,25},... | collective-permute-start | bytes 393224 | tf_op jit(solution)/shard_map/ppermute | solution.py:252
  64.8 5.9 %collective-permute-start.21 = (f32[64,512]{1,0:T(8,128)S(1)}, f32[64,512]{1,0:T(8,128)S(1)}, u32[]{:S(2)}, u32[]{:S(2)}) collective-permute-start(f32[64,512]{1,0:T(8,128)S(1)} %fusion.3.refs_0_), channel_id=1, source_target_pairs={{0,6},{1,25},{2,4},{3,27},{4,2},{5,29},{6,0},{7,31},{8,14},{9,17},... | collective-permute-start | bytes 393224 | tf_op jit(solution)/shard_map/ppermute | solution.py:252
  71.2 7.5 %collective-permute-start.24 = (f32[64,512]{1,0:T(8,128)S(1)}, f32[64,512]{1,0:T(8,128)S(1)}, u32[]{:S(2)}, u32[]{:S(2)}) collective-permute-start(f32[64,512]{1,0:T(8,128)S(1)} %get-tuple-element.51.refs_4_), channel_id=1, source_target_pairs={{0,16},{1,5},{2,18},{3,7},{4,20},{5,1},{6,22},{7,3},{8,24},{9,13},... | collective-permute-start | bytes 393224 | tf_op jit(solution)/shard_map/ppermute | solution.py:252
  73.2 5.5 %collective-permute-start.25 = (f32[64,512]{1,0:T(8,128)S(1)}, f32[64,512]{1,0:T(8,128)S(1)}, u32[]{:S(2)}, u32[]{:S(2)}) collective-permute-start(f32[64,512]{1,0:T(8,128)S(1)} %get-tuple-element.53), channel_id=1, source_target_pairs={{0,8},{1,3},{2,10},{3,1},{4,12},{5,7},{6,14},{7,5},{8,0},{9,11},{1... | collective-permute-start | bytes 393224 | tf_op jit(solution)/shard_map/ppermute | solution.py:252
  74.7 6.8 %collective-permute-start.26 = (f32[64,512]{1,0:T(8,128)S(1)}, f32[64,512]{1,0:T(8,128)S(1)}, u32[]{:S(2)}, u32[]{:S(2)}) collective-permute-start(f32[64,512]{1,0:T(8,128)S(1)} %get-tuple-element.54), channel_id=1, source_target_pairs={{0,24},{1,7},{2,26},{3,5},{4,28},{5,3},{6,30},{7,1},{8,16},{9,15},... | collective-permute-start | bytes 393224 | tf_op jit(solution)/shard_map/ppermute | solution.py:252
  81.6 1.3 %collective-permute-start.27 = (f32[64,256]{1,0:T(8,128)S(1)}, f32[64,256]{1,0:T(8,128)S(1)}, u32[]{:S(2)}, u32[]{:S(2)}) collective-permute-start(f32[64,256]{1,0:T(8,128)S(1)} %get-tuple-element.60), channel_id=1, source_target_pairs={{0,1},{1,0},{2,3},{3,2},{4,5},{5,4},{6,7},{7,6},{8,9},{9,8},{10,11... | collective-permute-start | bytes 196616 | tf_op jit(solution)/shard_map/ppermute | solution.py:437

commit v4 on v3

--- a/solution.py
+++ b/solution.py
@@ -276,6 +276,7 @@
     core_of = jnp.reshape(core, (1,)).astype(jnp.int32)
     scalar = [pl.BlockSpec(memory_space=pltpu.SMEM)]
     anywhere = [pl.BlockSpec(memory_space=pl.ANY)]
+
     def pull(which, spans, cols, before, last, skip=0, other=(), weight=1):
         first = before is None
         step = 2 if len(spans) % 2 == 0 else 1
@@ -287,18 +288,18 @@
         inputs = [core_of, *[blocks[k] for k in which]]
         if cols is None:
             first = "features"
-            shapes = [pltpu.VMEM((FEATURES, total_width), BF16)] + shapes
-            inputs += tgt_ctrl
+            shapes = [pltpu.VMEM((FEATURES, len(spans) * width), BF16)] + shapes
+            inputs += [tgt_ctrl[k] for k in spans]
         else:
             inputs.append(pltpu.with_memory_space_constraint(cols, pltpu.VMEM))
         if not first:
             inputs.append(pltpu.with_memory_space_constraint(before, pltpu.VMEM))
         in_specs = scalar + vmem(len(inputs) - 1) + anywhere * len(other)
         inputs += other
-        extra = len(tgt_ctrl) if cols is None else len(other)
+        extra = len(spans) if cols is None else len(other)
         return pl.pallas_call(
             functools.partial(
-                pull_kernel, inverse, full, width, len(which), spans, skip, first, last, extra
+                pull_kernel, inverse, full, width, len(which), [within[k] for k in spans], skip, first, last, extra
             ),
             out_shape=shapes,
             in_specs=in_specs,
@@ -314,12 +315,26 @@
         )(*inputs)
 
     near, far = list(range(peers // 2)), list(range(peers // 2, peers))
-    cols, far_sofar = pull([0], far, None, None, False)
-    (near_sofar,) = pull([0], near, cols, None, False)
+    within = {k: k - half_of[0] for half_of in (near, far) for k in half_of}
+    near_cols, near_sofar = pull([0], near, None, None, False)
+    far_cols, far_sofar = pull([0], far, None, None, False)
     sums = [None] * peers
     arriving = list(range(1, peers))
 
-    theirs = jnp.concatenate([b[full + 3 : full + 6, :owned] for b in blocks[1:]], axis=1)
+    def swapped(other, pieces=1):
+        rows = half // pieces
+        return [lax.ppermute(other[i * rows : (i + 1) * rows], "src", sibling) for i in range(pieces)]
+
+    def added(spans, mine, other):
+        other = jnp.concatenate(other, axis=0)
+        for i, k in enumerate(spans):
+            sums[k] = mine[i] + other[:, i * width : (i + 1) * width]
+
+    if peers > 2:
+        (far_sofar,) = pull(arriving[:1], far, far_cols, far_sofar, False, weight=8 * width)
+    *mine, other = pull(arriving[1:] or arriving, far, far_cols, far_sofar, True, weight=8 * width)
+    late, _ = lax.optimization_barrier((blocks[1:], other))
+    theirs = jnp.concatenate([b[full + 3 : full + 6, :owned] for b in late], axis=1)
     others = lax.ppermute(theirs, "src", sibling)
     src_points = [ctrl]
     for k in range(peers - 1):
@@ -329,21 +344,18 @@
     tgt_points = jnp.concatenate(tgt_ctrl, axis=1)
     row_points = jnp.where(first_core, src_points, tgt_points)
     col_points = jnp.where(first_core, tgt_points, src_points)
-
-    def added(spans, mine, other, pieces=1):
-        rows = half // pieces
-        other = [lax.ppermute(other[i * rows : (i + 1) * rows], "src", sibling) for i in range(pieces)]
-        other = jnp.concatenate(other, axis=0)
-        for i, k in enumerate(spans):
-            sums[k] = mine[i] + other[:, i * width : (i + 1) * width]
-
-    *mine, other = pull(arriving, far, cols, far_sofar, True, weight=8 * width)
-    added(far, mine, other)
+    given = swapped(other)
     if near[1:]:
-        *mine, other = pull(arriving, near[1:], cols, near_sofar, True, width, [other], 4 * width)
-        added(near[1:], mine, other)
-    *mine, other = pull(arriving, near[:1], cols, near_sofar, True, 0, [sums[k] for k in range(1, peers)] + [row_points, col_points])
-    added(near[:1], mine, other, 2)
+        *near_mine, other = pull(arriving, near[1:], near_cols, near_sofar, True, width, [other], 4 * width)
+        near_given = swapped(other)
+    added(far, mine, given)
+    *mine, other = pull(
+        arriving, near[:1], near_cols, near_sofar, True, 0, [sums[k] for k in far]
+    )
+    if near[1:]:
+        near_given, mine, other = lax.optimization_barrier((near_given, mine, other))
+        added(near[1:], near_mine, near_given)
+    added(near[:1], mine, swapped(other, 2))
 
     def summed(values):
         order = [peers // 2] + [k for k in range(1, peers) if k != peers // 2]
@@ -355,6 +367,7 @@
 
     kept = (peers * width) ** 2 * 4 <= KEPT_BYTES
     pullback = sums[0]
+
     def keep(start, count):
         return pl.pallas_call(
             functools.partial(keep_kernel, inverse, start * width),
@@ -394,8 +407,9 @@
             cost_estimate=cost(total_width, half),
         )(*inputs, other)
 
-    for k in range(1, peers):
-        pullback = pullback + exchange(sums[k], along_tgt[k])
+    got = {k: exchange(sums[k], along_tgt[k]) for k in far + near[1:]}
+    for value in got.values():
+        pullback = pullback + value
 
     iterate = pullback
     for sweep in range(STEPS):

time: 83.7 us -> 81 us (0.968)
  waiting for transfers between devices: 19.3 us -> 17.8 us
  starting transfers between devices: 35.1 us -> 33.7 us
    ppermute x21, starting transfers between devices: 33.3 us -> 31.9 us  [exchange(): return lax.ppermute(value, ('tgt', 'src'), pairs)]
    ppermute x4, waiting for transfers between devices: 1.26 us -> 0.01 us  [swapped(): lax.ppermute(other[i * rows:(i + 1) * rows], 'src', sibling)]
    pallas_call x5 -> x6, Pallas kernels: 10.8 us -> 10.9 us  [pull(): pl.pallas_call(functools.partial(pull_kernel, inverse, full, width, len(w...]
  transfers between devices with their start and end apart: 28 -> 28, of which waited for: 12 -> 11; matrix products, arithmetic and copies ran while one was open for 2% -> 3% of each run, Pallas kernels for 30% -> 28%
where the time goes in v4:
time: 81 us; the launch traced here: 80.8 us
  starting transfers between devices  33.7 us (42%)
  Pallas kernels  26 us (32%)
  waiting for transfers between devices  17.8 us (22%)
  other arithmetic  2.83 us (3%)
    ppermute x21, starting transfers between devices, exchange(): return lax.ppermute(value, ('tgt', 'src'), pairs)  31.9 us
    ppermute x21, waiting for transfers between devices, exchange(): return lax.ppermute(value, ('tgt', 'src'), pairs)  16.6 us
    pallas_call x6, Pallas kernels, pull(): pl.pallas_call(functools.partial(pull_kernel, inverse, full, width, len(w...  10.9 us
    pallas_call x2, Pallas kernels, keep(): pl.pallas_call(functools.partial(keep_kernel, inverse, start * width), ou...  8.7 us
    pallas_call x8, Pallas kernels, step(): pl.pallas_call(functools.partial(step_kernel, half, start, len(these), sp...  6.4 us
  transfers between devices with their start and end apart: 28, of which 11 were waited for; matrix products, arithmetic and copies ran while one was open for 3% of the time, Pallas kernels for 28%

profile of v4, /device:TPU:0, one launch (start us, length us, event | category | flops | bytes accessed | tf_op | source)
XLA Modules:
  0.0 80.8 jit_solution(2035999836302280756)
XLA Ops:
  0.0 0.5 collective-permute-start
  0.5 0.1 pad.41.clone
  0.5 1.1 %fusion.refs_1_ = f32[136,512]{1,0:T(8,128)S(1)} fusion(f32[3,256]{1,0:T(4,128)} %param.5, f32[3,512]{1,0:T(4,128)} %param.4, f32[128,512]{1,0:T(8,128)} %param.3, f32[136]{0:T(256)S(1)} %pad.41.clone), kind=kLoop, calls=%fused_computation.3 | loop fusion | flops 487424 | bytes 550432 | tf_op jit(solution)/shard_map/concatenate | solution.py:259
  1.6 2.7 %collective-permute-start.1 = (f32[136,512]{1,0:T(8,128)S(1)}, f32[136,512]{1,0:T(8,128)S(1)}, u32[]{:S(2)}, u32[]{:S(2)}) collective-permute-start(f32[136,512]{1,0:T(8,128)S(1)} %fusion.refs_1_), channel_id=1, source_target_pairs={{0,2},{1,3},{2,0},{3,1},{4,6},{5,7},{6,4},{7,5},{8,10},{9,11},{10,... | collective-permute-start | bytes 835592 | tf_op jit(solution)/shard_map/ppermute | solution.py:252
  4.3 1.5 %collective-permute-start.2 = (f32[136,512]{1,0:T(8,128)S(1)}, f32[136,512]{1,0:T(8,128)S(1)}, u32[]{:S(2)}, u32[]{:S(2)}) collective-permute-start(f32[136,512]{1,0:T(8,128)S(1)} %fusion.refs_1_), channel_id=1, source_target_pairs={{0,4},{1,5},{2,6},{3,7},{4,0},{5,1},{6,2},{7,3},{8,12},{9,13},{10,... | collective-permute-start | bytes 835592 | tf_op jit(solution)/shard_map/ppermute | solution.py:252
  5.9 0.8 maximum_select_fusion.1.refs_2_
  6.6 2.1 %collective-permute-start.4 = (f32[3,512]{1,0:T(4,128)S(1)}, f32[3,512]{1,0:T(4,128)S(1)}, u32[]{:S(2)}, u32[]{:S(2)}) collective-permute-start(f32[3,512]{1,0:T(4,128)S(1)} %maximum_select_fusion.1.refs_2_), channel_id=1, source_target_pairs={{0,8},{1,9},{2,10},{3,11},{4,12},{5,13},{6,14},{7,15},{8,0},{9,1},... | collective-permute-start | bytes 18440 | tf_op jit(solution)/shard_map/ppermute | solution.py:252
  8.7 2.6 %collective-permute-start.5 = (f32[3,512]{1,0:T(4,128)S(1)}, f32[3,512]{1,0:T(4,128)S(1)}, u32[]{:S(2)}, u32[]{:S(2)}) collective-permute-start(f32[3,512]{1,0:T(4,128)S(1)} %maximum_select_fusion.1.refs_2_), channel_id=1, source_target_pairs={{0,16},{1,17},{2,18},{3,19},{4,20},{5,21},{6,22},{7,23},{8,24},{9,... | collective-permute-start | bytes 18440 | tf_op jit(solution)/shard_map/ppermute | solution.py:252
  11.3 0.0 collective-permute-done.4.refs_3_
  11.3 3.1 %collective-permute-start.6 = (f32[3,512]{1,0:T(4,128)S(1)}, f32[3,512]{1,0:T(4,128)S(1)}, u32[]{:S(2)}, u32[]{:S(2)}) collective-permute-start(f32[3,512]{1,0:T(4,128)S(1)} %maximum_select_fusion.1.refs_2_), channel_id=1, source_target_pairs={{0,24},{1,25},{2,26},{3,27},{4,28},{5,29},{6,30},{7,31},{8,16},{9,... | collective-permute-start | bytes 18440 | tf_op jit(solution)/shard_map/ppermute | solution.py:252
  14.4 1.4 %shard_map.37 = (bf16[32,1024]{1,0:T(8,128)(2,1)S(1)}, f32[128,1024]{1,0:T(8,128)S(1)}) custom-call(s32[1]{0:T(128)} %bitcast.refs_0_, f32[136,512]{1,0:T(8,128)S(1)} %fusion.refs_1_, f32[3,512]{1,0:T(4,128)S(1)} %maximum_select_fusion.1.refs_2_, f32[3,512]{1,0:T(4,128)S(1)} %collective-permute-done.4.refs_3_), custom_call_target="tpu_custom_call" | custom-call | flops 65536 | bytes 128 | tf_op jit(solution)/shard_map/pallas_call | solution.py:300
  15.7 0.0 collective-permute-done.5.refs_2_
  15.7 1.0 %collective-permute-done.6.refs_3_ = f32[3,512]{1,0:T(4,128)S(1)} collective-permute-done((f32[3,512]{1,0:T(4,128)S(1)}, f32[3,512]{1,0:T(4,128)S(1)}, u32[]{:S(2)}, u32[]{:S(2)}) %collective-permute-start.6) | collective-permute-done | bytes 6176 | tf_op jit(solution)/shard_map/ppermute | solution.py:252
  16.7 1.4 %shard_map.38 = (bf16[32,1024]{1,0:T(8,128)(2,1)S(1)}, f32[128,1024]{1,0:T(8,128)S(1)}) custom-call(s32[1]{0:T(128)} %bitcast.refs_0_, f32[136,512]{1,0:T(8,128)S(1)} %fusion.refs_1_, f32[3,512]{1,0:T(4,128)S(1)} %collective-permute-done.5.refs_2_, f32[3,512]{1,0:T(4,128)S(1)} %collective-permute-done.6.refs_3_), custom_call_target="tpu_custom_call" | custom-call | flops 65536 | bytes 128 | tf_op jit(solution)/shard_map/pallas_call | solution.py:300
  18.1 0.0 collective-permute-done.1.refs_1_
  18.1 1.4 %shard_map.39.refs_4_ = f32[128,1024]{1,0:T(8,128)S(1)} custom-call(s32[1]{0:T(128)} %bitcast.refs_0_, f32[136,512]{1,0:T(8,128)S(1)} %collective-permute-done.1.refs_1_, bf16[32,1024]{1,0:T(8,128)(2,1)S(1)} %get-tuple-element.42.refs_2_.refs_3_, f32[128,1024]{1,0:T(8,128)S(1)} %get-tuple-element.43.refs_3_), custom_call_target="tpu_custom_call" | custom-call | flops 268435456 | bytes 128 | tf_op jit(solution)/shard_map/pallas_call | solution.py:300
  19.5 0.0 collective-permute-done.3.refs_2_.refs_3_
  19.5 2.5 %shard_map.40 = (f32[64,512]{1,0:T(8,128)S(1)}, f32[64,512]{1,0:T(8,128)S(1)}, f32[64,1024]{1,0:T(8,128)S(1)}) custom-call(s32[1]{0:T(128)} %bitcast.refs_0_, f32[136,512]{1,0:T(8,128)S(1)} %collective-permute-done.2.refs_1_.refs_2_, f32[136,512]{1,0:T(8,128)S(1)} %collective-permute-done.3.refs_2_.refs_3_, ...), custom_call_target="tpu_custom_call" | custom-call | flops 536870912 | bytes 128 | tf_op jit(solution)/shard_map/pallas_call | solution.py:300
  22.0 0.1 collective-permute-start.8
  22.1 0.5 collective-permute-start.11
  22.7 2.2 %shard_map.41 = (f32[64,512]{1,0:T(8,128)S(1)}, f32[64,512]{1,0:T(8,128)S(1)}) custom-call(s32[1]{0:T(128)} %bitcast.refs_0_, f32[136,512]{1,0:T(8,128)S(1)} %collective-permute-done.1.refs_1_, f32[136,512]{1,0:T(8,128)S(1)} %collective-permute-done.2.refs_1_.refs_2_, f32[136,512]{1,0:T(8,128)S(1)} %collective-permute-done.3.refs_2_.refs_3_, ...), custom_call_target="tpu_custom_call" | custom-call | flops 402653184 | bytes 128 | tf_op jit(solution)/shard_map/pallas_call | solution.py:300
  24.8 0.1 collective-permute-start.7
  25.0 2.1 %collective-permute-start.12 = (f32[64,512]{1,0:T(8,128)S(1)}, f32[64,512]{1,0:T(8,128)S(1)}, u32[]{:S(2)}, u32[]{:S(2)}) collective-permute-start(f32[64,512]{1,0:T(8,128)S(1)} %get-tuple-element.74.refs_6_), channel_id=1, source_target_pairs={{0,16},{1,17},{2,18},{3,19},{4,20},{5,21},{6,22},{7,23},{8,24},{9,... | collective-permute-start | bytes 393224 | tf_op jit(solution)/shard_map/ppermute | solution.py:252
  27.1 1.4 %collective-permute-start.13 = (f32[64,512]{1,0:T(8,128)S(1)}, f32[64,512]{1,0:T(8,128)S(1)}, u32[]{:S(2)}, u32[]{:S(2)}) collective-permute-start(f32[64,512]{1,0:T(8,128)S(1)} %get-tuple-element.73.refs_7_), channel_id=1, source_target_pairs={{0,24},{1,25},{2,26},{3,27},{4,28},{5,29},{6,30},{7,31},{8,16},{9,... | collective-permute-start | bytes 393224 | tf_op jit(solution)/shard_map/ppermute | solution.py:252
  28.5 2.2 %shard_map.42 = (f32[64,512]{1,0:T(8,128)S(1)}, f32[64,512]{1,0:T(8,128)S(1)}) custom-call(s32[1]{0:T(128)} %bitcast.refs_0_, f32[136,512]{1,0:T(8,128)S(1)} %collective-permute-done.1.refs_1_, f32[136,512]{1,0:T(8,128)S(1)} %collective-permute-done.2.refs_1_.refs_2_, f32[136,512]{1,0:T(8,128)S(1)} %collective-permute-done.3.refs_2_.refs_3_, ...), custom_call_target="tpu_custom_call" | custom-call | flops 196608 | bytes 128 | tf_op jit(solution)/shard_map/pallas_call | solution.py:300
  30.7 0.4 collective-permute-start.14
  31.1 0.1 collective-permute-start.10
  31.1 0.5 collective-permute-start.9
  31.6 6.3 %shard_map.43 = (bf16[1536,2048]{1,0:T(8,128)(2,1)S(1)}, bf16[1536,2048]{1,0:T(8,128)(2,1)S(1)}, f32[1,512]{1,0:T(1,128)S(1)}) custom-call(f32[3,2048]{1,0:T(4,128)S(1)} %get-tuple-element.80.row_points, f32[3,2048]{1,0:T(4,128)S(1)} %get-tuple-element.79.col_points), custom_call_target="tpu_custom_call" | custom-call | flops 131072 | bytes 64 | tf_op jit(solution)/shard_map/pallas_call | solution.py:372
  38.0 2.3 %collective-permute-done.14 = f32[64,512]{1,0:T(8,128)S(1)} collective-permute-done((f32[64,512]{1,0:T(8,128)S(1)}, f32[64,512]{1,0:T(8,128)S(1)}, u32[]{:S(2)}, u32[]{:S(2)}) %collective-permute-start.14) | collective-permute-done | bytes 131104 | tf_op jit(solution)/shard_map/ppermute | solution.py:252
  40.3 0.1 fusion.7.refs_0_
  40.4 1.6 %collective-permute-start.16 = (f32[64,512]{1,0:T(8,128)S(1)}, f32[64,512]{1,0:T(8,128)S(1)}, u32[]{:S(2)}, u32[]{:S(2)}) collective-permute-start(f32[64,512]{1,0:T(8,128)S(1)} %fusion.7.refs_0_), channel_id=1, source_target_pairs={{0,2},{1,9},{2,0},{3,11},{4,6},{5,13},{6,4},{7,15},{8,10},{9,1},{1... | collective-permute-start | bytes 393224 | tf_op jit(solution)/shard_map/ppermute | solution.py:252
  41.9 1.5 %collective-permute-start.17 = (f32[64,512]{1,0:T(8,128)S(1)}, f32[64,512]{1,0:T(8,128)S(1)}, u32[]{:S(2)}, u32[]{:S(2)}) collective-permute-start(f32[64,512]{1,0:T(8,128)S(1)} %fusion.7.refs_0_), channel_id=1, source_target_pairs={{0,4},{1,17},{2,6},{3,19},{4,0},{5,21},{6,2},{7,23},{8,12},{9,25},... | collective-permute-start | bytes 393224 | tf_op jit(solution)/shard_map/ppermute | solution.py:252
  43.4 0.5 collective-permute-start.15
  43.9 2.4 %shard_map.44 = (bf16[512,2048]{1,0:T(8,128)(2,1)S(1)}, bf16[512,2048]{1,0:T(8,128)(2,1)S(1)}, f32[1,512]{1,0:T(1,128)S(1)}) custom-call(f32[3,2048]{1,0:T(4,128)S(1)} %get-tuple-element.80.row_points, f32[3,2048]{1,0:T(4,128)S(1)} %get-tuple-element.79.col_points), custom_call_target="tpu_custom_call" | custom-call | flops 131072 | bytes 64 | tf_op jit(solution)/shard_map/pallas_call | solution.py:372
  46.3 0.8 %shard_map.45.refs_4_ = f32[72,2048]{1,0:T(8,128)S(1)} custom-call(f32[64,512]{1,0:T(8,128)S(1)} %fusion.7.refs_0_, bf16[1536,2048]{1,0:T(8,128)(2,1)S(1)} %get-tuple-element.60.refs_1_.refs_2_, bf16[1536,2048]{1,0:T(8,128)(2,1)S(1)} %get-tuple-element.61.refs_2_.refs_3_, f32[1,512]{1,0:T(1,128)S(1)} %get-tuple-element.62.refs_3_.refs_5_.refs_4_), custom_call_target="tpu_custom_call" | custom-call | flops 131072 | bytes 64 | tf_op jit(solution)/shard_map/pallas_call | solution.py:398
  47.1 1.5 %shard_map.46.refs_3_ = f32[72,2048]{1,0:T(8,128)S(1)} custom-call(f32[64,512]{1,0:T(8,128)S(1)} %collective-permute-done.16.refs_0_, f32[64,512]{1,0:T(8,128)S(1)} %collective-permute-done.17.refs_1_, bf16[1536,2048]{1,0:T(8,128)(2,1)S(1)} %get-tuple-element.60.refs_1_.refs_2_, bf16[1536,2048]{1,0:T(8,128)(2,1)S(1)} %get-tuple-element.61.refs_2_.refs_3_, ...), custom_call_target="tpu_custom_call" | custom-call | flops 131072 | bytes 64 | tf_op jit(solution)/shard_map/pallas_call | solution.py:398
  48.7 0.7 collective-permute-done.15.refs_0_
  49.3 0.5 shard_map.47
  49.8 1.5 %collective-permute-start.18 = (f32[72,512]{1,0:T(8,128)S(1)}, f32[72,512]{1,0:T(8,128)S(1)}, u32[]{:S(2)}, u32[]{:S(2)}) collective-permute-start(f32[72,512]{1,0:T(8,128)S(1)} %get-tuple-element.63.refs_4_), channel_id=1, source_target_pairs={{0,16},{1,5},{2,18},{3,7},{4,20},{5,1},{6,22},{7,3},{8,24},{9,13},... | collective-permute-start | bytes 442376 | tf_op jit(solution)/shard_map/ppermute | solution.py:252
  51.3 0.5 shard_map.48
  51.7 1.5 %collective-permute-start.19 = (f32[72,512]{1,0:T(8,128)S(1)}, f32[72,512]{1,0:T(8,128)S(1)}, u32[]{:S(2)}, u32[]{:S(2)}) collective-permute-start(f32[72,512]{1,0:T(8,128)S(1)} %get-tuple-element.65), channel_id=1, source_target_pairs={{0,8},{1,3},{2,10},{3,1},{4,12},{5,7},{6,14},{7,5},{8,0},{9,11},{1... | collective-permute-start | bytes 442376 | tf_op jit(solution)/shard_map/ppermute | solution.py:252
  53.2 1.5 %collective-permute-start.20 = (f32[72,512]{1,0:T(8,128)S(1)}, f32[72,512]{1,0:T(8,128)S(1)}, u32[]{:S(2)}, u32[]{:S(2)}) collective-permute-start(f32[72,512]{1,0:T(8,128)S(1)} %get-tuple-element.66), channel_id=1, source_target_pairs={{0,24},{1,7},{2,26},{3,5},{4,28},{5,3},{6,30},{7,1},{8,16},{9,15},... | collective-permute-start | bytes 442376 | tf_op jit(solution)/shard_map/ppermute | solution.py:252
  54.8 3.6 %collective-permute-done.19 = f32[72,512]{1,0:T(8,128)S(1)} collective-permute-done((f32[72,512]{1,0:T(8,128)S(1)}, f32[72,512]{1,0:T(8,128)S(1)}, u32[]{:S(2)}, u32[]{:S(2)}) %collective-permute-start.19) | collective-permute-done | bytes 147488 | tf_op jit(solution)/shard_map/ppermute | solution.py:252
  58.4 1.9 %collective-permute-done.20 = f32[72,512]{1,0:T(8,128)S(1)} collective-permute-done((f32[72,512]{1,0:T(8,128)S(1)}, f32[72,512]{1,0:T(8,128)S(1)}, u32[]{:S(2)}, u32[]{:S(2)}) %collective-permute-start.20) | collective-permute-done | bytes 147488 | tf_op jit(solution)/shard_map/ppermute | solution.py:252
  60.4 1.3 %collective-permute-start.22 = (f32[64,512]{1,0:T(8,128)S(1)}, f32[64,512]{1,0:T(8,128)S(1)}, u32[]{:S(2)}, u32[]{:S(2)}) collective-permute-start(f32[64,512]{1,0:T(8,128)S(1)} %fusion.3.refs_0_), channel_id=1, source_target_pairs={{0,2},{1,9},{2,0},{3,11},{4,6},{5,13},{6,4},{7,15},{8,10},{9,1},{1... | collective-permute-start | bytes 393224 | tf_op jit(solution)/shard_map/ppermute | solution.py:252
  61.7 0.8 %collective-permute-start.23 = (f32[64,512]{1,0:T(8,128)S(1)}, f32[64,512]{1,0:T(8,128)S(1)}, u32[]{:S(2)}, u32[]{:S(2)}) collective-permute-start(f32[64,512]{1,0:T(8,128)S(1)} %fusion.3.refs_0_), channel_id=1, source_target_pairs={{0,4},{1,17},{2,6},{3,19},{4,0},{5,21},{6,2},{7,23},{8,12},{9,25},... | collective-permute-start | bytes 393224 | tf_op jit(solution)/shard_map/ppermute | solution.py:252
  62.5 1.4 %collective-permute-start.21 = (f32[64,512]{1,0:T(8,128)S(1)}, f32[64,512]{1,0:T(8,128)S(1)}, u32[]{:S(2)}, u32[]{:S(2)}) collective-permute-start(f32[64,512]{1,0:T(8,128)S(1)} %fusion.3.refs_0_), channel_id=1, source_target_pairs={{0,6},{1,25},{2,4},{3,27},{4,2},{5,29},{6,0},{7,31},{8,14},{9,17},... | collective-permute-start | bytes 393224 | tf_op jit(solution)/shard_map/ppermute | solution.py:252
  64.0 0.8 shard_map.49.refs_4_
  64.7 0.7 collective-permute-done.22.refs_0_
  65.4 1.2 %collective-permute-done.23.refs_1_ = f32[64,512]{1,0:T(8,128)S(1)} collective-permute-done((f32[64,512]{1,0:T(8,128)S(1)}, f32[64,512]{1,0:T(8,128)S(1)}, u32[]{:S(2)}, u32[]{:S(2)}) %collective-permute-start.23) | collective-permute-done | bytes 131104 | tf_op jit(solution)/shard_map/ppermute | solution.py:252
  66.7 1.4 %shard_map.50.refs_3_ = f32[64,2048]{1,0:T(8,128)S(1)} custom-call(f32[64,512]{1,0:T(8,128)S(1)} %collective-permute-done.22.refs_0_, f32[64,512]{1,0:T(8,128)S(1)} %collective-permute-done.23.refs_1_, bf16[1536,2048]{1,0:T(8,128)(2,1)S(1)} %get-tuple-element.60.refs_1_.refs_2_, bf16[1536,2048]{1,0:T(8,128)(2,1)S(1)} %get-tuple-element.61.refs_2_.refs_3_, ...), custom_call_target="tpu_custom_call" | custom-call | flops 131072 | bytes 64 | tf_op jit(solution)/shard_map/pallas_call | solution.py:398
  68.1 0.3 collective-permute-done.21.refs_0_
  68.4 0.4 shard_map.51
  68.8 1.9 %collective-permute-start.24 = (f32[64,512]{1,0:T(8,128)S(1)}, f32[64,512]{1,0:T(8,128)S(1)}, u32[]{:S(2)}, u32[]{:S(2)}) collective-permute-start(f32[64,512]{1,0:T(8,128)S(1)} %get-tuple-element.67.refs_4_), channel_id=1, source_target_pairs={{0,16},{1,5},{2,18},{3,7},{4,20},{5,1},{6,22},{7,3},{8,24},{9,13},... | collective-permute-start | bytes 393224 | tf_op jit(solution)/shard_map/ppermute | solution.py:252
  70.7 0.4 shard_map.52
  71.2 0.7 collective-permute-start.25
  71.9 2.0 %collective-permute-start.26 = (f32[64,512]{1,0:T(8,128)S(1)}, f32[64,512]{1,0:T(8,128)S(1)}, u32[]{:S(2)}, u32[]{:S(2)}) collective-permute-start(f32[64,512]{1,0:T(8,128)S(1)} %get-tuple-element.70), channel_id=1, source_target_pairs={{0,24},{1,7},{2,26},{3,5},{4,28},{5,3},{6,30},{7,1},{8,16},{9,15},... | collective-permute-start | bytes 393224 | tf_op jit(solution)/shard_map/ppermute | solution.py:252
  73.8 3.0 %collective-permute-done.25 = f32[64,512]{1,0:T(8,128)S(1)} collective-permute-done((f32[64,512]{1,0:T(8,128)S(1)}, f32[64,512]{1,0:T(8,128)S(1)}, u32[]{:S(2)}, u32[]{:S(2)}) %collective-permute-start.25) | collective-permute-done | bytes 131104 | tf_op jit(solution)/shard_map/ppermute | solution.py:252
  76.8 1.9 %collective-permute-done.26 = f32[64,512]{1,0:T(8,128)S(1)} collective-permute-done((f32[64,512]{1,0:T(8,128)S(1)}, f32[64,512]{1,0:T(8,128)S(1)}, u32[]{:S(2)}, u32[]{:S(2)}) %collective-permute-start.26) | collective-permute-done | bytes 131104 | tf_op jit(solution)/shard_map/ppermute | solution.py:252
  78.7 0.1 multiply_add_fusion
  78.8 0.1 collective-permute-start.27
  78.9 1.2 %collective-permute-done.27 = f32[64,256]{1,0:T(8,128)S(1)} collective-permute-done((f32[64,256]{1,0:T(8,128)S(1)}, f32[64,256]{1,0:T(8,128)S(1)}, u32[]{:S(2)}, u32[]{:S(2)}) %collective-permute-start.27) | collective-permute-done | bytes 65568 | tf_op jit(solution)/shard_map/ppermute | solution.py:451
  80.2 0.7 maximum_select_fusion
  (31 shorter events, 0.3 us)
Async XLA Ops:
  0.0 1.6 %collective-permute-start = (f32[3,256]{1,0:T(4,128)}, f32[3,256]{1,0:T(4,128)S(1)}, u32[]{:S(2)}, u32[]{:S(2)}) collective-permute-start(f32[3,256]{1,0:T(4,128)} %param.5), channel_id=1, source_target_pairs={{0,1},{1,0},{2,3},{3,2},{4,5},{5,4},{6,7},{7,6},{8,9},{9,8},{10,11... | collective-permute-start | bytes 9224 | tf_op jit(solution)/shard_map/ppermute | solution.py:268
  1.6 16.5 %collective-permute-start.1 = (f32[136,512]{1,0:T(8,128)S(1)}, f32[136,512]{1,0:T(8,128)S(1)}, u32[]{:S(2)}, u32[]{:S(2)}) collective-permute-start(f32[136,512]{1,0:T(8,128)S(1)} %fusion.refs_1_), channel_id=1, source_target_pairs={{0,2},{1,3},{2,0},{3,1},{4,6},{5,7},{6,4},{7,5},{8,10},{9,11},{10,... | collective-permute-start | bytes 835592 | tf_op jit(solution)/shard_map/ppermute | solution.py:252
  4.3 15.2 %collective-permute-start.2 = (f32[136,512]{1,0:T(8,128)S(1)}, f32[136,512]{1,0:T(8,128)S(1)}, u32[]{:S(2)}, u32[]{:S(2)}) collective-permute-start(f32[136,512]{1,0:T(8,128)S(1)} %fusion.refs_1_), channel_id=1, source_target_pairs={{0,4},{1,5},{2,6},{3,7},{4,0},{5,1},{6,2},{7,3},{8,12},{9,13},{10,... | collective-permute-start | bytes 835592 | tf_op jit(solution)/shard_map/ppermute | solution.py:252
  5.9 13.6 %collective-permute-start.3 = (f32[136,512]{1,0:T(8,128)S(1)}, f32[136,512]{1,0:T(8,128)S(1)}, u32[]{:S(2)}, u32[]{:S(2)}) collective-permute-start(f32[136,512]{1,0:T(8,128)S(1)} %fusion.refs_1_), channel_id=1, source_target_pairs={{0,6},{1,7},{2,4},{3,5},{4,2},{5,3},{6,0},{7,1},{8,14},{9,15},{10,... | collective-permute-start | bytes 835592 | tf_op jit(solution)/shard_map/ppermute | solution.py:252
  6.6 4.6 %collective-permute-start.4 = (f32[3,512]{1,0:T(4,128)S(1)}, f32[3,512]{1,0:T(4,128)S(1)}, u32[]{:S(2)}, u32[]{:S(2)}) collective-permute-start(f32[3,512]{1,0:T(4,128)S(1)} %maximum_select_fusion.1.refs_2_), channel_id=1, source_target_pairs={{0,8},{1,9},{2,10},{3,11},{4,12},{5,13},{6,14},{7,15},{8,0},{9,1},... | collective-permute-start | bytes 18440 | tf_op jit(solution)/shard_map/ppermute | solution.py:252
  8.7 7.1 %collective-permute-start.5 = (f32[3,512]{1,0:T(4,128)S(1)}, f32[3,512]{1,0:T(4,128)S(1)}, u32[]{:S(2)}, u32[]{:S(2)}) collective-permute-start(f32[3,512]{1,0:T(4,128)S(1)} %maximum_select_fusion.1.refs_2_), channel_id=1, source_target_pairs={{0,16},{1,17},{2,18},{3,19},{4,20},{5,21},{6,22},{7,23},{8,24},{9,... | collective-permute-start | bytes 18440 | tf_op jit(solution)/shard_map/ppermute | solution.py:252
  11.3 5.4 %collective-permute-start.6 = (f32[3,512]{1,0:T(4,128)S(1)}, f32[3,512]{1,0:T(4,128)S(1)}, u32[]{:S(2)}, u32[]{:S(2)}) collective-permute-start(f32[3,512]{1,0:T(4,128)S(1)} %maximum_select_fusion.1.refs_2_), channel_id=1, source_target_pairs={{0,24},{1,25},{2,26},{3,27},{4,28},{5,29},{6,30},{7,31},{8,16},{9,... | collective-permute-start | bytes 18440 | tf_op jit(solution)/shard_map/ppermute | solution.py:252
  22.0 3.0 %collective-permute-start.8 = (f32[64,1024]{1,0:T(8,128)S(1)}, f32[64,1024]{1,0:T(8,128)S(1)}, u32[]{:S(2)}, u32[]{:S(2)}) collective-permute-start(f32[64,1024]{1,0:T(8,128)S(1)} %get-tuple-element.44.refs_6_), channel_id=1, source_target_pairs={{0,1},{1,0},{2,3},{3,2},{4,5},{5,4},{6,7},{7,6},{8,9},{9,8},{10,11... | collective-permute-start | bytes 786440 | tf_op jit(solution)/shard_map/ppermute | solution.py:326
  22.1 2.8 %collective-permute-start.11 = (f32[3,768]{1,0:T(4,128)S(1)}, f32[3,768]{1,0:T(4,128)S(1)}, u32[]{:S(2)}, u32[]{:S(2)}) collective-permute-start(f32[3,768]{1,0:T(4,128)S(1)} %pad_maximum_fusion.2), channel_id=1, source_target_pairs={{0,1},{1,0},{2,3},{3,2},{4,5},{5,4},{6,7},{7,6},{8,9},{9,8},{10,11... | collective-permute-start | bytes 27656 | tf_op jit(solution)/shard_map/ppermute | solution.py:338
  24.8 5.8 %collective-permute-start.7 = (f32[64,512]{1,0:T(8,128)S(1)}, f32[64,512]{1,0:T(8,128)S(1)}, u32[]{:S(2)}, u32[]{:S(2)}) collective-permute-start(f32[64,512]{1,0:T(8,128)S(1)} %get-tuple-element.45), channel_id=1, source_target_pairs={{0,1},{1,0},{2,3},{3,2},{4,5},{5,4},{6,7},{7,6},{8,9},{9,8},{10,11... | collective-permute-start | bytes 393224 | tf_op jit(solution)/shard_map/ppermute | solution.py:326
  25.0 15.3 %collective-permute-start.12 = (f32[64,512]{1,0:T(8,128)S(1)}, f32[64,512]{1,0:T(8,128)S(1)}, u32[]{:S(2)}, u32[]{:S(2)}) collective-permute-start(f32[64,512]{1,0:T(8,128)S(1)} %get-tuple-element.74.refs_6_), channel_id=1, source_target_pairs={{0,16},{1,17},{2,18},{3,19},{4,20},{5,21},{6,22},{7,23},{8,24},{9,... | collective-permute-start | bytes 393224 | tf_op jit(solution)/shard_map/ppermute | solution.py:252
  27.1 13.2 %collective-permute-start.13 = (f32[64,512]{1,0:T(8,128)S(1)}, f32[64,512]{1,0:T(8,128)S(1)}, u32[]{:S(2)}, u32[]{:S(2)}) collective-permute-start(f32[64,512]{1,0:T(8,128)S(1)} %get-tuple-element.73.refs_7_), channel_id=1, source_target_pairs={{0,24},{1,25},{2,26},{3,27},{4,28},{5,29},{6,30},{7,31},{8,16},{9,... | collective-permute-start | bytes 393224 | tf_op jit(solution)/shard_map/ppermute | solution.py:252
  30.7 9.6 %collective-permute-start.14 = (f32[64,512]{1,0:T(8,128)S(1)}, f32[64,512]{1,0:T(8,128)S(1)}, u32[]{:S(2)}, u32[]{:S(2)}) collective-permute-start(f32[64,512]{1,0:T(8,128)S(1)} %add.73), channel_id=1, source_target_pairs={{0,8},{1,9},{2,10},{3,11},{4,12},{5,13},{6,14},{7,15},{8,0},{9,1},... | collective-permute-start | bytes 393224 | tf_op jit(solution)/shard_map/ppermute | solution.py:252
  31.1 6.9 %collective-permute-start.10 = (f32[32,512]{1,0:T(8,128)S(1)}, f32[32,512]{1,0:T(8,128)S(1)}, u32[]{:S(2)}, u32[]{:S(2)}) collective-permute-start(f32[32,512]{1,0:T(8,128)S(1)} %get-tuple-element.78), channel_id=1, source_target_pairs={{0,1},{1,0},{2,3},{3,2},{4,5},{5,4},{6,7},{7,6},{8,9},{9,8},{10,11... | collective-permute-start | bytes 196616 | tf_op jit(solution)/shard_map/ppermute | solution.py:326
  31.1 6.9 %collective-permute-start.9 = (f32[32,512]{1,0:T(8,128)S(1)}, f32[32,512]{1,0:T(8,128)S(1)}, u32[]{:S(2)}, u32[]{:S(2)}) collective-permute-start(f32[32,512]{1,0:T(8,128)S(1)} %get-tuple-element.77), channel_id=1, source_target_pairs={{0,1},{1,0},{2,3},{3,2},{4,5},{5,4},{6,7},{7,6},{8,9},{9,8},{10,11... | collective-permute-start | bytes 196616 | tf_op jit(solution)/shard_map/ppermute | solution.py:326
  40.4 6.7 %collective-permute-start.16 = (f32[64,512]{1,0:T(8,128)S(1)}, f32[64,512]{1,0:T(8,128)S(1)}, u32[]{:S(2)}, u32[]{:S(2)}) collective-permute-start(f32[64,512]{1,0:T(8,128)S(1)} %fusion.7.refs_0_), channel_id=1, source_target_pairs={{0,2},{1,9},{2,0},{3,11},{4,6},{5,13},{6,4},{7,15},{8,10},{9,1},{1... | collective-permute-start | bytes 393224 | tf_op jit(solution)/shard_map/ppermute | solution.py:252
  41.9 5.2 %collective-permute-start.17 = (f32[64,512]{1,0:T(8,128)S(1)}, f32[64,512]{1,0:T(8,128)S(1)}, u32[]{:S(2)}, u32[]{:S(2)}) collective-permute-start(f32[64,512]{1,0:T(8,128)S(1)} %fusion.7.refs_0_), channel_id=1, source_target_pairs={{0,4},{1,17},{2,6},{3,19},{4,0},{5,21},{6,2},{7,23},{8,12},{9,25},... | collective-permute-start | bytes 393224 | tf_op jit(solution)/shard_map/ppermute | solution.py:252
  43.4 5.9 %collective-permute-start.15 = (f32[64,512]{1,0:T(8,128)S(1)}, f32[64,512]{1,0:T(8,128)S(1)}, u32[]{:S(2)}, u32[]{:S(2)}) collective-permute-start(f32[64,512]{1,0:T(8,128)S(1)} %fusion.7.refs_0_), channel_id=1, source_target_pairs={{0,6},{1,25},{2,4},{3,27},{4,2},{5,29},{6,0},{7,31},{8,14},{9,17},... | collective-permute-start | bytes 393224 | tf_op jit(solution)/shard_map/ppermute | solution.py:252
  49.8 8.6 %collective-permute-start.18 = (f32[72,512]{1,0:T(8,128)S(1)}, f32[72,512]{1,0:T(8,128)S(1)}, u32[]{:S(2)}, u32[]{:S(2)}) collective-permute-start(f32[72,512]{1,0:T(8,128)S(1)} %get-tuple-element.63.refs_4_), channel_id=1, source_target_pairs={{0,16},{1,5},{2,18},{3,7},{4,20},{5,1},{6,22},{7,3},{8,24},{9,13},... | collective-permute-start | bytes 442376 | tf_op jit(solution)/shard_map/ppermute | solution.py:252
  51.7 6.6 %collective-permute-start.19 = (f32[72,512]{1,0:T(8,128)S(1)}, f32[72,512]{1,0:T(8,128)S(1)}, u32[]{:S(2)}, u32[]{:S(2)}) collective-permute-start(f32[72,512]{1,0:T(8,128)S(1)} %get-tuple-element.65), channel_id=1, source_target_pairs={{0,8},{1,3},{2,10},{3,1},{4,12},{5,7},{6,14},{7,5},{8,0},{9,11},{1... | collective-permute-start | bytes 442376 | tf_op jit(solution)/shard_map/ppermute | solution.py:252
  53.2 7.0 %collective-permute-start.20 = (f32[72,512]{1,0:T(8,128)S(1)}, f32[72,512]{1,0:T(8,128)S(1)}, u32[]{:S(2)}, u32[]{:S(2)}) collective-permute-start(f32[72,512]{1,0:T(8,128)S(1)} %get-tuple-element.66), channel_id=1, source_target_pairs={{0,24},{1,7},{2,26},{3,5},{4,28},{5,3},{6,30},{7,1},{8,16},{9,15},... | collective-permute-start | bytes 442376 | tf_op jit(solution)/shard_map/ppermute | solution.py:252
  60.4 5.0 %collective-permute-start.22 = (f32[64,512]{1,0:T(8,128)S(1)}, f32[64,512]{1,0:T(8,128)S(1)}, u32[]{:S(2)}, u32[]{:S(2)}) collective-permute-start(f32[64,512]{1,0:T(8,128)S(1)} %fusion.3.refs_0_), channel_id=1, source_target_pairs={{0,2},{1,9},{2,0},{3,11},{4,6},{5,13},{6,4},{7,15},{8,10},{9,1},{1... | collective-permute-start | bytes 393224 | tf_op jit(solution)/shard_map/ppermute | solution.py:252
  61.7 5.0 %collective-permute-start.23 = (f32[64,512]{1,0:T(8,128)S(1)}, f32[64,512]{1,0:T(8,128)S(1)}, u32[]{:S(2)}, u32[]{:S(2)}) collective-permute-start(f32[64,512]{1,0:T(8,128)S(1)} %fusion.3.refs_0_), channel_id=1, source_target_pairs={{0,4},{1,17},{2,6},{3,19},{4,0},{5,21},{6,2},{7,23},{8,12},{9,25},... | collective-permute-start | bytes 393224 | tf_op jit(solution)/shard_map/ppermute | solution.py:252
  62.5 5.9 %collective-permute-start.21 = (f32[64,512]{1,0:T(8,128)S(1)}, f32[64,512]{1,0:T(8,128)S(1)}, u32[]{:S(2)}, u32[]{:S(2)}) collective-permute-start(f32[64,512]{1,0:T(8,128)S(1)} %fusion.3.refs_0_), channel_id=1, source_target_pairs={{0,6},{1,25},{2,4},{3,27},{4,2},{5,29},{6,0},{7,31},{8,14},{9,17},... | collective-permute-start | bytes 393224 | tf_op jit(solution)/shard_map/ppermute | solution.py:252
  68.8 7.9 %collective-permute-start.24 = (f32[64,512]{1,0:T(8,128)S(1)}, f32[64,512]{1,0:T(8,128)S(1)}, u32[]{:S(2)}, u32[]{:S(2)}) collective-permute-start(f32[64,512]{1,0:T(8,128)S(1)} %get-tuple-element.67.refs_4_), channel_id=1, source_target_pairs={{0,16},{1,5},{2,18},{3,7},{4,20},{5,1},{6,22},{7,3},{8,24},{9,13},... | collective-permute-start | bytes 393224 | tf_op jit(solution)/shard_map/ppermute | solution.py:252
  71.2 5.6 %collective-permute-start.25 = (f32[64,512]{1,0:T(8,128)S(1)}, f32[64,512]{1,0:T(8,128)S(1)}, u32[]{:S(2)}, u32[]{:S(2)}) collective-permute-start(f32[64,512]{1,0:T(8,128)S(1)} %get-tuple-element.69), channel_id=1, source_target_pairs={{0,8},{1,3},{2,10},{3,1},{4,12},{5,7},{6,14},{7,5},{8,0},{9,11},{1... | collective-permute-start | bytes 393224 | tf_op jit(solution)/shard_map/ppermute | solution.py:252
  71.9 6.9 %collective-permute-start.26 = (f32[64,512]{1,0:T(8,128)S(1)}, f32[64,512]{1,0:T(8,128)S(1)}, u32[]{:S(2)}, u32[]{:S(2)}) collective-permute-start(f32[64,512]{1,0:T(8,128)S(1)} %get-tuple-element.70), channel_id=1, source_target_pairs={{0,24},{1,7},{2,26},{3,5},{4,28},{5,3},{6,30},{7,1},{8,16},{9,15},... | collective-permute-start | bytes 393224 | tf_op jit(solution)/shard_map/ppermute | solution.py:252
  78.8 1.3 %collective-permute-start.27 = (f32[64,256]{1,0:T(8,128)S(1)}, f32[64,256]{1,0:T(8,128)S(1)}, u32[]{:S(2)}, u32[]{:S(2)}) collective-permute-start(f32[64,256]{1,0:T(8,128)S(1)} %get-tuple-element.76), channel_id=1, source_target_pairs={{0,1},{1,0},{2,3},{3,2},{4,5},{5,4},{6,7},{7,6},{8,9},{9,8},{10,11... | collective-permute-start | bytes 196616 | tf_op jit(solution)/shard_map/ppermute | solution.py:451

commit v5 on v4

--- a/solution.py
+++ b/solution.py
@@ -355,7 +355,7 @@
     if near[1:]:
         near_given, mine, other = lax.optimization_barrier((near_given, mine, other))
         added(near[1:], near_mine, near_given)
-    added(near[:1], mine, swapped(other, 2))
+    added(near[:1], mine, swapped(other))
 
     def summed(values):
         order = [peers // 2] + [k for k in range(1, peers) if k != peers // 2]
@@ -407,7 +407,7 @@
             cost_estimate=cost(total_width, half),
         )(*inputs, other)
 
-    got = {k: exchange(sums[k], along_tgt[k]) for k in far + near[1:]}
+    got = {k: exchange(sums[k], along_tgt[k]) for k in range(peers - 1, 0, -1)}
     for value in got.values():
         pullback = pullback + value
 
@@ -420,9 +420,7 @@
             (sofar,) = step(arrived[:1], early, 0, spans, None, with_sums, False, after_final)
             if peers > 2:
                 (sofar,) = step(arrived[1:-1], early, 1, spans, sofar, with_sums, False, after_final)
-            far_ones = step(arrived[-1:], final, 0, far, sofar, with_sums, True, after_final)
-            near_ones = step(arrived[-1:], final, 0, near, sofar, with_sums, True, far_ones[0])
-            products = [*near_ones, *far_ones]
+            products = step(arrived[-1:], final, 0, spans, sofar, with_sums, True, after_final)
         else:
             upper = half + (ONES if with_sums else 0)
             out_rows = half + (8 if with_sums else 0)

time: 81 us -> 79.9 us (0.986)
    ppermute x21, waiting for transfers between devices: 16.6 us -> 15.7 us  [exchange(): return lax.ppermute(value, ('tgt', 'src'), pairs)]
    pallas_call x8 -> x6, Pallas kernels: 6.4 us -> 6.17 us  [step(): pl.pallas_call(functools.partial(step_kernel, half, start, len(these), sp...]
  transfers between devices with their start and end apart: 28 -> 27, of which waited for: 11 -> 10; matrix products, arithmetic and copies ran while one was open for 3% -> 3% of each run, Pallas kernels for 28% -> 27%
where the time goes in v5:
time: 79.9 us; the launch traced here: 79.7 us
  starting transfers between devices  33.7 us (42%)
  Pallas kernels  25.8 us (32%)
  waiting for transfers between devices  17 us (21%)
  other arithmetic  2.81 us (4%)
    ppermute x21, starting transfers between devices, exchange(): return lax.ppermute(value, ('tgt', 'src'), pairs)  32.5 us
    ppermute x21, waiting for transfers between devices, exchange(): return lax.ppermute(value, ('tgt', 'src'), pairs)  15.7 us
    pallas_call x6, Pallas kernels, pull(): pl.pallas_call(functools.partial(pull_kernel, inverse, full, width, len(w...  10.9 us
    pallas_call x2, Pallas kernels, keep(): pl.pallas_call(functools.partial(keep_kernel, inverse, start * width), ou...  8.7 us
    pallas_call x6, Pallas kernels, step(): pl.pallas_call(functools.partial(step_kernel, half, start, len(these), sp...  6.17 us
  transfers between devices with their start and end apart: 27, of which 10 were waited for; matrix products, arithmetic and copies ran while one was open for 3% of the time, Pallas kernels for 27%

profile of v5, /device:TPU:0, one launch (start us, length us, event | category | flops | bytes accessed | tf_op | source)
XLA Modules:
  0.0 79.7 jit_solution(4509262819082654854)
XLA Ops:
  0.0 0.5 collective-permute-start
  0.5 0.1 pad.39.clone
  0.5 1.1 %fusion.refs_1_ = f32[136,512]{1,0:T(8,128)S(1)} fusion(f32[3,256]{1,0:T(4,128)} %param.5, f32[3,512]{1,0:T(4,128)} %param.4, f32[128,512]{1,0:T(8,128)} %param.3, f32[136]{0:T(256)S(1)} %pad.39.clone), kind=kLoop, calls=%fused_computation.3 | loop fusion | flops 487424 | bytes 550432 | tf_op jit(solution)/shard_map/concatenate | solution.py:259
  1.6 2.7 %collective-permute-start.1 = (f32[136,512]{1,0:T(8,128)S(1)}, f32[136,512]{1,0:T(8,128)S(1)}, u32[]{:S(2)}, u32[]{:S(2)}) collective-permute-start(f32[136,512]{1,0:T(8,128)S(1)} %fusion.refs_1_), channel_id=1, source_target_pairs={{0,2},{1,3},{2,0},{3,1},{4,6},{5,7},{6,4},{7,5},{8,10},{9,11},{10,... | collective-permute-start | bytes 835592 | tf_op jit(solution)/shard_map/ppermute | solution.py:252
  4.3 1.5 %collective-permute-start.2 = (f32[136,512]{1,0:T(8,128)S(1)}, f32[136,512]{1,0:T(8,128)S(1)}, u32[]{:S(2)}, u32[]{:S(2)}) collective-permute-start(f32[136,512]{1,0:T(8,128)S(1)} %fusion.refs_1_), channel_id=1, source_target_pairs={{0,4},{1,5},{2,6},{3,7},{4,0},{5,1},{6,2},{7,3},{8,12},{9,13},{10,... | collective-permute-start | bytes 835592 | tf_op jit(solution)/shard_map/ppermute | solution.py:252
  5.9 0.8 maximum_select_fusion.1.refs_2_
  6.6 2.1 %collective-permute-start.4 = (f32[3,512]{1,0:T(4,128)S(1)}, f32[3,512]{1,0:T(4,128)S(1)}, u32[]{:S(2)}, u32[]{:S(2)}) collective-permute-start(f32[3,512]{1,0:T(4,128)S(1)} %maximum_select_fusion.1.refs_2_), channel_id=1, source_target_pairs={{0,8},{1,9},{2,10},{3,11},{4,12},{5,13},{6,14},{7,15},{8,0},{9,1},... | collective-permute-start | bytes 18440 | tf_op jit(solution)/shard_map/ppermute | solution.py:252
  8.7 2.6 %collective-permute-start.5 = (f32[3,512]{1,0:T(4,128)S(1)}, f32[3,512]{1,0:T(4,128)S(1)}, u32[]{:S(2)}, u32[]{:S(2)}) collective-permute-start(f32[3,512]{1,0:T(4,128)S(1)} %maximum_select_fusion.1.refs_2_), channel_id=1, source_target_pairs={{0,16},{1,17},{2,18},{3,19},{4,20},{5,21},{6,22},{7,23},{8,24},{9,... | collective-permute-start | bytes 18440 | tf_op jit(solution)/shard_map/ppermute | solution.py:252
  11.3 0.0 collective-permute-done.4.refs_3_
  11.3 3.1 %collective-permute-start.6 = (f32[3,512]{1,0:T(4,128)S(1)}, f32[3,512]{1,0:T(4,128)S(1)}, u32[]{:S(2)}, u32[]{:S(2)}) collective-permute-start(f32[3,512]{1,0:T(4,128)S(1)} %maximum_select_fusion.1.refs_2_), channel_id=1, source_target_pairs={{0,24},{1,25},{2,26},{3,27},{4,28},{5,29},{6,30},{7,31},{8,16},{9,... | collective-permute-start | bytes 18440 | tf_op jit(solution)/shard_map/ppermute | solution.py:252
  14.4 1.4 %shard_map.37 = (bf16[32,1024]{1,0:T(8,128)(2,1)S(1)}, f32[128,1024]{1,0:T(8,128)S(1)}) custom-call(s32[1]{0:T(128)} %bitcast.refs_0_, f32[136,512]{1,0:T(8,128)S(1)} %fusion.refs_1_, f32[3,512]{1,0:T(4,128)S(1)} %maximum_select_fusion.1.refs_2_, f32[3,512]{1,0:T(4,128)S(1)} %collective-permute-done.4.refs_3_), custom_call_target="tpu_custom_call" | custom-call | flops 65536 | bytes 128 | tf_op jit(solution)/shard_map/pallas_call | solution.py:300
  15.7 0.0 collective-permute-done.5.refs_2_
  15.7 1.0 %collective-permute-done.6.refs_3_ = f32[3,512]{1,0:T(4,128)S(1)} collective-permute-done((f32[3,512]{1,0:T(4,128)S(1)}, f32[3,512]{1,0:T(4,128)S(1)}, u32[]{:S(2)}, u32[]{:S(2)}) %collective-permute-start.6) | collective-permute-done | bytes 6176 | tf_op jit(solution)/shard_map/ppermute | solution.py:252
  16.7 1.4 %shard_map.38 = (bf16[32,1024]{1,0:T(8,128)(2,1)S(1)}, f32[128,1024]{1,0:T(8,128)S(1)}) custom-call(s32[1]{0:T(128)} %bitcast.refs_0_, f32[136,512]{1,0:T(8,128)S(1)} %fusion.refs_1_, f32[3,512]{1,0:T(4,128)S(1)} %collective-permute-done.5.refs_2_, f32[3,512]{1,0:T(4,128)S(1)} %collective-permute-done.6.refs_3_), custom_call_target="tpu_custom_call" | custom-call | flops 65536 | bytes 128 | tf_op jit(solution)/shard_map/pallas_call | solution.py:300
  18.1 0.0 collective-permute-done.1.refs_1_
  18.1 1.4 %shard_map.39.refs_4_ = f32[128,1024]{1,0:T(8,128)S(1)} custom-call(s32[1]{0:T(128)} %bitcast.refs_0_, f32[136,512]{1,0:T(8,128)S(1)} %collective-permute-done.1.refs_1_, bf16[32,1024]{1,0:T(8,128)(2,1)S(1)} %get-tuple-element.42.refs_2_.refs_3_, f32[128,1024]{1,0:T(8,128)S(1)} %get-tuple-element.43.refs_3_), custom_call_target="tpu_custom_call" | custom-call | flops 268435456 | bytes 128 | tf_op jit(solution)/shard_map/pallas_call | solution.py:300
  19.5 0.0 collective-permute-done.3.refs_2_.refs_3_
  19.5 2.5 %shard_map.40 = (f32[64,512]{1,0:T(8,128)S(1)}, f32[64,512]{1,0:T(8,128)S(1)}, f32[64,1024]{1,0:T(8,128)S(1)}) custom-call(s32[1]{0:T(128)} %bitcast.refs_0_, f32[136,512]{1,0:T(8,128)S(1)} %collective-permute-done.2.refs_1_.refs_2_, f32[136,512]{1,0:T(8,128)S(1)} %collective-permute-done.3.refs_2_.refs_3_, ...), custom_call_target="tpu_custom_call" | custom-call | flops 536870912 | bytes 128 | tf_op jit(solution)/shard_map/pallas_call | solution.py:300
  22.0 0.1 collective-permute-start.8
  22.1 0.5 collective-permute-start.10
  22.7 2.2 %shard_map.41 = (f32[64,512]{1,0:T(8,128)S(1)}, f32[64,512]{1,0:T(8,128)S(1)}) custom-call(s32[1]{0:T(128)} %bitcast.refs_0_, f32[136,512]{1,0:T(8,128)S(1)} %collective-permute-done.1.refs_1_, f32[136,512]{1,0:T(8,128)S(1)} %collective-permute-done.2.refs_1_.refs_2_, f32[136,512]{1,0:T(8,128)S(1)} %collective-permute-done.3.refs_2_.refs_3_, ...), custom_call_target="tpu_custom_call" | custom-call | flops 402653184 | bytes 128 | tf_op jit(solution)/shard_map/pallas_call | solution.py:300
  24.8 0.1 collective-permute-start.7
  24.9 0.0 collective-permute-done.10
  25.0 0.0 collective-permute-done.8
  25.0 3.2 %collective-permute-start.11 = (f32[64,512]{1,0:T(8,128)S(1)}, f32[64,512]{1,0:T(8,128)S(1)}, u32[]{:S(2)}, u32[]{:S(2)}) collective-permute-start(f32[64,512]{1,0:T(8,128)S(1)} %get-tuple-element.73.refs_7_), channel_id=1, source_target_pairs={{0,24},{1,25},{2,26},{3,27},{4,28},{5,29},{6,30},{7,31},{8,16},{9,... | collective-permute-start | bytes 393224 | tf_op jit(solution)/shard_map/ppermute | solution.py:252
  28.2 0.0 collective-permute-start.12
  28.2 2.2 %shard_map.42 = (f32[64,512]{1,0:T(8,128)S(1)}, f32[64,512]{1,0:T(8,128)S(1)}) custom-call(s32[1]{0:T(128)} %bitcast.refs_0_, f32[136,512]{1,0:T(8,128)S(1)} %collective-permute-done.1.refs_1_, f32[136,512]{1,0:T(8,128)S(1)} %collective-permute-done.2.refs_1_.refs_2_, f32[136,512]{1,0:T(8,128)S(1)} %collective-permute-done.3.refs_2_.refs_3_, ...), custom_call_target="tpu_custom_call" | custom-call | flops 196608 | bytes 128 | tf_op jit(solution)/shard_map/pallas_call | solution.py:300
  30.4 0.0 collective-permute-done.7
  30.4 1.4 %collective-permute-start.13 = (f32[64,512]{1,0:T(8,128)S(1)}, f32[64,512]{1,0:T(8,128)S(1)}, u32[]{:S(2)}, u32[]{:S(2)}) collective-permute-start(f32[64,512]{1,0:T(8,128)S(1)} %add.73), channel_id=1, source_target_pairs={{0,8},{1,9},{2,10},{3,11},{4,12},{5,13},{6,14},{7,15},{8,0},{9,1},... | collective-permute-start | bytes 393224 | tf_op jit(solution)/shard_map/ppermute | solution.py:252
  31.8 6.3 %shard_map.43 = (bf16[1536,2048]{1,0:T(8,128)(2,1)S(1)}, bf16[1536,2048]{1,0:T(8,128)(2,1)S(1)}, f32[1,512]{1,0:T(1,128)S(1)}) custom-call(f32[3,2048]{1,0:T(4,128)S(1)} %get-tuple-element.78.row_points, f32[3,2048]{1,0:T(4,128)S(1)} %get-tuple-element.77.col_points), custom_call_target="tpu_custom_call" | custom-call | flops 131072 | bytes 64 | tf_op jit(solution)/shard_map/pallas_call | solution.py:372
  38.1 0.0 collective-permute-done.9
  38.2 1.7 %collective-permute-done.12 = f32[64,512]{1,0:T(8,128)S(1)} collective-permute-done((f32[64,512]{1,0:T(8,128)S(1)}, f32[64,512]{1,0:T(8,128)S(1)}, u32[]{:S(2)}, u32[]{:S(2)}) %collective-permute-start.12) | collective-permute-done | bytes 131104 | tf_op jit(solution)/shard_map/ppermute | solution.py:252
  39.8 0.1 add_add_fusion.1.refs_0_
  39.9 1.3 %collective-permute-start.15 = (f32[64,512]{1,0:T(8,128)S(1)}, f32[64,512]{1,0:T(8,128)S(1)}, u32[]{:S(2)}, u32[]{:S(2)}) collective-permute-start(f32[64,512]{1,0:T(8,128)S(1)} %add_add_fusion.1.refs_0_), channel_id=1, source_target_pairs={{0,2},{1,9},{2,0},{3,11},{4,6},{5,13},{6,4},{7,15},{8,10},{9,1},{1... | collective-permute-start | bytes 393224 | tf_op jit(solution)/shard_map/ppermute | solution.py:252
  41.2 0.8 %collective-permute-start.16 = (f32[64,512]{1,0:T(8,128)S(1)}, f32[64,512]{1,0:T(8,128)S(1)}, u32[]{:S(2)}, u32[]{:S(2)}) collective-permute-start(f32[64,512]{1,0:T(8,128)S(1)} %add_add_fusion.1.refs_0_), channel_id=1, source_target_pairs={{0,4},{1,17},{2,6},{3,19},{4,0},{5,21},{6,2},{7,23},{8,12},{9,25},... | collective-permute-start | bytes 393224 | tf_op jit(solution)/shard_map/ppermute | solution.py:252
  42.0 1.4 %collective-permute-start.14 = (f32[64,512]{1,0:T(8,128)S(1)}, f32[64,512]{1,0:T(8,128)S(1)}, u32[]{:S(2)}, u32[]{:S(2)}) collective-permute-start(f32[64,512]{1,0:T(8,128)S(1)} %add_add_fusion.1.refs_0_), channel_id=1, source_target_pairs={{0,6},{1,25},{2,4},{3,27},{4,2},{5,29},{6,0},{7,31},{8,14},{9,17},... | collective-permute-start | bytes 393224 | tf_op jit(solution)/shard_map/ppermute | solution.py:252
  43.5 2.4 %shard_map.44 = (bf16[512,2048]{1,0:T(8,128)(2,1)S(1)}, bf16[512,2048]{1,0:T(8,128)(2,1)S(1)}, f32[1,512]{1,0:T(1,128)S(1)}) custom-call(f32[3,2048]{1,0:T(4,128)S(1)} %get-tuple-element.78.row_points, f32[3,2048]{1,0:T(4,128)S(1)} %get-tuple-element.77.col_points), custom_call_target="tpu_custom_call" | custom-call | flops 131072 | bytes 64 | tf_op jit(solution)/shard_map/pallas_call | solution.py:372
  45.8 0.8 %shard_map.45.refs_4_ = f32[72,2048]{1,0:T(8,128)S(1)} custom-call(f32[64,512]{1,0:T(8,128)S(1)} %add_add_fusion.1.refs_0_, bf16[1536,2048]{1,0:T(8,128)(2,1)S(1)} %get-tuple-element.60.refs_1_.refs_2_, bf16[1536,2048]{1,0:T(8,128)(2,1)S(1)} %get-tuple-element.61.refs_2_.refs_3_, f32[1,512]{1,0:T(1,128)S(1)} %get-tuple-element.62.refs_3_.refs_5_.refs_4_), custom_call_target="tpu_custom_call" | custom-call | flops 131072 | bytes 64 | tf_op jit(solution)/shard_map/pallas_call | solution.py:398
  46.7 1.5 %shard_map.46.refs_3_ = f32[72,2048]{1,0:T(8,128)S(1)} custom-call(f32[64,512]{1,0:T(8,128)S(1)} %collective-permute-done.15.refs_0_, f32[64,512]{1,0:T(8,128)S(1)} %collective-permute-done.16.refs_1_, bf16[1536,2048]{1,0:T(8,128)(2,1)S(1)} %get-tuple-element.60.refs_1_.refs_2_, bf16[1536,2048]{1,0:T(8,128)(2,1)S(1)} %get-tuple-element.61.refs_2_.refs_3_, ...), custom_call_target="tpu_custom_call" | custom-call | flops 131072 | bytes 64 | tf_op jit(solution)/shard_map/pallas_call | solution.py:398
  48.2 0.8 %shard_map.47 = (f32[72,512]{1,0:T(8,128)S(1)}, f32[72,512]{1,0:T(8,128)S(1)}, f32[72,512]{1,0:T(8,128)S(1)}, f32[72,512]{1,0:T(8,128)S(1)}) custom-call(f32[64,512]{1,0:T(8,128)S(1)} %collective-permute-done.14.refs_0_, bf16[512,2048]{1,0:T(8,128)(2,1)S(1)} %get-tuple-element.58.refs_1_, bf16[512,2048]{1,0:T(8,128)(2,1)S(1)} %get-tuple-element.59.refs_2_, ...), custom_call_target="tpu_custom_call" | custom-call | flops 131072 | bytes 64 | tf_op jit(solution)/shard_map/pallas_call | solution.py:398
  49.0 0.8 collective-permute-start.17
  49.8 2.3 %collective-permute-start.18 = (f32[72,512]{1,0:T(8,128)S(1)}, f32[72,512]{1,0:T(8,128)S(1)}, u32[]{:S(2)}, u32[]{:S(2)}) collective-permute-start(f32[72,512]{1,0:T(8,128)S(1)} %get-tuple-element.65), channel_id=1, source_target_pairs={{0,8},{1,3},{2,10},{3,1},{4,12},{5,7},{6,14},{7,5},{8,0},{9,11},{1... | collective-permute-start | bytes 442376 | tf_op jit(solution)/shard_map/ppermute | solution.py:252
  52.1 1.4 %collective-permute-start.19 = (f32[72,512]{1,0:T(8,128)S(1)}, f32[72,512]{1,0:T(8,128)S(1)}, u32[]{:S(2)}, u32[]{:S(2)}) collective-permute-start(f32[72,512]{1,0:T(8,128)S(1)} %get-tuple-element.66), channel_id=1, source_target_pairs={{0,24},{1,7},{2,26},{3,5},{4,28},{5,3},{6,30},{7,1},{8,16},{9,15},... | collective-permute-start | bytes 442376 | tf_op jit(solution)/shard_map/ppermute | solution.py:252
  53.5 3.3 %collective-permute-done.17 = f32[72,512]{1,0:T(8,128)S(1)} collective-permute-done((f32[72,512]{1,0:T(8,128)S(1)}, f32[72,512]{1,0:T(8,128)S(1)}, u32[]{:S(2)}, u32[]{:S(2)}) %collective-permute-start.17) | collective-permute-done | bytes 147488 | tf_op jit(solution)/shard_map/ppermute | solution.py:252
  56.8 0.0 collective-permute-done.18
  56.8 2.4 %collective-permute-done.19 = f32[72,512]{1,0:T(8,128)S(1)} collective-permute-done((f32[72,512]{1,0:T(8,128)S(1)}, f32[72,512]{1,0:T(8,128)S(1)}, u32[]{:S(2)}, u32[]{:S(2)}) %collective-permute-start.19) | collective-permute-done | bytes 147488 | tf_op jit(solution)/shard_map/ppermute | solution.py:252
  59.3 1.3 %collective-permute-start.21 = (f32[64,512]{1,0:T(8,128)S(1)}, f32[64,512]{1,0:T(8,128)S(1)}, u32[]{:S(2)}, u32[]{:S(2)}) collective-permute-start(f32[64,512]{1,0:T(8,128)S(1)} %fusion.3.refs_0_), channel_id=1, source_target_pairs={{0,2},{1,9},{2,0},{3,11},{4,6},{5,13},{6,4},{7,15},{8,10},{9,1},{1... | collective-permute-start | bytes 393224 | tf_op jit(solution)/shard_map/ppermute | solution.py:252
  60.6 0.8 collective-permute-start.22
  61.4 1.4 %collective-permute-start.20 = (f32[64,512]{1,0:T(8,128)S(1)}, f32[64,512]{1,0:T(8,128)S(1)}, u32[]{:S(2)}, u32[]{:S(2)}) collective-permute-start(f32[64,512]{1,0:T(8,128)S(1)} %fusion.3.refs_0_), channel_id=1, source_target_pairs={{0,6},{1,25},{2,4},{3,27},{4,2},{5,29},{6,0},{7,31},{8,14},{9,17},... | collective-permute-start | bytes 393224 | tf_op jit(solution)/shard_map/ppermute | solution.py:252
  62.9 0.8 shard_map.48.refs_4_
  63.6 0.7 collective-permute-done.21.refs_0_
  64.3 1.3 %collective-permute-done.22.refs_1_ = f32[64,512]{1,0:T(8,128)S(1)} collective-permute-done((f32[64,512]{1,0:T(8,128)S(1)}, f32[64,512]{1,0:T(8,128)S(1)}, u32[]{:S(2)}, u32[]{:S(2)}) %collective-permute-start.22) | collective-permute-done | bytes 131104 | tf_op jit(solution)/shard_map/ppermute | solution.py:252
  65.6 1.4 %shard_map.49.refs_3_ = f32[64,2048]{1,0:T(8,128)S(1)} custom-call(f32[64,512]{1,0:T(8,128)S(1)} %collective-permute-done.21.refs_0_, f32[64,512]{1,0:T(8,128)S(1)} %collective-permute-done.22.refs_1_, bf16[1536,2048]{1,0:T(8,128)(2,1)S(1)} %get-tuple-element.60.refs_1_.refs_2_, bf16[1536,2048]{1,0:T(8,128)(2,1)S(1)} %get-tuple-element.61.refs_2_.refs_3_, ...), custom_call_target="tpu_custom_call" | custom-call | flops 131072 | bytes 64 | tf_op jit(solution)/shard_map/pallas_call | solution.py:398
  67.1 0.2 collective-permute-done.20.refs_0_
  67.3 0.8 shard_map.50
  68.1 1.8 %collective-permute-start.23 = (f32[64,512]{1,0:T(8,128)S(1)}, f32[64,512]{1,0:T(8,128)S(1)}, u32[]{:S(2)}, u32[]{:S(2)}) collective-permute-start(f32[64,512]{1,0:T(8,128)S(1)} %get-tuple-element.68), channel_id=1, source_target_pairs={{0,16},{1,5},{2,18},{3,7},{4,20},{5,1},{6,22},{7,3},{8,24},{9,13},... | collective-permute-start | bytes 393224 | tf_op jit(solution)/shard_map/ppermute | solution.py:252
  69.9 0.4 collective-permute-start.24
  70.3 2.2 %collective-permute-start.25 = (f32[64,512]{1,0:T(8,128)S(1)}, f32[64,512]{1,0:T(8,128)S(1)}, u32[]{:S(2)}, u32[]{:S(2)}) collective-permute-start(f32[64,512]{1,0:T(8,128)S(1)} %get-tuple-element.70), channel_id=1, source_target_pairs={{0,24},{1,7},{2,26},{3,5},{4,28},{5,3},{6,30},{7,1},{8,16},{9,15},... | collective-permute-start | bytes 393224 | tf_op jit(solution)/shard_map/ppermute | solution.py:252
  72.5 2.9 %collective-permute-done.23 = f32[64,512]{1,0:T(8,128)S(1)} collective-permute-done((f32[64,512]{1,0:T(8,128)S(1)}, f32[64,512]{1,0:T(8,128)S(1)}, u32[]{:S(2)}, u32[]{:S(2)}) %collective-permute-start.23) | collective-permute-done | bytes 131104 | tf_op jit(solution)/shard_map/ppermute | solution.py:252
  75.5 2.2 %collective-permute-done.25 = f32[64,512]{1,0:T(8,128)S(1)} collective-permute-done((f32[64,512]{1,0:T(8,128)S(1)}, f32[64,512]{1,0:T(8,128)S(1)}, u32[]{:S(2)}, u32[]{:S(2)}) %collective-permute-start.25) | collective-permute-done | bytes 131104 | tf_op jit(solution)/shard_map/ppermute | solution.py:252
  77.7 0.1 multiply_add_fusion
  77.8 0.1 collective-permute-start.26
  77.8 1.2 %collective-permute-done.26 = f32[64,256]{1,0:T(8,128)S(1)} collective-permute-done((f32[64,256]{1,0:T(8,128)S(1)}, f32[64,256]{1,0:T(8,128)S(1)}, u32[]{:S(2)}, u32[]{:S(2)}) %collective-permute-start.26) | collective-permute-done | bytes 65568 | tf_op jit(solution)/shard_map/ppermute | solution.py:449
  79.1 0.7 maximum_select_fusion
  (26 shorter events, 0.2 us)
Async XLA Ops:
  0.0 1.6 %collective-permute-start = (f32[3,256]{1,0:T(4,128)}, f32[3,256]{1,0:T(4,128)S(1)}, u32[]{:S(2)}, u32[]{:S(2)}) collective-permute-start(f32[3,256]{1,0:T(4,128)} %param.5), channel_id=1, source_target_pairs={{0,1},{1,0},{2,3},{3,2},{4,5},{5,4},{6,7},{7,6},{8,9},{9,8},{10,11... | collective-permute-start | bytes 9224 | tf_op jit(solution)/shard_map/ppermute | solution.py:268
  1.6 16.5 %collective-permute-start.1 = (f32[136,512]{1,0:T(8,128)S(1)}, f32[136,512]{1,0:T(8,128)S(1)}, u32[]{:S(2)}, u32[]{:S(2)}) collective-permute-start(f32[136,512]{1,0:T(8,128)S(1)} %fusion.refs_1_), channel_id=1, source_target_pairs={{0,2},{1,3},{2,0},{3,1},{4,6},{5,7},{6,4},{7,5},{8,10},{9,11},{10,... | collective-permute-start | bytes 835592 | tf_op jit(solution)/shard_map/ppermute | solution.py:252
  4.3 15.2 %collective-permute-start.2 = (f32[136,512]{1,0:T(8,128)S(1)}, f32[136,512]{1,0:T(8,128)S(1)}, u32[]{:S(2)}, u32[]{:S(2)}) collective-permute-start(f32[136,512]{1,0:T(8,128)S(1)} %fusion.refs_1_), channel_id=1, source_target_pairs={{0,4},{1,5},{2,6},{3,7},{4,0},{5,1},{6,2},{7,3},{8,12},{9,13},{10,... | collective-permute-start | bytes 835592 | tf_op jit(solution)/shard_map/ppermute | solution.py:252
  5.9 13.6 %collective-permute-start.3 = (f32[136,512]{1,0:T(8,128)S(1)}, f32[136,512]{1,0:T(8,128)S(1)}, u32[]{:S(2)}, u32[]{:S(2)}) collective-permute-start(f32[136,512]{1,0:T(8,128)S(1)} %fusion.refs_1_), channel_id=1, source_target_pairs={{0,6},{1,7},{2,4},{3,5},{4,2},{5,3},{6,0},{7,1},{8,14},{9,15},{10,... | collective-permute-start | bytes 835592 | tf_op jit(solution)/shard_map/ppermute | solution.py:252
  6.6 4.6 %collective-permute-start.4 = (f32[3,512]{1,0:T(4,128)S(1)}, f32[3,512]{1,0:T(4,128)S(1)}, u32[]{:S(2)}, u32[]{:S(2)}) collective-permute-start(f32[3,512]{1,0:T(4,128)S(1)} %maximum_select_fusion.1.refs_2_), channel_id=1, source_target_pairs={{0,8},{1,9},{2,10},{3,11},{4,12},{5,13},{6,14},{7,15},{8,0},{9,1},... | collective-permute-start | bytes 18440 | tf_op jit(solution)/shard_map/ppermute | solution.py:252
  8.7 7.1 %collective-permute-start.5 = (f32[3,512]{1,0:T(4,128)S(1)}, f32[3,512]{1,0:T(4,128)S(1)}, u32[]{:S(2)}, u32[]{:S(2)}) collective-permute-start(f32[3,512]{1,0:T(4,128)S(1)} %maximum_select_fusion.1.refs_2_), channel_id=1, source_target_pairs={{0,16},{1,17},{2,18},{3,19},{4,20},{5,21},{6,22},{7,23},{8,24},{9,... | collective-permute-start | bytes 18440 | tf_op jit(solution)/shard_map/ppermute | solution.py:252
  11.3 5.4 %collective-permute-start.6 = (f32[3,512]{1,0:T(4,128)S(1)}, f32[3,512]{1,0:T(4,128)S(1)}, u32[]{:S(2)}, u32[]{:S(2)}) collective-permute-start(f32[3,512]{1,0:T(4,128)S(1)} %maximum_select_fusion.1.refs_2_), channel_id=1, source_target_pairs={{0,24},{1,25},{2,26},{3,27},{4,28},{5,29},{6,30},{7,31},{8,16},{9,... | collective-permute-start | bytes 18440 | tf_op jit(solution)/shard_map/ppermute | solution.py:252
  22.0 3.0 %collective-permute-start.8 = (f32[64,1024]{1,0:T(8,128)S(1)}, f32[64,1024]{1,0:T(8,128)S(1)}, u32[]{:S(2)}, u32[]{:S(2)}) collective-permute-start(f32[64,1024]{1,0:T(8,128)S(1)} %get-tuple-element.44.refs_6_), channel_id=1, source_target_pairs={{0,1},{1,0},{2,3},{3,2},{4,5},{5,4},{6,7},{7,6},{8,9},{9,8},{10,11... | collective-permute-start | bytes 786440 | tf_op jit(solution)/shard_map/ppermute | solution.py:326
  22.1 2.8 %collective-permute-start.10 = (f32[3,768]{1,0:T(4,128)S(1)}, f32[3,768]{1,0:T(4,128)S(1)}, u32[]{:S(2)}, u32[]{:S(2)}) collective-permute-start(f32[3,768]{1,0:T(4,128)S(1)} %pad_maximum_fusion.2), channel_id=1, source_target_pairs={{0,1},{1,0},{2,3},{3,2},{4,5},{5,4},{6,7},{7,6},{8,9},{9,8},{10,11... | collective-permute-start | bytes 27656 | tf_op jit(solution)/shard_map/ppermute | solution.py:338
  24.8 5.5 %collective-permute-start.7 = (f32[64,512]{1,0:T(8,128)S(1)}, f32[64,512]{1,0:T(8,128)S(1)}, u32[]{:S(2)}, u32[]{:S(2)}) collective-permute-start(f32[64,512]{1,0:T(8,128)S(1)} %get-tuple-element.45), channel_id=1, source_target_pairs={{0,1},{1,0},{2,3},{3,2},{4,5},{5,4},{6,7},{7,6},{8,9},{9,8},{10,11... | collective-permute-start | bytes 393224 | tf_op jit(solution)/shard_map/ppermute | solution.py:326
  25.0 13.1 %collective-permute-start.11 = (f32[64,512]{1,0:T(8,128)S(1)}, f32[64,512]{1,0:T(8,128)S(1)}, u32[]{:S(2)}, u32[]{:S(2)}) collective-permute-start(f32[64,512]{1,0:T(8,128)S(1)} %get-tuple-element.73.refs_7_), channel_id=1, source_target_pairs={{0,24},{1,25},{2,26},{3,27},{4,28},{5,29},{6,30},{7,31},{8,16},{9,... | collective-permute-start | bytes 393224 | tf_op jit(solution)/shard_map/ppermute | solution.py:252
  28.2 11.7 %collective-permute-start.12 = (f32[64,512]{1,0:T(8,128)S(1)}, f32[64,512]{1,0:T(8,128)S(1)}, u32[]{:S(2)}, u32[]{:S(2)}) collective-permute-start(f32[64,512]{1,0:T(8,128)S(1)} %get-tuple-element.74.refs_6_), channel_id=1, source_target_pairs={{0,16},{1,17},{2,18},{3,19},{4,20},{5,21},{6,22},{7,23},{8,24},{9,... | collective-permute-start | bytes 393224 | tf_op jit(solution)/shard_map/ppermute | solution.py:252
  30.4 7.7 %collective-permute-start.13 = (f32[64,512]{1,0:T(8,128)S(1)}, f32[64,512]{1,0:T(8,128)S(1)}, u32[]{:S(2)}, u32[]{:S(2)}) collective-permute-start(f32[64,512]{1,0:T(8,128)S(1)} %add.73), channel_id=1, source_target_pairs={{0,8},{1,9},{2,10},{3,11},{4,12},{5,13},{6,14},{7,15},{8,0},{9,1},... | collective-permute-start | bytes 393224 | tf_op jit(solution)/shard_map/ppermute | solution.py:252
  31.8 6.4 %collective-permute-start.9 = (f32[64,512]{1,0:T(8,128)S(1)}, f32[64,512]{1,0:T(8,128)S(1)}, u32[]{:S(2)}, u32[]{:S(2)}) collective-permute-start(f32[64,512]{1,0:T(8,128)S(1)} %get-tuple-element.51), channel_id=1, source_target_pairs={{0,1},{1,0},{2,3},{3,2},{4,5},{5,4},{6,7},{7,6},{8,9},{9,8},{10,11... | collective-permute-start | bytes 393224 | tf_op jit(solution)/shard_map/ppermute | solution.py:326
  39.9 6.8 %collective-permute-start.15 = (f32[64,512]{1,0:T(8,128)S(1)}, f32[64,512]{1,0:T(8,128)S(1)}, u32[]{:S(2)}, u32[]{:S(2)}) collective-permute-start(f32[64,512]{1,0:T(8,128)S(1)} %add_add_fusion.1.refs_0_), channel_id=1, source_target_pairs={{0,2},{1,9},{2,0},{3,11},{4,6},{5,13},{6,4},{7,15},{8,10},{9,1},{1... | collective-permute-start | bytes 393224 | tf_op jit(solution)/shard_map/ppermute | solution.py:252
  41.2 5.5 %collective-permute-start.16 = (f32[64,512]{1,0:T(8,128)S(1)}, f32[64,512]{1,0:T(8,128)S(1)}, u32[]{:S(2)}, u32[]{:S(2)}) collective-permute-start(f32[64,512]{1,0:T(8,128)S(1)} %add_add_fusion.1.refs_0_), channel_id=1, source_target_pairs={{0,4},{1,17},{2,6},{3,19},{4,0},{5,21},{6,2},{7,23},{8,12},{9,25},... | collective-permute-start | bytes 393224 | tf_op jit(solution)/shard_map/ppermute | solution.py:252
  42.0 6.1 %collective-permute-start.14 = (f32[64,512]{1,0:T(8,128)S(1)}, f32[64,512]{1,0:T(8,128)S(1)}, u32[]{:S(2)}, u32[]{:S(2)}) collective-permute-start(f32[64,512]{1,0:T(8,128)S(1)} %add_add_fusion.1.refs_0_), channel_id=1, source_target_pairs={{0,6},{1,25},{2,4},{3,27},{4,2},{5,29},{6,0},{7,31},{8,14},{9,17},... | collective-permute-start | bytes 393224 | tf_op jit(solution)/shard_map/ppermute | solution.py:252
  49.0 7.8 %collective-permute-start.17 = (f32[72,512]{1,0:T(8,128)S(1)}, f32[72,512]{1,0:T(8,128)S(1)}, u32[]{:S(2)}, u32[]{:S(2)}) collective-permute-start(f32[72,512]{1,0:T(8,128)S(1)} %get-tuple-element.64), channel_id=1, source_target_pairs={{0,16},{1,5},{2,18},{3,7},{4,20},{5,1},{6,22},{7,3},{8,24},{9,13},... | collective-permute-start | bytes 442376 | tf_op jit(solution)/shard_map/ppermute | solution.py:252
  49.8 7.0 %collective-permute-start.18 = (f32[72,512]{1,0:T(8,128)S(1)}, f32[72,512]{1,0:T(8,128)S(1)}, u32[]{:S(2)}, u32[]{:S(2)}) collective-permute-start(f32[72,512]{1,0:T(8,128)S(1)} %get-tuple-element.65), channel_id=1, source_target_pairs={{0,8},{1,3},{2,10},{3,1},{4,12},{5,7},{6,14},{7,5},{8,0},{9,11},{1... | collective-permute-start | bytes 442376 | tf_op jit(solution)/shard_map/ppermute | solution.py:252
  52.1 7.1 %collective-permute-start.19 = (f32[72,512]{1,0:T(8,128)S(1)}, f32[72,512]{1,0:T(8,128)S(1)}, u32[]{:S(2)}, u32[]{:S(2)}) collective-permute-start(f32[72,512]{1,0:T(8,128)S(1)} %get-tuple-element.66), channel_id=1, source_target_pairs={{0,24},{1,7},{2,26},{3,5},{4,28},{5,3},{6,30},{7,1},{8,16},{9,15},... | collective-permute-start | bytes 442376 | tf_op jit(solution)/shard_map/ppermute | solution.py:252
  59.3 5.0 %collective-permute-start.21 = (f32[64,512]{1,0:T(8,128)S(1)}, f32[64,512]{1,0:T(8,128)S(1)}, u32[]{:S(2)}, u32[]{:S(2)}) collective-permute-start(f32[64,512]{1,0:T(8,128)S(1)} %fusion.3.refs_0_), channel_id=1, source_target_pairs={{0,2},{1,9},{2,0},{3,11},{4,6},{5,13},{6,4},{7,15},{8,10},{9,1},{1... | collective-permute-start | bytes 393224 | tf_op jit(solution)/shard_map/ppermute | solution.py:252
  60.6 5.0 %collective-permute-start.22 = (f32[64,512]{1,0:T(8,128)S(1)}, f32[64,512]{1,0:T(8,128)S(1)}, u32[]{:S(2)}, u32[]{:S(2)}) collective-permute-start(f32[64,512]{1,0:T(8,128)S(1)} %fusion.3.refs_0_), channel_id=1, source_target_pairs={{0,4},{1,17},{2,6},{3,19},{4,0},{5,21},{6,2},{7,23},{8,12},{9,25},... | collective-permute-start | bytes 393224 | tf_op jit(solution)/shard_map/ppermute | solution.py:252
  61.4 5.9 %collective-permute-start.20 = (f32[64,512]{1,0:T(8,128)S(1)}, f32[64,512]{1,0:T(8,128)S(1)}, u32[]{:S(2)}, u32[]{:S(2)}) collective-permute-start(f32[64,512]{1,0:T(8,128)S(1)} %fusion.3.refs_0_), channel_id=1, source_target_pairs={{0,6},{1,25},{2,4},{3,27},{4,2},{5,29},{6,0},{7,31},{8,14},{9,17},... | collective-permute-start | bytes 393224 | tf_op jit(solution)/shard_map/ppermute | solution.py:252
  68.1 7.4 %collective-permute-start.23 = (f32[64,512]{1,0:T(8,128)S(1)}, f32[64,512]{1,0:T(8,128)S(1)}, u32[]{:S(2)}, u32[]{:S(2)}) collective-permute-start(f32[64,512]{1,0:T(8,128)S(1)} %get-tuple-element.68), channel_id=1, source_target_pairs={{0,16},{1,5},{2,18},{3,7},{4,20},{5,1},{6,22},{7,3},{8,24},{9,13},... | collective-permute-start | bytes 393224 | tf_op jit(solution)/shard_map/ppermute | solution.py:252
  69.9 5.6 %collective-permute-start.24 = (f32[64,512]{1,0:T(8,128)S(1)}, f32[64,512]{1,0:T(8,128)S(1)}, u32[]{:S(2)}, u32[]{:S(2)}) collective-permute-start(f32[64,512]{1,0:T(8,128)S(1)} %get-tuple-element.69), channel_id=1, source_target_pairs={{0,8},{1,3},{2,10},{3,1},{4,12},{5,7},{6,14},{7,5},{8,0},{9,11},{1... | collective-permute-start | bytes 393224 | tf_op jit(solution)/shard_map/ppermute | solution.py:252
  70.3 7.4 %collective-permute-start.25 = (f32[64,512]{1,0:T(8,128)S(1)}, f32[64,512]{1,0:T(8,128)S(1)}, u32[]{:S(2)}, u32[]{:S(2)}) collective-permute-start(f32[64,512]{1,0:T(8,128)S(1)} %get-tuple-element.70), channel_id=1, source_target_pairs={{0,24},{1,7},{2,26},{3,5},{4,28},{5,3},{6,30},{7,1},{8,16},{9,15},... | collective-permute-start | bytes 393224 | tf_op jit(solution)/shard_map/ppermute | solution.py:252
  77.8 1.3 %collective-permute-start.26 = (f32[64,256]{1,0:T(8,128)S(1)}, f32[64,256]{1,0:T(8,128)S(1)}, u32[]{:S(2)}, u32[]{:S(2)}) collective-permute-start(f32[64,256]{1,0:T(8,128)S(1)} %get-tuple-element.76), channel_id=1, source_target_pairs={{0,1},{1,0},{2,3},{3,2},{4,5},{5,4},{6,7},{7,6},{8,9},{9,8},{10,11... | collective-permute-start | bytes 196616 | tf_op jit(solution)/shard_map/ppermute | solution.py:449

commit v6 on v5

--- a/solution.py
+++ b/solution.py
@@ -95,31 +95,27 @@
         for k, source in enumerate(sources):
             cols[:, k * width : (k + 1) * width] = point_features(source[...], inverse, False)
     step = 2 if len(spans) % 2 == 0 else 1
-    sums = [None] * len(spans)
+    length = blocks[0].shape[1]
     for n in range(count):
+        along = slice(n * length, (n + 1) * length)
         a, b = parts_of(blocks[n][:full] * 4.0, 2)
-        stacked[:full] = a
-        stacked[full:] = b
-        rows[...] = point_features(blocks[n][full : full + 3], inverse, True)
-        for k in range(0, len(spans), step):
-            evaluate(rows, 0, cols[:, spans[k] * width : (spans[k] + step) * width], high, low, 0, 128)
-            coarse, fine = product(stacked[...], full, high[...], low[...])
-            total = coarse[:full] + coarse[full:] + fine
-            at = slice(k * width, (k + step) * width)
-            if n:
-                total = sums[k] + total
-            elif not first:
-                total = before[:, skip + at.start : skip + at.stop] + total
-            sums[k] = total
-            if n < count - 1:
-                continue
-            if not last:
-                after[:, at] = total
-                continue
-            mine = jnp.where(core[0] == 0, total[:half], total[half:])
-            for i in range(step):
-                after[k + i][...] = mine[:, i * width : (i + 1) * width]
-            after[-1][:, at] = jnp.where(core[0] == 0, total[half:], total[:half])
+        stacked[:full, along] = a
+        stacked[full:, along] = b
+        rows[:, along] = point_features(blocks[n][full : full + 3], inverse, True)
+    for k in range(0, len(spans), step):
+        evaluate(rows, 0, cols[:, spans[k] * width : (spans[k] + step) * width], high, low, 0, 128)
+        coarse, fine = product(stacked[...], full, high[...], low[...])
+        total = coarse[:full] + coarse[full:] + fine
+        at = slice(k * width, (k + step) * width)
+        if not first:
+            total = before[:, skip + at.start : skip + at.stop] + total
+        if not last:
+            after[:, at] = total
+            continue
+        mine = jnp.where(core[0] == 0, total[:half], total[half:])
+        for i in range(step):
+            after[k + i][...] = mine[:, i * width : (i + 1) * width]
+        after[-1][:, at] = jnp.where(core[0] == 0, total[half:], total[:half])
 
 
 def keep_kernel(inverse, start, row_points, col_points, high, low, zero, rows, cols):
@@ -305,10 +301,10 @@
             in_specs=in_specs,
             out_specs=vmem(len(shapes)),
             scratch_shapes=[
-                pltpu.VMEM((2 * full, volume), BF16),
-                pltpu.VMEM((FEATURES, volume), BF16),
-                pltpu.VMEM((volume, step * width), BF16),
-                pltpu.VMEM((volume, step * width), BF16),
+                pltpu.VMEM((2 * full, len(which) * volume), BF16),
+                pltpu.VMEM((FEATURES, len(which) * volume), BF16),
+                pltpu.VMEM((len(which) * volume, step * width), BF16),
+                pltpu.VMEM((len(which) * volume, step * width), BF16),
             ],
             compiler_params=params(),
             cost_estimate=cost(len(which) * volume, full, weight),

time: 79.9 us -> 80 us (level)
  no operation moved by 1% of the time
where the time goes in v6:
time: 80 us; the launch traced here: 79.8 us
  starting transfers between devices  33.7 us (42%)
  Pallas kernels  25.8 us (32%)
  waiting for transfers between devices  17 us (21%)
  other arithmetic  2.81 us (4%)
    ppermute x21, starting transfers between devices, exchange(): return lax.ppermute(value, ('tgt', 'src'), pairs)  32.5 us
    ppermute x21, waiting for transfers between devices, exchange(): return lax.ppermute(value, ('tgt', 'src'), pairs)  15.8 us
    pallas_call x6, Pallas kernels, pull(): pl.pallas_call(functools.partial(pull_kernel, inverse, full, width, len(w...  10.9 us
    pallas_call x2, Pallas kernels, keep(): pl.pallas_call(functools.partial(keep_kernel, inverse, start * width), ou...  8.7 us
    pallas_call x6, Pallas kernels, step(): pl.pallas_call(functools.partial(step_kernel, half, start, len(these), sp...  6.17 us
  transfers between devices with their start and end apart: 27, of which 10 were waited for; matrix products, arithmetic and copies ran while one was open for 3% of the time, Pallas kernels for 27%

profile of v6, /device:TPU:0, one launch (start us, length us, event | category | flops | bytes accessed | tf_op | source)
XLA Modules:
  0.0 79.8 jit_solution(18387650223274019393)
XLA Ops:
  0.0 0.5 collective-permute-start
  0.5 0.1 pad.39.clone
  0.5 1.1 %fusion.refs_1_ = f32[136,512]{1,0:T(8,128)S(1)} fusion(f32[3,256]{1,0:T(4,128)} %param.5, f32[3,512]{1,0:T(4,128)} %param.4, f32[128,512]{1,0:T(8,128)} %param.3, f32[136]{0:T(256)S(1)} %pad.39.clone), kind=kLoop, calls=%fused_computation.3 | loop fusion | flops 487424 | bytes 550432 | tf_op jit(solution)/shard_map/concatenate | solution.py:255
  1.6 2.7 %collective-permute-start.1 = (f32[136,512]{1,0:T(8,128)S(1)}, f32[136,512]{1,0:T(8,128)S(1)}, u32[]{:S(2)}, u32[]{:S(2)}) collective-permute-start(f32[136,512]{1,0:T(8,128)S(1)} %fusion.refs_1_), channel_id=1, source_target_pairs={{0,2},{1,3},{2,0},{3,1},{4,6},{5,7},{6,4},{7,5},{8,10},{9,11},{10,... | collective-permute-start | bytes 835592 | tf_op jit(solution)/shard_map/ppermute | solution.py:248
  4.3 1.5 %collective-permute-start.2 = (f32[136,512]{1,0:T(8,128)S(1)}, f32[136,512]{1,0:T(8,128)S(1)}, u32[]{:S(2)}, u32[]{:S(2)}) collective-permute-start(f32[136,512]{1,0:T(8,128)S(1)} %fusion.refs_1_), channel_id=1, source_target_pairs={{0,4},{1,5},{2,6},{3,7},{4,0},{5,1},{6,2},{7,3},{8,12},{9,13},{10,... | collective-permute-start | bytes 835592 | tf_op jit(solution)/shard_map/ppermute | solution.py:248
  5.9 0.8 maximum_select_fusion.1.refs_2_
  6.6 2.1 %collective-permute-start.4 = (f32[3,512]{1,0:T(4,128)S(1)}, f32[3,512]{1,0:T(4,128)S(1)}, u32[]{:S(2)}, u32[]{:S(2)}) collective-permute-start(f32[3,512]{1,0:T(4,128)S(1)} %maximum_select_fusion.1.refs_2_), channel_id=1, source_target_pairs={{0,8},{1,9},{2,10},{3,11},{4,12},{5,13},{6,14},{7,15},{8,0},{9,1},... | collective-permute-start | bytes 18440 | tf_op jit(solution)/shard_map/ppermute | solution.py:248
  8.7 2.6 %collective-permute-start.5 = (f32[3,512]{1,0:T(4,128)S(1)}, f32[3,512]{1,0:T(4,128)S(1)}, u32[]{:S(2)}, u32[]{:S(2)}) collective-permute-start(f32[3,512]{1,0:T(4,128)S(1)} %maximum_select_fusion.1.refs_2_), channel_id=1, source_target_pairs={{0,16},{1,17},{2,18},{3,19},{4,20},{5,21},{6,22},{7,23},{8,24},{9,... | collective-permute-start | bytes 18440 | tf_op jit(solution)/shard_map/ppermute | solution.py:248
  11.3 0.0 collective-permute-done.4.refs_3_
  11.3 3.1 %collective-permute-start.6 = (f32[3,512]{1,0:T(4,128)S(1)}, f32[3,512]{1,0:T(4,128)S(1)}, u32[]{:S(2)}, u32[]{:S(2)}) collective-permute-start(f32[3,512]{1,0:T(4,128)S(1)} %maximum_select_fusion.1.refs_2_), channel_id=1, source_target_pairs={{0,24},{1,25},{2,26},{3,27},{4,28},{5,29},{6,30},{7,31},{8,16},{9,... | collective-permute-start | bytes 18440 | tf_op jit(solution)/shard_map/ppermute | solution.py:248
  14.4 1.4 %shard_map.37 = (bf16[32,1024]{1,0:T(8,128)(2,1)S(1)}, f32[128,1024]{1,0:T(8,128)S(1)}) custom-call(s32[1]{0:T(128)} %bitcast.refs_0_, f32[136,512]{1,0:T(8,128)S(1)} %fusion.refs_1_, f32[3,512]{1,0:T(4,128)S(1)} %maximum_select_fusion.1.refs_2_, f32[3,512]{1,0:T(4,128)S(1)} %collective-permute-done.4.refs_3_), custom_call_target="tpu_custom_call" | custom-call | flops 65536 | bytes 128 | tf_op jit(solution)/shard_map/pallas_call | solution.py:296
  15.7 0.0 collective-permute-done.5.refs_2_
  15.7 1.0 %collective-permute-done.6.refs_3_ = f32[3,512]{1,0:T(4,128)S(1)} collective-permute-done((f32[3,512]{1,0:T(4,128)S(1)}, f32[3,512]{1,0:T(4,128)S(1)}, u32[]{:S(2)}, u32[]{:S(2)}) %collective-permute-start.6) | collective-permute-done | bytes 6176 | tf_op jit(solution)/shard_map/ppermute | solution.py:248
  16.7 1.4 %shard_map.38 = (bf16[32,1024]{1,0:T(8,128)(2,1)S(1)}, f32[128,1024]{1,0:T(8,128)S(1)}) custom-call(s32[1]{0:T(128)} %bitcast.refs_0_, f32[136,512]{1,0:T(8,128)S(1)} %fusion.refs_1_, f32[3,512]{1,0:T(4,128)S(1)} %collective-permute-done.5.refs_2_, f32[3,512]{1,0:T(4,128)S(1)} %collective-permute-done.6.refs_3_), custom_call_target="tpu_custom_call" | custom-call | flops 65536 | bytes 128 | tf_op jit(solution)/shard_map/pallas_call | solution.py:296
  18.1 0.0 collective-permute-done.1.refs_1_
  18.1 1.4 %shard_map.39.refs_4_ = f32[128,1024]{1,0:T(8,128)S(1)} custom-call(s32[1]{0:T(128)} %bitcast.refs_0_, f32[136,512]{1,0:T(8,128)S(1)} %collective-permute-done.1.refs_1_, bf16[32,1024]{1,0:T(8,128)(2,1)S(1)} %get-tuple-element.42.refs_2_.refs_3_, f32[128,1024]{1,0:T(8,128)S(1)} %get-tuple-element.43.refs_3_), custom_call_target="tpu_custom_call" | custom-call | flops 268435456 | bytes 128 | tf_op jit(solution)/shard_map/pallas_call | solution.py:296
  19.5 0.0 collective-permute-done.3.refs_2_.refs_3_
  19.5 2.6 %shard_map.40 = (f32[64,512]{1,0:T(8,128)S(1)}, f32[64,512]{1,0:T(8,128)S(1)}, f32[64,1024]{1,0:T(8,128)S(1)}) custom-call(s32[1]{0:T(128)} %bitcast.refs_0_, f32[136,512]{1,0:T(8,128)S(1)} %collective-permute-done.2.refs_1_.refs_2_, f32[136,512]{1,0:T(8,128)S(1)} %collective-permute-done.3.refs_2_.refs_3_, ...), custom_call_target="tpu_custom_call" | custom-call | flops 536870912 | bytes 128 | tf_op jit(solution)/shard_map/pallas_call | solution.py:296
  22.1 0.1 collective-permute-start.8
  22.3 0.5 collective-permute-start.10
  22.8 2.1 %shard_map.41 = (f32[64,512]{1,0:T(8,128)S(1)}, f32[64,512]{1,0:T(8,128)S(1)}) custom-call(s32[1]{0:T(128)} %bitcast.refs_0_, f32[136,512]{1,0:T(8,128)S(1)} %collective-permute-done.1.refs_1_, f32[136,512]{1,0:T(8,128)S(1)} %collective-permute-done.2.refs_1_.refs_2_, f32[136,512]{1,0:T(8,128)S(1)} %collective-permute-done.3.refs_2_.refs_3_, ...), custom_call_target="tpu_custom_call" | custom-call | flops 402653184 | bytes 128 | tf_op jit(solution)/shard_map/pallas_call | solution.py:296
  24.9 0.1 collective-permute-start.7
  25.0 0.0 collective-permute-done.10
  25.1 3.2 %collective-permute-start.11 = (f32[64,512]{1,0:T(8,128)S(1)}, f32[64,512]{1,0:T(8,128)S(1)}, u32[]{:S(2)}, u32[]{:S(2)}) collective-permute-start(f32[64,512]{1,0:T(8,128)S(1)} %get-tuple-element.73.refs_7_), channel_id=1, source_target_pairs={{0,24},{1,25},{2,26},{3,27},{4,28},{5,29},{6,30},{7,31},{8,16},{9,... | collective-permute-start | bytes 393224 | tf_op jit(solution)/shard_map/ppermute | solution.py:248
  28.3 0.0 collective-permute-start.12
  28.3 2.1 %shard_map.42 = (f32[64,512]{1,0:T(8,128)S(1)}, f32[64,512]{1,0:T(8,128)S(1)}) custom-call(s32[1]{0:T(128)} %bitcast.refs_0_, f32[136,512]{1,0:T(8,128)S(1)} %collective-permute-done.1.refs_1_, f32[136,512]{1,0:T(8,128)S(1)} %collective-permute-done.2.refs_1_.refs_2_, f32[136,512]{1,0:T(8,128)S(1)} %collective-permute-done.3.refs_2_.refs_3_, ...), custom_call_target="tpu_custom_call" | custom-call | flops 196608 | bytes 128 | tf_op jit(solution)/shard_map/pallas_call | solution.py:296
  30.4 1.4 %collective-permute-start.13 = (f32[64,512]{1,0:T(8,128)S(1)}, f32[64,512]{1,0:T(8,128)S(1)}, u32[]{:S(2)}, u32[]{:S(2)}) collective-permute-start(f32[64,512]{1,0:T(8,128)S(1)} %add.73), channel_id=1, source_target_pairs={{0,8},{1,9},{2,10},{3,11},{4,12},{5,13},{6,14},{7,15},{8,0},{9,1},... | collective-permute-start | bytes 393224 | tf_op jit(solution)/shard_map/ppermute | solution.py:248
  31.8 6.3 %shard_map.43 = (bf16[1536,2048]{1,0:T(8,128)(2,1)S(1)}, bf16[1536,2048]{1,0:T(8,128)(2,1)S(1)}, f32[1,512]{1,0:T(1,128)S(1)}) custom-call(f32[3,2048]{1,0:T(4,128)S(1)} %get-tuple-element.78.row_points, f32[3,2048]{1,0:T(4,128)S(1)} %get-tuple-element.77.col_points), custom_call_target="tpu_custom_call" | custom-call | flops 131072 | bytes 64 | tf_op jit(solution)/shard_map/pallas_call | solution.py:368
  38.1 0.0 collective-permute-done.9
  38.2 0.0 collective-permute-done.11
  38.2 1.8 %collective-permute-done.12 = f32[64,512]{1,0:T(8,128)S(1)} collective-permute-done((f32[64,512]{1,0:T(8,128)S(1)}, f32[64,512]{1,0:T(8,128)S(1)}, u32[]{:S(2)}, u32[]{:S(2)}) %collective-permute-start.12) | collective-permute-done | bytes 131104 | tf_op jit(solution)/shard_map/ppermute | solution.py:248
  39.9 0.1 add_add_fusion.1.refs_0_
  40.0 1.3 %collective-permute-start.15 = (f32[64,512]{1,0:T(8,128)S(1)}, f32[64,512]{1,0:T(8,128)S(1)}, u32[]{:S(2)}, u32[]{:S(2)}) collective-permute-start(f32[64,512]{1,0:T(8,128)S(1)} %add_add_fusion.1.refs_0_), channel_id=1, source_target_pairs={{0,2},{1,9},{2,0},{3,11},{4,6},{5,13},{6,4},{7,15},{8,10},{9,1},{1... | collective-permute-start | bytes 393224 | tf_op jit(solution)/shard_map/ppermute | solution.py:248
  41.3 0.8 %collective-permute-start.16 = (f32[64,512]{1,0:T(8,128)S(1)}, f32[64,512]{1,0:T(8,128)S(1)}, u32[]{:S(2)}, u32[]{:S(2)}) collective-permute-start(f32[64,512]{1,0:T(8,128)S(1)} %add_add_fusion.1.refs_0_), channel_id=1, source_target_pairs={{0,4},{1,17},{2,6},{3,19},{4,0},{5,21},{6,2},{7,23},{8,12},{9,25},... | collective-permute-start | bytes 393224 | tf_op jit(solution)/shard_map/ppermute | solution.py:248
  42.1 1.4 %collective-permute-start.14 = (f32[64,512]{1,0:T(8,128)S(1)}, f32[64,512]{1,0:T(8,128)S(1)}, u32[]{:S(2)}, u32[]{:S(2)}) collective-permute-start(f32[64,512]{1,0:T(8,128)S(1)} %add_add_fusion.1.refs_0_), channel_id=1, source_target_pairs={{0,6},{1,25},{2,4},{3,27},{4,2},{5,29},{6,0},{7,31},{8,14},{9,17},... | collective-permute-start | bytes 393224 | tf_op jit(solution)/shard_map/ppermute | solution.py:248
  43.5 2.4 %shard_map.44 = (bf16[512,2048]{1,0:T(8,128)(2,1)S(1)}, bf16[512,2048]{1,0:T(8,128)(2,1)S(1)}, f32[1,512]{1,0:T(1,128)S(1)}) custom-call(f32[3,2048]{1,0:T(4,128)S(1)} %get-tuple-element.78.row_points, f32[3,2048]{1,0:T(4,128)S(1)} %get-tuple-element.77.col_points), custom_call_target="tpu_custom_call" | custom-call | flops 131072 | bytes 64 | tf_op jit(solution)/shard_map/pallas_call | solution.py:368
  45.9 0.8 %shard_map.45.refs_4_ = f32[72,2048]{1,0:T(8,128)S(1)} custom-call(f32[64,512]{1,0:T(8,128)S(1)} %add_add_fusion.1.refs_0_, bf16[1536,2048]{1,0:T(8,128)(2,1)S(1)} %get-tuple-element.60.refs_1_.refs_2_, bf16[1536,2048]{1,0:T(8,128)(2,1)S(1)} %get-tuple-element.61.refs_2_.refs_3_, f32[1,512]{1,0:T(1,128)S(1)} %get-tuple-element.62.refs_3_.refs_5_.refs_4_), custom_call_target="tpu_custom_call" | custom-call | flops 131072 | bytes 64 | tf_op jit(solution)/shard_map/pallas_call | solution.py:394
  46.7 0.0 collective-permute-done.16.refs_1_
  46.7 1.5 %shard_map.46.refs_3_ = f32[72,2048]{1,0:T(8,128)S(1)} custom-call(f32[64,512]{1,0:T(8,128)S(1)} %collective-permute-done.15.refs_0_, f32[64,512]{1,0:T(8,128)S(1)} %collective-permute-done.16.refs_1_, bf16[1536,2048]{1,0:T(8,128)(2,1)S(1)} %get-tuple-element.60.refs_1_.refs_2_, bf16[1536,2048]{1,0:T(8,128)(2,1)S(1)} %get-tuple-element.61.refs_2_.refs_3_, ...), custom_call_target="tpu_custom_call" | custom-call | flops 131072 | bytes 64 | tf_op jit(solution)/shard_map/pallas_call | solution.py:394
  48.2 0.8 %shard_map.47 = (f32[72,512]{1,0:T(8,128)S(1)}, f32[72,512]{1,0:T(8,128)S(1)}, f32[72,512]{1,0:T(8,128)S(1)}, f32[72,512]{1,0:T(8,128)S(1)}) custom-call(f32[64,512]{1,0:T(8,128)S(1)} %collective-permute-done.14.refs_0_, bf16[512,2048]{1,0:T(8,128)(2,1)S(1)} %get-tuple-element.58.refs_1_, bf16[512,2048]{1,0:T(8,128)(2,1)S(1)} %get-tuple-element.59.refs_2_, ...), custom_call_target="tpu_custom_call" | custom-call | flops 131072 | bytes 64 | tf_op jit(solution)/shard_map/pallas_call | solution.py:394
  49.1 0.7 collective-permute-start.17
  49.8 2.4 %collective-permute-start.18 = (f32[72,512]{1,0:T(8,128)S(1)}, f32[72,512]{1,0:T(8,128)S(1)}, u32[]{:S(2)}, u32[]{:S(2)}) collective-permute-start(f32[72,512]{1,0:T(8,128)S(1)} %get-tuple-element.65), channel_id=1, source_target_pairs={{0,8},{1,3},{2,10},{3,1},{4,12},{5,7},{6,14},{7,5},{8,0},{9,11},{1... | collective-permute-start | bytes 442376 | tf_op jit(solution)/shard_map/ppermute | solution.py:248
  52.2 1.4 %collective-permute-start.19 = (f32[72,512]{1,0:T(8,128)S(1)}, f32[72,512]{1,0:T(8,128)S(1)}, u32[]{:S(2)}, u32[]{:S(2)}) collective-permute-start(f32[72,512]{1,0:T(8,128)S(1)} %get-tuple-element.66), channel_id=1, source_target_pairs={{0,24},{1,7},{2,26},{3,5},{4,28},{5,3},{6,30},{7,1},{8,16},{9,15},... | collective-permute-start | bytes 442376 | tf_op jit(solution)/shard_map/ppermute | solution.py:248
  53.6 3.3 %collective-permute-done.17 = f32[72,512]{1,0:T(8,128)S(1)} collective-permute-done((f32[72,512]{1,0:T(8,128)S(1)}, f32[72,512]{1,0:T(8,128)S(1)}, u32[]{:S(2)}, u32[]{:S(2)}) %collective-permute-start.17) | collective-permute-done | bytes 147488 | tf_op jit(solution)/shard_map/ppermute | solution.py:248
  56.9 0.0 collective-permute-done.18
  56.9 2.4 %collective-permute-done.19 = f32[72,512]{1,0:T(8,128)S(1)} collective-permute-done((f32[72,512]{1,0:T(8,128)S(1)}, f32[72,512]{1,0:T(8,128)S(1)}, u32[]{:S(2)}, u32[]{:S(2)}) %collective-permute-start.19) | collective-permute-done | bytes 147488 | tf_op jit(solution)/shard_map/ppermute | solution.py:248
  59.4 1.3 %collective-permute-start.21 = (f32[64,512]{1,0:T(8,128)S(1)}, f32[64,512]{1,0:T(8,128)S(1)}, u32[]{:S(2)}, u32[]{:S(2)}) collective-permute-start(f32[64,512]{1,0:T(8,128)S(1)} %fusion.3.refs_0_), channel_id=1, source_target_pairs={{0,2},{1,9},{2,0},{3,11},{4,6},{5,13},{6,4},{7,15},{8,10},{9,1},{1... | collective-permute-start | bytes 393224 | tf_op jit(solution)/shard_map/ppermute | solution.py:248
  60.7 0.8 collective-permute-start.22
  61.5 1.5 %collective-permute-start.20 = (f32[64,512]{1,0:T(8,128)S(1)}, f32[64,512]{1,0:T(8,128)S(1)}, u32[]{:S(2)}, u32[]{:S(2)}) collective-permute-start(f32[64,512]{1,0:T(8,128)S(1)} %fusion.3.refs_0_), channel_id=1, source_target_pairs={{0,6},{1,25},{2,4},{3,27},{4,2},{5,29},{6,0},{7,31},{8,14},{9,17},... | collective-permute-start | bytes 393224 | tf_op jit(solution)/shard_map/ppermute | solution.py:248
  62.9 0.8 shard_map.48.refs_4_
  63.7 0.7 collective-permute-done.21.refs_0_
  64.4 1.3 %collective-permute-done.22.refs_1_ = f32[64,512]{1,0:T(8,128)S(1)} collective-permute-done((f32[64,512]{1,0:T(8,128)S(1)}, f32[64,512]{1,0:T(8,128)S(1)}, u32[]{:S(2)}, u32[]{:S(2)}) %collective-permute-start.22) | collective-permute-done | bytes 131104 | tf_op jit(solution)/shard_map/ppermute | solution.py:248
  65.7 1.4 %shard_map.49.refs_3_ = f32[64,2048]{1,0:T(8,128)S(1)} custom-call(f32[64,512]{1,0:T(8,128)S(1)} %collective-permute-done.21.refs_0_, f32[64,512]{1,0:T(8,128)S(1)} %collective-permute-done.22.refs_1_, bf16[1536,2048]{1,0:T(8,128)(2,1)S(1)} %get-tuple-element.60.refs_1_.refs_2_, bf16[1536,2048]{1,0:T(8,128)(2,1)S(1)} %get-tuple-element.61.refs_2_.refs_3_, ...), custom_call_target="tpu_custom_call" | custom-call | flops 131072 | bytes 64 | tf_op jit(solution)/shard_map/pallas_call | solution.py:394
  67.1 0.2 collective-permute-done.20.refs_0_
  67.3 0.8 shard_map.50
  68.1 1.7 %collective-permute-start.23 = (f32[64,512]{1,0:T(8,128)S(1)}, f32[64,512]{1,0:T(8,128)S(1)}, u32[]{:S(2)}, u32[]{:S(2)}) collective-permute-start(f32[64,512]{1,0:T(8,128)S(1)} %get-tuple-element.68), channel_id=1, source_target_pairs={{0,16},{1,5},{2,18},{3,7},{4,20},{5,1},{6,22},{7,3},{8,24},{9,13},... | collective-permute-start | bytes 393224 | tf_op jit(solution)/shard_map/ppermute | solution.py:248
  69.9 0.5 collective-permute-start.24
  70.3 2.2 %collective-permute-start.25 = (f32[64,512]{1,0:T(8,128)S(1)}, f32[64,512]{1,0:T(8,128)S(1)}, u32[]{:S(2)}, u32[]{:S(2)}) collective-permute-start(f32[64,512]{1,0:T(8,128)S(1)} %get-tuple-element.70), channel_id=1, source_target_pairs={{0,24},{1,7},{2,26},{3,5},{4,28},{5,3},{6,30},{7,1},{8,16},{9,15},... | collective-permute-start | bytes 393224 | tf_op jit(solution)/shard_map/ppermute | solution.py:248
  72.6 2.9 %collective-permute-done.23 = f32[64,512]{1,0:T(8,128)S(1)} collective-permute-done((f32[64,512]{1,0:T(8,128)S(1)}, f32[64,512]{1,0:T(8,128)S(1)}, u32[]{:S(2)}, u32[]{:S(2)}) %collective-permute-start.23) | collective-permute-done | bytes 131104 | tf_op jit(solution)/shard_map/ppermute | solution.py:248
  75.5 2.2 %collective-permute-done.25 = f32[64,512]{1,0:T(8,128)S(1)} collective-permute-done((f32[64,512]{1,0:T(8,128)S(1)}, f32[64,512]{1,0:T(8,128)S(1)}, u32[]{:S(2)}, u32[]{:S(2)}) %collective-permute-start.25) | collective-permute-done | bytes 131104 | tf_op jit(solution)/shard_map/ppermute | solution.py:248
  77.7 0.1 multiply_add_fusion
  77.8 0.1 collective-permute-start.26
  77.9 1.2 %collective-permute-done.26 = f32[64,256]{1,0:T(8,128)S(1)} collective-permute-done((f32[64,256]{1,0:T(8,128)S(1)}, f32[64,256]{1,0:T(8,128)S(1)}, u32[]{:S(2)}, u32[]{:S(2)}) %collective-permute-start.26) | collective-permute-done | bytes 65568 | tf_op jit(solution)/shard_map/ppermute | solution.py:445
  79.1 0.7 maximum_select_fusion
  (26 shorter events, 0.2 us)
Async XLA Ops:
  0.0 1.6 %collective-permute-start = (f32[3,256]{1,0:T(4,128)}, f32[3,256]{1,0:T(4,128)S(1)}, u32[]{:S(2)}, u32[]{:S(2)}) collective-permute-start(f32[3,256]{1,0:T(4,128)} %param.5), channel_id=1, source_target_pairs={{0,1},{1,0},{2,3},{3,2},{4,5},{5,4},{6,7},{7,6},{8,9},{9,8},{10,11... | collective-permute-start | bytes 9224 | tf_op jit(solution)/shard_map/ppermute | solution.py:264
  1.6 16.5 %collective-permute-start.1 = (f32[136,512]{1,0:T(8,128)S(1)}, f32[136,512]{1,0:T(8,128)S(1)}, u32[]{:S(2)}, u32[]{:S(2)}) collective-permute-start(f32[136,512]{1,0:T(8,128)S(1)} %fusion.refs_1_), channel_id=1, source_target_pairs={{0,2},{1,3},{2,0},{3,1},{4,6},{5,7},{6,4},{7,5},{8,10},{9,11},{10,... | collective-permute-start | bytes 835592 | tf_op jit(solution)/shard_map/ppermute | solution.py:248
  4.3 15.2 %collective-permute-start.2 = (f32[136,512]{1,0:T(8,128)S(1)}, f32[136,512]{1,0:T(8,128)S(1)}, u32[]{:S(2)}, u32[]{:S(2)}) collective-permute-start(f32[136,512]{1,0:T(8,128)S(1)} %fusion.refs_1_), channel_id=1, source_target_pairs={{0,4},{1,5},{2,6},{3,7},{4,0},{5,1},{6,2},{7,3},{8,12},{9,13},{10,... | collective-permute-start | bytes 835592 | tf_op jit(solution)/shard_map/ppermute | solution.py:248
  5.9 13.6 %collective-permute-start.3 = (f32[136,512]{1,0:T(8,128)S(1)}, f32[136,512]{1,0:T(8,128)S(1)}, u32[]{:S(2)}, u32[]{:S(2)}) collective-permute-start(f32[136,512]{1,0:T(8,128)S(1)} %fusion.refs_1_), channel_id=1, source_target_pairs={{0,6},{1,7},{2,4},{3,5},{4,2},{5,3},{6,0},{7,1},{8,14},{9,15},{10,... | collective-permute-start | bytes 835592 | tf_op jit(solution)/shard_map/ppermute | solution.py:248
  6.6 4.6 %collective-permute-start.4 = (f32[3,512]{1,0:T(4,128)S(1)}, f32[3,512]{1,0:T(4,128)S(1)}, u32[]{:S(2)}, u32[]{:S(2)}) collective-permute-start(f32[3,512]{1,0:T(4,128)S(1)} %maximum_select_fusion.1.refs_2_), channel_id=1, source_target_pairs={{0,8},{1,9},{2,10},{3,11},{4,12},{5,13},{6,14},{7,15},{8,0},{9,1},... | collective-permute-start | bytes 18440 | tf_op jit(solution)/shard_map/ppermute | solution.py:248
  8.7 7.1 %collective-permute-start.5 = (f32[3,512]{1,0:T(4,128)S(1)}, f32[3,512]{1,0:T(4,128)S(1)}, u32[]{:S(2)}, u32[]{:S(2)}) collective-permute-start(f32[3,512]{1,0:T(4,128)S(1)} %maximum_select_fusion.1.refs_2_), channel_id=1, source_target_pairs={{0,16},{1,17},{2,18},{3,19},{4,20},{5,21},{6,22},{7,23},{8,24},{9,... | collective-permute-start | bytes 18440 | tf_op jit(solution)/shard_map/ppermute | solution.py:248
  11.3 5.4 %collective-permute-start.6 = (f32[3,512]{1,0:T(4,128)S(1)}, f32[3,512]{1,0:T(4,128)S(1)}, u32[]{:S(2)}, u32[]{:S(2)}) collective-permute-start(f32[3,512]{1,0:T(4,128)S(1)} %maximum_select_fusion.1.refs_2_), channel_id=1, source_target_pairs={{0,24},{1,25},{2,26},{3,27},{4,28},{5,29},{6,30},{7,31},{8,16},{9,... | collective-permute-start | bytes 18440 | tf_op jit(solution)/shard_map/ppermute | solution.py:248
  22.1 2.9 %collective-permute-start.8 = (f32[64,1024]{1,0:T(8,128)S(1)}, f32[64,1024]{1,0:T(8,128)S(1)}, u32[]{:S(2)}, u32[]{:S(2)}) collective-permute-start(f32[64,1024]{1,0:T(8,128)S(1)} %get-tuple-element.44.refs_6_), channel_id=1, source_target_pairs={{0,1},{1,0},{2,3},{3,2},{4,5},{5,4},{6,7},{7,6},{8,9},{9,8},{10,11... | collective-permute-start | bytes 786440 | tf_op jit(solution)/shard_map/ppermute | solution.py:322
  22.3 2.8 %collective-permute-start.10 = (f32[3,768]{1,0:T(4,128)S(1)}, f32[3,768]{1,0:T(4,128)S(1)}, u32[]{:S(2)}, u32[]{:S(2)}) collective-permute-start(f32[3,768]{1,0:T(4,128)S(1)} %pad_maximum_fusion.2), channel_id=1, source_target_pairs={{0,1},{1,0},{2,3},{3,2},{4,5},{5,4},{6,7},{7,6},{8,9},{9,8},{10,11... | collective-permute-start | bytes 27656 | tf_op jit(solution)/shard_map/ppermute | solution.py:334
  24.9 5.5 %collective-permute-start.7 = (f32[64,512]{1,0:T(8,128)S(1)}, f32[64,512]{1,0:T(8,128)S(1)}, u32[]{:S(2)}, u32[]{:S(2)}) collective-permute-start(f32[64,512]{1,0:T(8,128)S(1)} %get-tuple-element.45), channel_id=1, source_target_pairs={{0,1},{1,0},{2,3},{3,2},{4,5},{5,4},{6,7},{7,6},{8,9},{9,8},{10,11... | collective-permute-start | bytes 393224 | tf_op jit(solution)/shard_map/ppermute | solution.py:322
  25.1 13.1 %collective-permute-start.11 = (f32[64,512]{1,0:T(8,128)S(1)}, f32[64,512]{1,0:T(8,128)S(1)}, u32[]{:S(2)}, u32[]{:S(2)}) collective-permute-start(f32[64,512]{1,0:T(8,128)S(1)} %get-tuple-element.73.refs_7_), channel_id=1, source_target_pairs={{0,24},{1,25},{2,26},{3,27},{4,28},{5,29},{6,30},{7,31},{8,16},{9,... | collective-permute-start | bytes 393224 | tf_op jit(solution)/shard_map/ppermute | solution.py:248
  28.3 11.7 %collective-permute-start.12 = (f32[64,512]{1,0:T(8,128)S(1)}, f32[64,512]{1,0:T(8,128)S(1)}, u32[]{:S(2)}, u32[]{:S(2)}) collective-permute-start(f32[64,512]{1,0:T(8,128)S(1)} %get-tuple-element.74.refs_6_), channel_id=1, source_target_pairs={{0,16},{1,17},{2,18},{3,19},{4,20},{5,21},{6,22},{7,23},{8,24},{9,... | collective-permute-start | bytes 393224 | tf_op jit(solution)/shard_map/ppermute | solution.py:248
  30.4 7.7 %collective-permute-start.13 = (f32[64,512]{1,0:T(8,128)S(1)}, f32[64,512]{1,0:T(8,128)S(1)}, u32[]{:S(2)}, u32[]{:S(2)}) collective-permute-start(f32[64,512]{1,0:T(8,128)S(1)} %add.73), channel_id=1, source_target_pairs={{0,8},{1,9},{2,10},{3,11},{4,12},{5,13},{6,14},{7,15},{8,0},{9,1},... | collective-permute-start | bytes 393224 | tf_op jit(solution)/shard_map/ppermute | solution.py:248
  31.8 6.4 %collective-permute-start.9 = (f32[64,512]{1,0:T(8,128)S(1)}, f32[64,512]{1,0:T(8,128)S(1)}, u32[]{:S(2)}, u32[]{:S(2)}) collective-permute-start(f32[64,512]{1,0:T(8,128)S(1)} %get-tuple-element.51), channel_id=1, source_target_pairs={{0,1},{1,0},{2,3},{3,2},{4,5},{5,4},{6,7},{7,6},{8,9},{9,8},{10,11... | collective-permute-start | bytes 393224 | tf_op jit(solution)/shard_map/ppermute | solution.py:322
  40.0 6.7 %collective-permute-start.15 = (f32[64,512]{1,0:T(8,128)S(1)}, f32[64,512]{1,0:T(8,128)S(1)}, u32[]{:S(2)}, u32[]{:S(2)}) collective-permute-start(f32[64,512]{1,0:T(8,128)S(1)} %add_add_fusion.1.refs_0_), channel_id=1, source_target_pairs={{0,2},{1,9},{2,0},{3,11},{4,6},{5,13},{6,4},{7,15},{8,10},{9,1},{1... | collective-permute-start | bytes 393224 | tf_op jit(solution)/shard_map/ppermute | solution.py:248
  41.3 5.5 %collective-permute-start.16 = (f32[64,512]{1,0:T(8,128)S(1)}, f32[64,512]{1,0:T(8,128)S(1)}, u32[]{:S(2)}, u32[]{:S(2)}) collective-permute-start(f32[64,512]{1,0:T(8,128)S(1)} %add_add_fusion.1.refs_0_), channel_id=1, source_target_pairs={{0,4},{1,17},{2,6},{3,19},{4,0},{5,21},{6,2},{7,23},{8,12},{9,25},... | collective-permute-start | bytes 393224 | tf_op jit(solution)/shard_map/ppermute | solution.py:248
  42.1 6.2 %collective-permute-start.14 = (f32[64,512]{1,0:T(8,128)S(1)}, f32[64,512]{1,0:T(8,128)S(1)}, u32[]{:S(2)}, u32[]{:S(2)}) collective-permute-start(f32[64,512]{1,0:T(8,128)S(1)} %add_add_fusion.1.refs_0_), channel_id=1, source_target_pairs={{0,6},{1,25},{2,4},{3,27},{4,2},{5,29},{6,0},{7,31},{8,14},{9,17},... | collective-permute-start | bytes 393224 | tf_op jit(solution)/shard_map/ppermute | solution.py:248
  49.1 7.8 %collective-permute-start.17 = (f32[72,512]{1,0:T(8,128)S(1)}, f32[72,512]{1,0:T(8,128)S(1)}, u32[]{:S(2)}, u32[]{:S(2)}) collective-permute-start(f32[72,512]{1,0:T(8,128)S(1)} %get-tuple-element.64), channel_id=1, source_target_pairs={{0,16},{1,5},{2,18},{3,7},{4,20},{5,1},{6,22},{7,3},{8,24},{9,13},... | collective-permute-start | bytes 442376 | tf_op jit(solution)/shard_map/ppermute | solution.py:248
  49.8 7.1 %collective-permute-start.18 = (f32[72,512]{1,0:T(8,128)S(1)}, f32[72,512]{1,0:T(8,128)S(1)}, u32[]{:S(2)}, u32[]{:S(2)}) collective-permute-start(f32[72,512]{1,0:T(8,128)S(1)} %get-tuple-element.65), channel_id=1, source_target_pairs={{0,8},{1,3},{2,10},{3,1},{4,12},{5,7},{6,14},{7,5},{8,0},{9,11},{1... | collective-permute-start | bytes 442376 | tf_op jit(solution)/shard_map/ppermute | solution.py:248
  52.2 7.1 %collective-permute-start.19 = (f32[72,512]{1,0:T(8,128)S(1)}, f32[72,512]{1,0:T(8,128)S(1)}, u32[]{:S(2)}, u32[]{:S(2)}) collective-permute-start(f32[72,512]{1,0:T(8,128)S(1)} %get-tuple-element.66), channel_id=1, source_target_pairs={{0,24},{1,7},{2,26},{3,5},{4,28},{5,3},{6,30},{7,1},{8,16},{9,15},... | collective-permute-start | bytes 442376 | tf_op jit(solution)/shard_map/ppermute | solution.py:248
  59.4 5.0 %collective-permute-start.21 = (f32[64,512]{1,0:T(8,128)S(1)}, f32[64,512]{1,0:T(8,128)S(1)}, u32[]{:S(2)}, u32[]{:S(2)}) collective-permute-start(f32[64,512]{1,0:T(8,128)S(1)} %fusion.3.refs_0_), channel_id=1, source_target_pairs={{0,2},{1,9},{2,0},{3,11},{4,6},{5,13},{6,4},{7,15},{8,10},{9,1},{1... | collective-permute-start | bytes 393224 | tf_op jit(solution)/shard_map/ppermute | solution.py:248
  60.7 5.0 %collective-permute-start.22 = (f32[64,512]{1,0:T(8,128)S(1)}, f32[64,512]{1,0:T(8,128)S(1)}, u32[]{:S(2)}, u32[]{:S(2)}) collective-permute-start(f32[64,512]{1,0:T(8,128)S(1)} %fusion.3.refs_0_), channel_id=1, source_target_pairs={{0,4},{1,17},{2,6},{3,19},{4,0},{5,21},{6,2},{7,23},{8,12},{9,25},... | collective-permute-start | bytes 393224 | tf_op jit(solution)/shard_map/ppermute | solution.py:248
  61.5 5.9 %collective-permute-start.20 = (f32[64,512]{1,0:T(8,128)S(1)}, f32[64,512]{1,0:T(8,128)S(1)}, u32[]{:S(2)}, u32[]{:S(2)}) collective-permute-start(f32[64,512]{1,0:T(8,128)S(1)} %fusion.3.refs_0_), channel_id=1, source_target_pairs={{0,6},{1,25},{2,4},{3,27},{4,2},{5,29},{6,0},{7,31},{8,14},{9,17},... | collective-permute-start | bytes 393224 | tf_op jit(solution)/shard_map/ppermute | solution.py:248
  68.1 7.3 %collective-permute-start.23 = (f32[64,512]{1,0:T(8,128)S(1)}, f32[64,512]{1,0:T(8,128)S(1)}, u32[]{:S(2)}, u32[]{:S(2)}) collective-permute-start(f32[64,512]{1,0:T(8,128)S(1)} %get-tuple-element.68), channel_id=1, source_target_pairs={{0,16},{1,5},{2,18},{3,7},{4,20},{5,1},{6,22},{7,3},{8,24},{9,13},... | collective-permute-start | bytes 393224 | tf_op jit(solution)/shard_map/ppermute | solution.py:248
  69.9 5.6 %collective-permute-start.24 = (f32[64,512]{1,0:T(8,128)S(1)}, f32[64,512]{1,0:T(8,128)S(1)}, u32[]{:S(2)}, u32[]{:S(2)}) collective-permute-start(f32[64,512]{1,0:T(8,128)S(1)} %get-tuple-element.69), channel_id=1, source_target_pairs={{0,8},{1,3},{2,10},{3,1},{4,12},{5,7},{6,14},{7,5},{8,0},{9,11},{1... | collective-permute-start | bytes 393224 | tf_op jit(solution)/shard_map/ppermute | solution.py:248
  70.3 7.4 %collective-permute-start.25 = (f32[64,512]{1,0:T(8,128)S(1)}, f32[64,512]{1,0:T(8,128)S(1)}, u32[]{:S(2)}, u32[]{:S(2)}) collective-permute-start(f32[64,512]{1,0:T(8,128)S(1)} %get-tuple-element.70), channel_id=1, source_target_pairs={{0,24},{1,7},{2,26},{3,5},{4,28},{5,3},{6,30},{7,1},{8,16},{9,15},... | collective-permute-start | bytes 393224 | tf_op jit(solution)/shard_map/ppermute | solution.py:248
  77.8 1.3 %collective-permute-start.26 = (f32[64,256]{1,0:T(8,128)S(1)}, f32[64,256]{1,0:T(8,128)S(1)}, u32[]{:S(2)}, u32[]{:S(2)}) collective-permute-start(f32[64,256]{1,0:T(8,128)S(1)} %get-tuple-element.76), channel_id=1, source_target_pairs={{0,1},{1,0},{2,3},{3,2},{4,5},{5,4},{6,7},{7,6},{8,9},{9,8},{10,11... | collective-permute-start | bytes 196616 | tf_op jit(solution)/shard_map/ppermute | solution.py:445

commit v7 on v5

--- a/solution.py
+++ b/solution.py
@@ -269,7 +269,7 @@
     block, got = lax.optimization_barrier((block, got))
     ctrl = ordered(ctrl_coords, got, 1)
     blocks = [block] + [exchange(block, along_src[k]) for k in range(1, peers)]
-    tgt_ctrl = [ctrl] + [exchange(ctrl, along_tgt[k]) for k in range(1, peers)]
+    tgt_ctrl = [ctrl] + [exchange(ctrl, along_tgt[k]) for k in range(peers - 1, 0, -1)][::-1]
 
     width, full = 2 * owned, 2 * half
     total_width = peers * width
@@ -447,9 +447,7 @@
     own = jnp.where(first_core, iterate[:, :owned], iterate[:, owned:])
     theirs = jnp.where(first_core, iterate[:, owned:], iterate[:, :owned])
     back = lax.ppermute(theirs, "src", sibling)
-    return jnp.where(
-        first_core, jnp.concatenate([own, back], axis=0), jnp.concatenate([back, own], axis=0)
-    )
+    return lax.dynamic_update_slice(jnp.concatenate([own, own], axis=0), back, (jnp.where(first_core, half, 0), 0))
 
 
 def solution(mesh):

time: 79.9 us -> 79.9 us (level)
  no operation moved by 1% of the time
where the time goes in v7:
time: 79.9 us; the launch traced here: 79.7 us
  starting transfers between devices  33.7 us (42%)
  Pallas kernels  25.8 us (32%)
  waiting for transfers between devices  16.3 us (20%)
  other arithmetic  2.81 us (4%)
    ppermute x21, starting transfers between devices, exchange(): return lax.ppermute(value, ('tgt', 'src'), pairs)  32.5 us
    ppermute x21, waiting for transfers between devices, exchange(): return lax.ppermute(value, ('tgt', 'src'), pairs)  15.7 us
    pallas_call x6, Pallas kernels, pull(): pl.pallas_call(functools.partial(pull_kernel, inverse, full, width, len(w...  10.9 us
    pallas_call x2, Pallas kernels, keep(): pl.pallas_call(functools.partial(keep_kernel, inverse, start * width), ou...  8.7 us
    pallas_call x6, Pallas kernels, step(): pl.pallas_call(functools.partial(step_kernel, half, start, len(these), sp...  6.19 us
  transfers between devices with their start and end apart: 27, of which 10 were waited for; matrix products, arithmetic and copies ran while one was open for 3% of the time, Pallas kernels for 27%

profile of v7, /device:TPU:0, one launch (start us, length us, event | category | flops | bytes accessed | tf_op | source)
XLA Modules:
  0.0 79.7 jit_solution(17524491151878908149)
XLA Ops:
  0.0 0.5 collective-permute-start
  0.5 0.1 pad.37.clone
  0.5 1.1 %fusion.refs_1_ = f32[136,512]{1,0:T(8,128)S(1)} fusion(f32[3,256]{1,0:T(4,128)} %param.5, f32[3,512]{1,0:T(4,128)} %param.4, f32[128,512]{1,0:T(8,128)} %param.3, f32[136]{0:T(256)S(1)} %pad.37.clone), kind=kLoop, calls=%fused_computation.3 | loop fusion | flops 487424 | bytes 550432 | tf_op jit(solution)/shard_map/concatenate | solution.py:259
  1.6 0.0 collective-permute-done
  1.6 2.7 %collective-permute-start.1 = (f32[136,512]{1,0:T(8,128)S(1)}, f32[136,512]{1,0:T(8,128)S(1)}, u32[]{:S(2)}, u32[]{:S(2)}) collective-permute-start(f32[136,512]{1,0:T(8,128)S(1)} %fusion.refs_1_), channel_id=1, source_target_pairs={{0,2},{1,3},{2,0},{3,1},{4,6},{5,7},{6,4},{7,5},{8,10},{9,11},{10,... | collective-permute-start | bytes 835592 | tf_op jit(solution)/shard_map/ppermute | solution.py:252
  4.3 1.5 %collective-permute-start.2 = (f32[136,512]{1,0:T(8,128)S(1)}, f32[136,512]{1,0:T(8,128)S(1)}, u32[]{:S(2)}, u32[]{:S(2)}) collective-permute-start(f32[136,512]{1,0:T(8,128)S(1)} %fusion.refs_1_), channel_id=1, source_target_pairs={{0,4},{1,5},{2,6},{3,7},{4,0},{5,1},{6,2},{7,3},{8,12},{9,13},{10,... | collective-permute-start | bytes 835592 | tf_op jit(solution)/shard_map/ppermute | solution.py:252
  5.9 0.0 collective-permute-start.3
  5.9 0.8 maximum_select_fusion.refs_2_
  6.6 2.1 %collective-permute-start.4 = (f32[3,512]{1,0:T(4,128)S(1)}, f32[3,512]{1,0:T(4,128)S(1)}, u32[]{:S(2)}, u32[]{:S(2)}) collective-permute-start(f32[3,512]{1,0:T(4,128)S(1)} %maximum_select_fusion.refs_2_), channel_id=1, source_target_pairs={{0,8},{1,9},{2,10},{3,11},{4,12},{5,13},{6,14},{7,15},{8,0},{9,1},... | collective-permute-start | bytes 18440 | tf_op jit(solution)/shard_map/ppermute | solution.py:252
  8.7 2.6 %collective-permute-start.5 = (f32[3,512]{1,0:T(4,128)S(1)}, f32[3,512]{1,0:T(4,128)S(1)}, u32[]{:S(2)}, u32[]{:S(2)}) collective-permute-start(f32[3,512]{1,0:T(4,128)S(1)} %maximum_select_fusion.refs_2_), channel_id=1, source_target_pairs={{0,16},{1,17},{2,18},{3,19},{4,20},{5,21},{6,22},{7,23},{8,24},{9,... | collective-permute-start | bytes 18440 | tf_op jit(solution)/shard_map/ppermute | solution.py:252
  11.3 0.0 collective-permute-done.4.refs_3_
  11.3 3.1 %collective-permute-start.6 = (f32[3,512]{1,0:T(4,128)S(1)}, f32[3,512]{1,0:T(4,128)S(1)}, u32[]{:S(2)}, u32[]{:S(2)}) collective-permute-start(f32[3,512]{1,0:T(4,128)S(1)} %maximum_select_fusion.refs_2_), channel_id=1, source_target_pairs={{0,24},{1,25},{2,26},{3,27},{4,28},{5,29},{6,30},{7,31},{8,16},{9,... | collective-permute-start | bytes 18440 | tf_op jit(solution)/shard_map/ppermute | solution.py:252
  14.4 1.4 %shard_map.37 = (bf16[32,1024]{1,0:T(8,128)(2,1)S(1)}, f32[128,1024]{1,0:T(8,128)S(1)}) custom-call(s32[1]{0:T(128)} %bitcast.refs_0_, f32[136,512]{1,0:T(8,128)S(1)} %fusion.refs_1_, f32[3,512]{1,0:T(4,128)S(1)} %maximum_select_fusion.refs_2_, f32[3,512]{1,0:T(4,128)S(1)} %collective-permute-done.4.refs_3_), custom_call_target="tpu_custom_call" | custom-call | flops 65536 | bytes 128 | tf_op jit(solution)/shard_map/pallas_call | solution.py:300
  15.7 1.0 %collective-permute-done.6.refs_3_ = f32[3,512]{1,0:T(4,128)S(1)} collective-permute-done((f32[3,512]{1,0:T(4,128)S(1)}, f32[3,512]{1,0:T(4,128)S(1)}, u32[]{:S(2)}, u32[]{:S(2)}) %collective-permute-start.6) | collective-permute-done | bytes 6176 | tf_op jit(solution)/shard_map/ppermute | solution.py:252
  16.7 1.4 %shard_map.38 = (bf16[32,1024]{1,0:T(8,128)(2,1)S(1)}, f32[128,1024]{1,0:T(8,128)S(1)}) custom-call(s32[1]{0:T(128)} %bitcast.refs_0_, f32[136,512]{1,0:T(8,128)S(1)} %fusion.refs_1_, f32[3,512]{1,0:T(4,128)S(1)} %collective-permute-done.5.refs_2_, f32[3,512]{1,0:T(4,128)S(1)} %collective-permute-done.6.refs_3_), custom_call_target="tpu_custom_call" | custom-call | flops 65536 | bytes 128 | tf_op jit(solution)/shard_map/pallas_call | solution.py:300
  18.1 0.0 collective-permute-done.1.refs_1_
  18.1 1.4 %shard_map.39.refs_4_ = f32[128,1024]{1,0:T(8,128)S(1)} custom-call(s32[1]{0:T(128)} %bitcast.refs_0_, f32[136,512]{1,0:T(8,128)S(1)} %collective-permute-done.1.refs_1_, bf16[32,1024]{1,0:T(8,128)(2,1)S(1)} %get-tuple-element.42.refs_2_.refs_3_, f32[128,1024]{1,0:T(8,128)S(1)} %get-tuple-element.43.refs_3_), custom_call_target="tpu_custom_call" | custom-call | flops 268435456 | bytes 128 | tf_op jit(solution)/shard_map/pallas_call | solution.py:300
  19.5 0.0 collective-permute-done.2.refs_1_.refs_2_
  19.5 0.0 collective-permute-done.3.refs_2_.refs_3_
  19.5 2.5 %shard_map.40 = (f32[64,512]{1,0:T(8,128)S(1)}, f32[64,512]{1,0:T(8,128)S(1)}, f32[64,1024]{1,0:T(8,128)S(1)}) custom-call(s32[1]{0:T(128)} %bitcast.refs_0_, f32[136,512]{1,0:T(8,128)S(1)} %collective-permute-done.2.refs_1_.refs_2_, f32[136,512]{1,0:T(8,128)S(1)} %collective-permute-done.3.refs_2_.refs_3_, ...), custom_call_target="tpu_custom_call" | custom-call | flops 536870912 | bytes 128 | tf_op jit(solution)/shard_map/pallas_call | solution.py:300
  22.0 0.1 collective-permute-start.8
  22.1 0.5 collective-permute-start.10
  22.7 2.2 %shard_map.41 = (f32[64,512]{1,0:T(8,128)S(1)}, f32[64,512]{1,0:T(8,128)S(1)}) custom-call(s32[1]{0:T(128)} %bitcast.refs_0_, f32[136,512]{1,0:T(8,128)S(1)} %collective-permute-done.1.refs_1_, f32[136,512]{1,0:T(8,128)S(1)} %collective-permute-done.2.refs_1_.refs_2_, f32[136,512]{1,0:T(8,128)S(1)} %collective-permute-done.3.refs_2_.refs_3_, ...), custom_call_target="tpu_custom_call" | custom-call | flops 402653184 | bytes 128 | tf_op jit(solution)/shard_map/pallas_call | solution.py:300
  24.8 0.1 collective-permute-start.7
  24.9 0.0 collective-permute-done.10
  25.0 0.0 collective-permute-done.8
  25.0 3.2 %collective-permute-start.11 = (f32[64,512]{1,0:T(8,128)S(1)}, f32[64,512]{1,0:T(8,128)S(1)}, u32[]{:S(2)}, u32[]{:S(2)}) collective-permute-start(f32[64,512]{1,0:T(8,128)S(1)} %get-tuple-element.73.refs_7_), channel_id=1, source_target_pairs={{0,24},{1,25},{2,26},{3,27},{4,28},{5,29},{6,30},{7,31},{8,16},{9,... | collective-permute-start | bytes 393224 | tf_op jit(solution)/shard_map/ppermute | solution.py:252
  28.2 2.2 %shard_map.42 = (f32[64,512]{1,0:T(8,128)S(1)}, f32[64,512]{1,0:T(8,128)S(1)}) custom-call(s32[1]{0:T(128)} %bitcast.refs_0_, f32[136,512]{1,0:T(8,128)S(1)} %collective-permute-done.1.refs_1_, f32[136,512]{1,0:T(8,128)S(1)} %collective-permute-done.2.refs_1_.refs_2_, f32[136,512]{1,0:T(8,128)S(1)} %collective-permute-done.3.refs_2_.refs_3_, ...), custom_call_target="tpu_custom_call" | custom-call | flops 196608 | bytes 128 | tf_op jit(solution)/shard_map/pallas_call | solution.py:300
  30.4 1.4 %collective-permute-start.13 = (f32[64,512]{1,0:T(8,128)S(1)}, f32[64,512]{1,0:T(8,128)S(1)}, u32[]{:S(2)}, u32[]{:S(2)}) collective-permute-start(f32[64,512]{1,0:T(8,128)S(1)} %add.74), channel_id=1, source_target_pairs={{0,8},{1,9},{2,10},{3,11},{4,12},{5,13},{6,14},{7,15},{8,0},{9,1},... | collective-permute-start | bytes 393224 | tf_op jit(solution)/shard_map/ppermute | solution.py:252
  31.8 6.3 %shard_map.43 = (bf16[1536,2048]{1,0:T(8,128)(2,1)S(1)}, bf16[1536,2048]{1,0:T(8,128)(2,1)S(1)}, f32[1,512]{1,0:T(1,128)S(1)}) custom-call(f32[3,2048]{1,0:T(4,128)S(1)} %get-tuple-element.78.row_points, f32[3,2048]{1,0:T(4,128)S(1)} %get-tuple-element.77.col_points), custom_call_target="tpu_custom_call" | custom-call | flops 131072 | bytes 64 | tf_op jit(solution)/shard_map/pallas_call | solution.py:372
  38.2 1.7 %collective-permute-done.12 = f32[64,512]{1,0:T(8,128)S(1)} collective-permute-done((f32[64,512]{1,0:T(8,128)S(1)}, f32[64,512]{1,0:T(8,128)S(1)}, u32[]{:S(2)}, u32[]{:S(2)}) %collective-permute-start.12) | collective-permute-done | bytes 131104 | tf_op jit(solution)/shard_map/ppermute | solution.py:252
  39.8 0.1 add_add_fusion.1.refs_0_
  39.9 1.3 %collective-permute-start.15 = (f32[64,512]{1,0:T(8,128)S(1)}, f32[64,512]{1,0:T(8,128)S(1)}, u32[]{:S(2)}, u32[]{:S(2)}) collective-permute-start(f32[64,512]{1,0:T(8,128)S(1)} %add_add_fusion.1.refs_0_), channel_id=1, source_target_pairs={{0,2},{1,9},{2,0},{3,11},{4,6},{5,13},{6,4},{7,15},{8,10},{9,1},{1... | collective-permute-start | bytes 393224 | tf_op jit(solution)/shard_map/ppermute | solution.py:252
  41.2 0.8 %collective-permute-start.16 = (f32[64,512]{1,0:T(8,128)S(1)}, f32[64,512]{1,0:T(8,128)S(1)}, u32[]{:S(2)}, u32[]{:S(2)}) collective-permute-start(f32[64,512]{1,0:T(8,128)S(1)} %add_add_fusion.1.refs_0_), channel_id=1, source_target_pairs={{0,4},{1,17},{2,6},{3,19},{4,0},{5,21},{6,2},{7,23},{8,12},{9,25},... | collective-permute-start | bytes 393224 | tf_op jit(solution)/shard_map/ppermute | solution.py:252
  42.0 1.4 %collective-permute-start.14 = (f32[64,512]{1,0:T(8,128)S(1)}, f32[64,512]{1,0:T(8,128)S(1)}, u32[]{:S(2)}, u32[]{:S(2)}) collective-permute-start(f32[64,512]{1,0:T(8,128)S(1)} %add_add_fusion.1.refs_0_), channel_id=1, source_target_pairs={{0,6},{1,25},{2,4},{3,27},{4,2},{5,29},{6,0},{7,31},{8,14},{9,17},... | collective-permute-start | bytes 393224 | tf_op jit(solution)/shard_map/ppermute | solution.py:252
  43.5 2.4 %shard_map.44 = (bf16[512,2048]{1,0:T(8,128)(2,1)S(1)}, bf16[512,2048]{1,0:T(8,128)(2,1)S(1)}, f32[1,512]{1,0:T(1,128)S(1)}) custom-call(f32[3,2048]{1,0:T(4,128)S(1)} %get-tuple-element.78.row_points, f32[3,2048]{1,0:T(4,128)S(1)} %get-tuple-element.77.col_points), custom_call_target="tpu_custom_call" | custom-call | flops 131072 | bytes 64 | tf_op jit(solution)/shard_map/pallas_call | solution.py:372
  45.8 0.8 %shard_map.45.refs_4_ = f32[72,2048]{1,0:T(8,128)S(1)} custom-call(f32[64,512]{1,0:T(8,128)S(1)} %add_add_fusion.1.refs_0_, bf16[1536,2048]{1,0:T(8,128)(2,1)S(1)} %get-tuple-element.60.refs_1_.refs_2_, bf16[1536,2048]{1,0:T(8,128)(2,1)S(1)} %get-tuple-element.61.refs_2_.refs_3_, f32[1,512]{1,0:T(1,128)S(1)} %get-tuple-element.62.refs_3_.refs_5_.refs_4_), custom_call_target="tpu_custom_call" | custom-call | flops 131072 | bytes 64 | tf_op jit(solution)/shard_map/pallas_call | solution.py:398
  46.7 1.5 %shard_map.46.refs_3_ = f32[72,2048]{1,0:T(8,128)S(1)} custom-call(f32[64,512]{1,0:T(8,128)S(1)} %collective-permute-done.15.refs_0_, f32[64,512]{1,0:T(8,128)S(1)} %collective-permute-done.16.refs_1_, bf16[1536,2048]{1,0:T(8,128)(2,1)S(1)} %get-tuple-element.60.refs_1_.refs_2_, bf16[1536,2048]{1,0:T(8,128)(2,1)S(1)} %get-tuple-element.61.refs_2_.refs_3_, ...), custom_call_target="tpu_custom_call" | custom-call | flops 131072 | bytes 64 | tf_op jit(solution)/shard_map/pallas_call | solution.py:398
  48.2 0.8 %shard_map.47 = (f32[72,512]{1,0:T(8,128)S(1)}, f32[72,512]{1,0:T(8,128)S(1)}, f32[72,512]{1,0:T(8,128)S(1)}, f32[72,512]{1,0:T(8,128)S(1)}) custom-call(f32[64,512]{1,0:T(8,128)S(1)} %collective-permute-done.14.refs_0_, bf16[512,2048]{1,0:T(8,128)(2,1)S(1)} %get-tuple-element.58.refs_1_, bf16[512,2048]{1,0:T(8,128)(2,1)S(1)} %get-tuple-element.59.refs_2_, ...), custom_call_target="tpu_custom_call" | custom-call | flops 131072 | bytes 64 | tf_op jit(solution)/shard_map/pallas_call | solution.py:398
  49.0 0.8 collective-permute-start.17
  49.8 2.3 %collective-permute-start.18 = (f32[72,512]{1,0:T(8,128)S(1)}, f32[72,512]{1,0:T(8,128)S(1)}, u32[]{:S(2)}, u32[]{:S(2)}) collective-permute-start(f32[72,512]{1,0:T(8,128)S(1)} %get-tuple-element.65), channel_id=1, source_target_pairs={{0,8},{1,3},{2,10},{3,1},{4,12},{5,7},{6,14},{7,5},{8,0},{9,11},{1... | collective-permute-start | bytes 442376 | tf_op jit(solution)/shard_map/ppermute | solution.py:252
  52.1 1.3 %collective-permute-start.19 = (f32[72,512]{1,0:T(8,128)S(1)}, f32[72,512]{1,0:T(8,128)S(1)}, u32[]{:S(2)}, u32[]{:S(2)}) collective-permute-start(f32[72,512]{1,0:T(8,128)S(1)} %get-tuple-element.66), channel_id=1, source_target_pairs={{0,24},{1,7},{2,26},{3,5},{4,28},{5,3},{6,30},{7,1},{8,16},{9,15},... | collective-permute-start | bytes 442376 | tf_op jit(solution)/shard_map/ppermute | solution.py:252
  53.5 3.3 %collective-permute-done.17 = f32[72,512]{1,0:T(8,128)S(1)} collective-permute-done((f32[72,512]{1,0:T(8,128)S(1)}, f32[72,512]{1,0:T(8,128)S(1)}, u32[]{:S(2)}, u32[]{:S(2)}) %collective-permute-start.17) | collective-permute-done | bytes 147488 | tf_op jit(solution)/shard_map/ppermute | solution.py:252
  56.8 0.0 collective-permute-done.18
  56.8 2.4 %collective-permute-done.19 = f32[72,512]{1,0:T(8,128)S(1)} collective-permute-done((f32[72,512]{1,0:T(8,128)S(1)}, f32[72,512]{1,0:T(8,128)S(1)}, u32[]{:S(2)}, u32[]{:S(2)}) %collective-permute-start.19) | collective-permute-done | bytes 147488 | tf_op jit(solution)/shard_map/ppermute | solution.py:252
  59.3 1.3 %collective-permute-start.21 = (f32[64,512]{1,0:T(8,128)S(1)}, f32[64,512]{1,0:T(8,128)S(1)}, u32[]{:S(2)}, u32[]{:S(2)}) collective-permute-start(f32[64,512]{1,0:T(8,128)S(1)} %fusion.3.refs_0_), channel_id=1, source_target_pairs={{0,2},{1,9},{2,0},{3,11},{4,6},{5,13},{6,4},{7,15},{8,10},{9,1},{1... | collective-permute-start | bytes 393224 | tf_op jit(solution)/shard_map/ppermute | solution.py:252
  60.6 0.8 collective-permute-start.22
  61.4 1.4 %collective-permute-start.20 = (f32[64,512]{1,0:T(8,128)S(1)}, f32[64,512]{1,0:T(8,128)S(1)}, u32[]{:S(2)}, u32[]{:S(2)}) collective-permute-start(f32[64,512]{1,0:T(8,128)S(1)} %fusion.3.refs_0_), channel_id=1, source_target_pairs={{0,6},{1,25},{2,4},{3,27},{4,2},{5,29},{6,0},{7,31},{8,14},{9,17},... | collective-permute-start | bytes 393224 | tf_op jit(solution)/shard_map/ppermute | solution.py:252
  62.9 0.8 %shard_map.48.refs_4_ = f32[64,2048]{1,0:T(8,128)S(1)} custom-call(f32[64,512]{1,0:T(8,128)S(1)} %fusion.3.refs_0_, bf16[1536,2048]{1,0:T(8,128)(2,1)S(1)} %get-tuple-element.60.refs_1_.refs_2_, bf16[1536,2048]{1,0:T(8,128)(2,1)S(1)} %get-tuple-element.61.refs_2_.refs_3_, f32[1,512]{1,0:T(1,128)S(1)} %get-tuple-element.62.refs_3_.refs_5_.refs_4_), custom_call_target="tpu_custom_call" | custom-call | flops 131072 | bytes 64 | tf_op jit(solution)/shard_map/pallas_call | solution.py:398
  63.7 0.7 collective-permute-done.21.refs_0_
  64.3 1.3 %collective-permute-done.22.refs_1_ = f32[64,512]{1,0:T(8,128)S(1)} collective-permute-done((f32[64,512]{1,0:T(8,128)S(1)}, f32[64,512]{1,0:T(8,128)S(1)}, u32[]{:S(2)}, u32[]{:S(2)}) %collective-permute-start.22) | collective-permute-done | bytes 131104 | tf_op jit(solution)/shard_map/ppermute | solution.py:252
  65.6 1.4 %shard_map.49.refs_3_ = f32[64,2048]{1,0:T(8,128)S(1)} custom-call(f32[64,512]{1,0:T(8,128)S(1)} %collective-permute-done.21.refs_0_, f32[64,512]{1,0:T(8,128)S(1)} %collective-permute-done.22.refs_1_, bf16[1536,2048]{1,0:T(8,128)(2,1)S(1)} %get-tuple-element.60.refs_1_.refs_2_, bf16[1536,2048]{1,0:T(8,128)(2,1)S(1)} %get-tuple-element.61.refs_2_.refs_3_, ...), custom_call_target="tpu_custom_call" | custom-call | flops 131072 | bytes 64 | tf_op jit(solution)/shard_map/pallas_call | solution.py:398
  67.0 0.2 collective-permute-done.20.refs_0_
  67.3 0.8 shard_map.50
  68.1 1.8 %collective-permute-start.23 = (f32[64,512]{1,0:T(8,128)S(1)}, f32[64,512]{1,0:T(8,128)S(1)}, u32[]{:S(2)}, u32[]{:S(2)}) collective-permute-start(f32[64,512]{1,0:T(8,128)S(1)} %get-tuple-element.68), channel_id=1, source_target_pairs={{0,16},{1,5},{2,18},{3,7},{4,20},{5,1},{6,22},{7,3},{8,24},{9,13},... | collective-permute-start | bytes 393224 | tf_op jit(solution)/shard_map/ppermute | solution.py:252
  69.9 0.4 collective-permute-start.24
  70.3 2.2 %collective-permute-start.25 = (f32[64,512]{1,0:T(8,128)S(1)}, f32[64,512]{1,0:T(8,128)S(1)}, u32[]{:S(2)}, u32[]{:S(2)}) collective-permute-start(f32[64,512]{1,0:T(8,128)S(1)} %get-tuple-element.70), channel_id=1, source_target_pairs={{0,24},{1,7},{2,26},{3,5},{4,28},{5,3},{6,30},{7,1},{8,16},{9,15},... | collective-permute-start | bytes 393224 | tf_op jit(solution)/shard_map/ppermute | solution.py:252
  72.5 2.9 %collective-permute-done.23 = f32[64,512]{1,0:T(8,128)S(1)} collective-permute-done((f32[64,512]{1,0:T(8,128)S(1)}, f32[64,512]{1,0:T(8,128)S(1)}, u32[]{:S(2)}, u32[]{:S(2)}) %collective-permute-start.23) | collective-permute-done | bytes 131104 | tf_op jit(solution)/shard_map/ppermute | solution.py:252
  75.5 2.2 %collective-permute-done.25 = f32[64,512]{1,0:T(8,128)S(1)} collective-permute-done((f32[64,512]{1,0:T(8,128)S(1)}, f32[64,512]{1,0:T(8,128)S(1)}, u32[]{:S(2)}, u32[]{:S(2)}) %collective-permute-start.25) | collective-permute-done | bytes 131104 | tf_op jit(solution)/shard_map/ppermute | solution.py:252
  77.7 0.1 multiply_add_fusion
  77.8 0.1 collective-permute-start.26
  77.8 0.7 pad_maximum_fusion
  78.5 0.6 collective-permute-done.26
  79.1 0.6 constant_dynamic-update-slice_fusion
  (27 shorter events, 0.2 us)
Async XLA Ops:
  0.0 1.6 %collective-permute-start = (f32[3,256]{1,0:T(4,128)}, f32[3,256]{1,0:T(4,128)S(1)}, u32[]{:S(2)}, u32[]{:S(2)}) collective-permute-start(f32[3,256]{1,0:T(4,128)} %param.5), channel_id=1, source_target_pairs={{0,1},{1,0},{2,3},{3,2},{4,5},{5,4},{6,7},{7,6},{8,9},{9,8},{10,11... | collective-permute-start | bytes 9224 | tf_op jit(solution)/shard_map/ppermute | solution.py:268
  1.6 16.5 %collective-permute-start.1 = (f32[136,512]{1,0:T(8,128)S(1)}, f32[136,512]{1,0:T(8,128)S(1)}, u32[]{:S(2)}, u32[]{:S(2)}) collective-permute-start(f32[136,512]{1,0:T(8,128)S(1)} %fusion.refs_1_), channel_id=1, source_target_pairs={{0,2},{1,3},{2,0},{3,1},{4,6},{5,7},{6,4},{7,5},{8,10},{9,11},{10,... | collective-permute-start | bytes 835592 | tf_op jit(solution)/shard_map/ppermute | solution.py:252
  4.3 15.2 %collective-permute-start.2 = (f32[136,512]{1,0:T(8,128)S(1)}, f32[136,512]{1,0:T(8,128)S(1)}, u32[]{:S(2)}, u32[]{:S(2)}) collective-permute-start(f32[136,512]{1,0:T(8,128)S(1)} %fusion.refs_1_), channel_id=1, source_target_pairs={{0,4},{1,5},{2,6},{3,7},{4,0},{5,1},{6,2},{7,3},{8,12},{9,13},{10,... | collective-permute-start | bytes 835592 | tf_op jit(solution)/shard_map/ppermute | solution.py:252
  5.9 13.6 %collective-permute-start.3 = (f32[136,512]{1,0:T(8,128)S(1)}, f32[136,512]{1,0:T(8,128)S(1)}, u32[]{:S(2)}, u32[]{:S(2)}) collective-permute-start(f32[136,512]{1,0:T(8,128)S(1)} %fusion.refs_1_), channel_id=1, source_target_pairs={{0,6},{1,7},{2,4},{3,5},{4,2},{5,3},{6,0},{7,1},{8,14},{9,15},{10,... | collective-permute-start | bytes 835592 | tf_op jit(solution)/shard_map/ppermute | solution.py:252
  6.6 4.6 %collective-permute-start.4 = (f32[3,512]{1,0:T(4,128)S(1)}, f32[3,512]{1,0:T(4,128)S(1)}, u32[]{:S(2)}, u32[]{:S(2)}) collective-permute-start(f32[3,512]{1,0:T(4,128)S(1)} %maximum_select_fusion.refs_2_), channel_id=1, source_target_pairs={{0,8},{1,9},{2,10},{3,11},{4,12},{5,13},{6,14},{7,15},{8,0},{9,1},... | collective-permute-start | bytes 18440 | tf_op jit(solution)/shard_map/ppermute | solution.py:252
  8.7 7.1 %collective-permute-start.5 = (f32[3,512]{1,0:T(4,128)S(1)}, f32[3,512]{1,0:T(4,128)S(1)}, u32[]{:S(2)}, u32[]{:S(2)}) collective-permute-start(f32[3,512]{1,0:T(4,128)S(1)} %maximum_select_fusion.refs_2_), channel_id=1, source_target_pairs={{0,16},{1,17},{2,18},{3,19},{4,20},{5,21},{6,22},{7,23},{8,24},{9,... | collective-permute-start | bytes 18440 | tf_op jit(solution)/shard_map/ppermute | solution.py:252
  11.3 5.4 %collective-permute-start.6 = (f32[3,512]{1,0:T(4,128)S(1)}, f32[3,512]{1,0:T(4,128)S(1)}, u32[]{:S(2)}, u32[]{:S(2)}) collective-permute-start(f32[3,512]{1,0:T(4,128)S(1)} %maximum_select_fusion.refs_2_), channel_id=1, source_target_pairs={{0,24},{1,25},{2,26},{3,27},{4,28},{5,29},{6,30},{7,31},{8,16},{9,... | collective-permute-start | bytes 18440 | tf_op jit(solution)/shard_map/ppermute | solution.py:252
  22.0 3.0 %collective-permute-start.8 = (f32[64,1024]{1,0:T(8,128)S(1)}, f32[64,1024]{1,0:T(8,128)S(1)}, u32[]{:S(2)}, u32[]{:S(2)}) collective-permute-start(f32[64,1024]{1,0:T(8,128)S(1)} %get-tuple-element.44.refs_6_), channel_id=1, source_target_pairs={{0,1},{1,0},{2,3},{3,2},{4,5},{5,4},{6,7},{7,6},{8,9},{9,8},{10,11... | collective-permute-start | bytes 786440 | tf_op jit(solution)/shard_map/ppermute | solution.py:326
  22.1 2.8 %collective-permute-start.10 = (f32[3,768]{1,0:T(4,128)S(1)}, f32[3,768]{1,0:T(4,128)S(1)}, u32[]{:S(2)}, u32[]{:S(2)}) collective-permute-start(f32[3,768]{1,0:T(4,128)S(1)} %pad_maximum_fusion.3), channel_id=1, source_target_pairs={{0,1},{1,0},{2,3},{3,2},{4,5},{5,4},{6,7},{7,6},{8,9},{9,8},{10,11... | collective-permute-start | bytes 27656 | tf_op jit(solution)/shard_map/ppermute | solution.py:338
  24.8 5.5 %collective-permute-start.7 = (f32[64,512]{1,0:T(8,128)S(1)}, f32[64,512]{1,0:T(8,128)S(1)}, u32[]{:S(2)}, u32[]{:S(2)}) collective-permute-start(f32[64,512]{1,0:T(8,128)S(1)} %get-tuple-element.45), channel_id=1, source_target_pairs={{0,1},{1,0},{2,3},{3,2},{4,5},{5,4},{6,7},{7,6},{8,9},{9,8},{10,11... | collective-permute-start | bytes 393224 | tf_op jit(solution)/shard_map/ppermute | solution.py:326
  25.0 13.1 %collective-permute-start.11 = (f32[64,512]{1,0:T(8,128)S(1)}, f32[64,512]{1,0:T(8,128)S(1)}, u32[]{:S(2)}, u32[]{:S(2)}) collective-permute-start(f32[64,512]{1,0:T(8,128)S(1)} %get-tuple-element.73.refs_7_), channel_id=1, source_target_pairs={{0,24},{1,25},{2,26},{3,27},{4,28},{5,29},{6,30},{7,31},{8,16},{9,... | collective-permute-start | bytes 393224 | tf_op jit(solution)/shard_map/ppermute | solution.py:252
  28.2 11.7 %collective-permute-start.12 = (f32[64,512]{1,0:T(8,128)S(1)}, f32[64,512]{1,0:T(8,128)S(1)}, u32[]{:S(2)}, u32[]{:S(2)}) collective-permute-start(f32[64,512]{1,0:T(8,128)S(1)} %get-tuple-element.74.refs_6_), channel_id=1, source_target_pairs={{0,16},{1,17},{2,18},{3,19},{4,20},{5,21},{6,22},{7,23},{8,24},{9,... | collective-permute-start | bytes 393224 | tf_op jit(solution)/shard_map/ppermute | solution.py:252
  30.4 7.7 %collective-permute-start.13 = (f32[64,512]{1,0:T(8,128)S(1)}, f32[64,512]{1,0:T(8,128)S(1)}, u32[]{:S(2)}, u32[]{:S(2)}) collective-permute-start(f32[64,512]{1,0:T(8,128)S(1)} %add.74), channel_id=1, source_target_pairs={{0,8},{1,9},{2,10},{3,11},{4,12},{5,13},{6,14},{7,15},{8,0},{9,1},... | collective-permute-start | bytes 393224 | tf_op jit(solution)/shard_map/ppermute | solution.py:252
  31.8 6.4 %collective-permute-start.9 = (f32[64,512]{1,0:T(8,128)S(1)}, f32[64,512]{1,0:T(8,128)S(1)}, u32[]{:S(2)}, u32[]{:S(2)}) collective-permute-start(f32[64,512]{1,0:T(8,128)S(1)} %get-tuple-element.51), channel_id=1, source_target_pairs={{0,1},{1,0},{2,3},{3,2},{4,5},{5,4},{6,7},{7,6},{8,9},{9,8},{10,11... | collective-permute-start | bytes 393224 | tf_op jit(solution)/shard_map/ppermute | solution.py:326
  39.9 6.7 %collective-permute-start.15 = (f32[64,512]{1,0:T(8,128)S(1)}, f32[64,512]{1,0:T(8,128)S(1)}, u32[]{:S(2)}, u32[]{:S(2)}) collective-permute-start(f32[64,512]{1,0:T(8,128)S(1)} %add_add_fusion.1.refs_0_), channel_id=1, source_target_pairs={{0,2},{1,9},{2,0},{3,11},{4,6},{5,13},{6,4},{7,15},{8,10},{9,1},{1... | collective-permute-start | bytes 393224 | tf_op jit(solution)/shard_map/ppermute | solution.py:252
  41.2 5.5 %collective-permute-start.16 = (f32[64,512]{1,0:T(8,128)S(1)}, f32[64,512]{1,0:T(8,128)S(1)}, u32[]{:S(2)}, u32[]{:S(2)}) collective-permute-start(f32[64,512]{1,0:T(8,128)S(1)} %add_add_fusion.1.refs_0_), channel_id=1, source_target_pairs={{0,4},{1,17},{2,6},{3,19},{4,0},{5,21},{6,2},{7,23},{8,12},{9,25},... | collective-permute-start | bytes 393224 | tf_op jit(solution)/shard_map/ppermute | solution.py:252
  42.0 6.1 %collective-permute-start.14 = (f32[64,512]{1,0:T(8,128)S(1)}, f32[64,512]{1,0:T(8,128)S(1)}, u32[]{:S(2)}, u32[]{:S(2)}) collective-permute-start(f32[64,512]{1,0:T(8,128)S(1)} %add_add_fusion.1.refs_0_), channel_id=1, source_target_pairs={{0,6},{1,25},{2,4},{3,27},{4,2},{5,29},{6,0},{7,31},{8,14},{9,17},... | collective-permute-start | bytes 393224 | tf_op jit(solution)/shard_map/ppermute | solution.py:252
  49.0 7.8 %collective-permute-start.17 = (f32[72,512]{1,0:T(8,128)S(1)}, f32[72,512]{1,0:T(8,128)S(1)}, u32[]{:S(2)}, u32[]{:S(2)}) collective-permute-start(f32[72,512]{1,0:T(8,128)S(1)} %get-tuple-element.64), channel_id=1, source_target_pairs={{0,16},{1,5},{2,18},{3,7},{4,20},{5,1},{6,22},{7,3},{8,24},{9,13},... | collective-permute-start | bytes 442376 | tf_op jit(solution)/shard_map/ppermute | solution.py:252
  49.8 7.0 %collective-permute-start.18 = (f32[72,512]{1,0:T(8,128)S(1)}, f32[72,512]{1,0:T(8,128)S(1)}, u32[]{:S(2)}, u32[]{:S(2)}) collective-permute-start(f32[72,512]{1,0:T(8,128)S(1)} %get-tuple-element.65), channel_id=1, source_target_pairs={{0,8},{1,3},{2,10},{3,1},{4,12},{5,7},{6,14},{7,5},{8,0},{9,11},{1... | collective-permute-start | bytes 442376 | tf_op jit(solution)/shard_map/ppermute | solution.py:252
  52.1 7.1 %collective-permute-start.19 = (f32[72,512]{1,0:T(8,128)S(1)}, f32[72,512]{1,0:T(8,128)S(1)}, u32[]{:S(2)}, u32[]{:S(2)}) collective-permute-start(f32[72,512]{1,0:T(8,128)S(1)} %get-tuple-element.66), channel_id=1, source_target_pairs={{0,24},{1,7},{2,26},{3,5},{4,28},{5,3},{6,30},{7,1},{8,16},{9,15},... | collective-permute-start | bytes 442376 | tf_op jit(solution)/shard_map/ppermute | solution.py:252
  59.3 5.0 %collective-permute-start.21 = (f32[64,512]{1,0:T(8,128)S(1)}, f32[64,512]{1,0:T(8,128)S(1)}, u32[]{:S(2)}, u32[]{:S(2)}) collective-permute-start(f32[64,512]{1,0:T(8,128)S(1)} %fusion.3.refs_0_), channel_id=1, source_target_pairs={{0,2},{1,9},{2,0},{3,11},{4,6},{5,13},{6,4},{7,15},{8,10},{9,1},{1... | collective-permute-start | bytes 393224 | tf_op jit(solution)/shard_map/ppermute | solution.py:252
  60.6 5.0 %collective-permute-start.22 = (f32[64,512]{1,0:T(8,128)S(1)}, f32[64,512]{1,0:T(8,128)S(1)}, u32[]{:S(2)}, u32[]{:S(2)}) collective-permute-start(f32[64,512]{1,0:T(8,128)S(1)} %fusion.3.refs_0_), channel_id=1, source_target_pairs={{0,4},{1,17},{2,6},{3,19},{4,0},{5,21},{6,2},{7,23},{8,12},{9,25},... | collective-permute-start | bytes 393224 | tf_op jit(solution)/shard_map/ppermute | solution.py:252
  61.4 5.9 %collective-permute-start.20 = (f32[64,512]{1,0:T(8,128)S(1)}, f32[64,512]{1,0:T(8,128)S(1)}, u32[]{:S(2)}, u32[]{:S(2)}) collective-permute-start(f32[64,512]{1,0:T(8,128)S(1)} %fusion.3.refs_0_), channel_id=1, source_target_pairs={{0,6},{1,25},{2,4},{3,27},{4,2},{5,29},{6,0},{7,31},{8,14},{9,17},... | collective-permute-start | bytes 393224 | tf_op jit(solution)/shard_map/ppermute | solution.py:252
  68.1 7.4 %collective-permute-start.23 = (f32[64,512]{1,0:T(8,128)S(1)}, f32[64,512]{1,0:T(8,128)S(1)}, u32[]{:S(2)}, u32[]{:S(2)}) collective-permute-start(f32[64,512]{1,0:T(8,128)S(1)} %get-tuple-element.68), channel_id=1, source_target_pairs={{0,16},{1,5},{2,18},{3,7},{4,20},{5,1},{6,22},{7,3},{8,24},{9,13},... | collective-permute-start | bytes 393224 | tf_op jit(solution)/shard_map/ppermute | solution.py:252
  69.9 5.6 %collective-permute-start.24 = (f32[64,512]{1,0:T(8,128)S(1)}, f32[64,512]{1,0:T(8,128)S(1)}, u32[]{:S(2)}, u32[]{:S(2)}) collective-permute-start(f32[64,512]{1,0:T(8,128)S(1)} %get-tuple-element.69), channel_id=1, source_target_pairs={{0,8},{1,3},{2,10},{3,1},{4,12},{5,7},{6,14},{7,5},{8,0},{9,11},{1... | collective-permute-start | bytes 393224 | tf_op jit(solution)/shard_map/ppermute | solution.py:252
  70.3 7.4 %collective-permute-start.25 = (f32[64,512]{1,0:T(8,128)S(1)}, f32[64,512]{1,0:T(8,128)S(1)}, u32[]{:S(2)}, u32[]{:S(2)}) collective-permute-start(f32[64,512]{1,0:T(8,128)S(1)} %get-tuple-element.70), channel_id=1, source_target_pairs={{0,24},{1,7},{2,26},{3,5},{4,28},{5,3},{6,30},{7,1},{8,16},{9,15},... | collective-permute-start | bytes 393224 | tf_op jit(solution)/shard_map/ppermute | solution.py:252
  77.8 1.3 %collective-permute-start.26 = (f32[64,256]{1,0:T(8,128)S(1)}, f32[64,256]{1,0:T(8,128)S(1)}, u32[]{:S(2)}, u32[]{:S(2)}) collective-permute-start(f32[64,256]{1,0:T(8,128)S(1)} %get-tuple-element.75), channel_id=1, source_target_pairs={{0,1},{1,0},{2,3},{3,2},{4,5},{5,4},{6,7},{7,6},{8,9},{9,8},{10,11... | collective-permute-start | bytes 196616 | tf_op jit(solution)/shard_map/ppermute | solution.py:449
